TPU v7x, 512 devices: a whole 4x4x16 slice. The times are simulated.
512 devices in a mesh: dp: 64 (over z, y_lo, core), expert: 8 (over y_hi, x).
Axes of the slice: x: 4, y: 4 (y_hi: 2, y_lo: 2; y = y_hi * 2 + y_lo), z: 16, core: 2. Of those that a mesh axis runs over, the one named last changes fastest.
Arguments:
- tokens: bfloat16 [65536, 2048], P(('dp', 'expert')), may hold values from -24 to 24
- cotangent: bfloat16 [65536, 2048], P(('dp', 'expert')), may hold values from -24 to 24
- expert_ids: int32 [65536, 8], P(('dp', 'expert')), may hold values from 0 to 127, as said below
- route_weights: float32 [65536, 8], P(('dp', 'expert')), may hold values from 0.1 to 1
- join_groups: int32 [64], replicated, may hold values from 0 to 1
- w_gate: bfloat16 [2048, 1024], P('dp', 'expert'), may hold values from -0.125 to 0.125
- w_up: bfloat16 [2048, 1024], P('dp', 'expert'), may hold values from -0.125 to 0.125
- w_down: bfloat16 [2048, 1024], P('dp', 'expert'), may hold values from -0.1875 to 0.1875
Outputs:
- mixed: bfloat16 [65536, 2048], P(('dp', 'expert'))
- grad_gate: bfloat16 [2048, 1024], P('dp', 'expert')
- grad_up: bfloat16 [2048, 1024], P('dp', 'expert')
- grad_down: bfloat16 [2048, 1024], P('dp', 'expert')
Inputs may be any that keep to these rules, and one draw needn't show every extreme that they name: `expert_ids`: each row names 8 different experts; the rows of one device name expert 0 at most 16 times, and the rows of some device exactly 16 times.
All inputs are finite; a program needn't handle non-finite values.
Results may differ from a plain program's by a relative error of at most 0.014.
Values may be sent and summed in bfloat16 or wider, within the bound.
No kernel may reach another device: no remote copies, remote signals or barrier semaphores. Data moves between devices by JAX's collectives and lax.ppermute only.
A program may use at most 64 MiB of HBM per device.

v0:
```python
import jax
import jax.numpy as jnp
from jax import lax
from jax.sharding import Mesh
from jax.sharding import PartitionSpec as P

DP = ("dp_0", "dp_1", "dp_2")
DP_EXPERT = ("dp_0", "dp_1", "dp_2", "expert")


def from_everyone(shard, axis):
    copies = jnp.broadcast_to(shard, (lax.axis_size(axis), *shard.shape))
    return lax.all_to_all(copies, axis, split_axis=0, concat_axis=0, tiled=True)


def laid_out(blocks, dim):
    blocks = jnp.moveaxis(blocks, 0, dim)
    lengths = blocks.shape
    return blocks.reshape(*lengths[:dim], lengths[dim] * lengths[dim + 1], *lengths[dim + 2 :])


def gathered_copies(shard, axis, dim):
    blocks = from_everyone(shard, axis)
    return laid_out(blocks, dim)


def side_by_side(arrays, axis, dim, along):
    ends, at = ([], 0)
    for a in arrays[:-1]:
        at += a.shape[along]
        ends.append(at)
    both = jnp.concatenate(arrays, axis=along)
    return tuple(jnp.split(lax.all_gather(both, axis, axis=dim, tiled=True), ends, axis=along))


def in_blocks(shard, dim, length):
    before, after = (shard.shape[:dim], shard.shape[dim + 1 :])
    return jnp.moveaxis(shard.reshape(*before, length, -1, *after), dim, 0)


def sent_and_summed(shard, axis, dim):
    length = lax.axis_size(axis)
    blocks = lax.all_to_all(in_blocks(shard, dim, length), axis, 0, 0, tiled=True)
    return jnp.sum(blocks.astype(jnp.float32), axis=0)


def sum_in_order(blocks, axes, sequence):
    lengths = [lax.axis_size(a) for a in axes]
    blocks = blocks.reshape(*lengths, *blocks.shape[1:])
    blocks = blocks.transpose(*sequence, *range(len(axes), blocks.ndim))
    blocks = blocks.reshape(-1, *blocks.shape[len(axes) :])
    for k in sequence:
        blocks = lax.psum_scatter(blocks, axes[k], scatter_dimension=0, tiled=True)
    return blocks[0]


def scatter_axes(shard, axes, sequence, dim):
    length = lax.axis_size(axes)
    return sum_in_order(in_blocks(shard, dim, length), axes, sequence)


def per_device(tokens, cotangent, expert_ids, route_weights, join_groups, w_gate, w_up, w_down):
    highest = lax.Precision.HIGHEST
    tok_count = tokens.shape[0]
    slot_count = tok_count // 8
    slice_width = w_gate.shape[1]
    chosen_mask = expert_ids == 0
    routed = jnp.any(chosen_mask, -1)
    weight = jnp.sum(jnp.where(chosen_mask, route_weights, 0.0), -1)
    places = jnp.cumsum(routed.astype(jnp.int32)) - 1
    slot_ids = jnp.arange(slot_count, dtype=jnp.int32)
    chooser = ((places[None, :] == slot_ids[:, None]) & routed[None, :]).astype(jnp.float32)
    chooser_half = chooser.astype(jnp.bfloat16)
    picked_local = jnp.dot(chooser_half, tokens, preferred_element_type=jnp.float32).astype(
        jnp.bfloat16
    )
    picked = gathered_copies(picked_local, "expert", 0)
    pieces = side_by_side((w_gate, w_up), DP, 0, 1)
    gate_acts = jnp.dot(picked, pieces[0], preferred_element_type=jnp.float32)
    up_acts = jnp.dot(picked, pieces[1], preferred_element_type=jnp.float32)
    hidden = (jax.nn.silu(gate_acts) * up_acts).astype(jnp.bfloat16)
    trans_dims = (((1,), (1,)), ((), ()))
    full_down = gathered_copies(w_down, DP, 0)
    partial_out = lax.dot_general(hidden, full_down, trans_dims, preferred_element_type=jnp.float32)
    out_rows = sent_and_summed(partial_out.astype(jnp.bfloat16), "expert", 0)
    placed = lax.dot_general(
        chooser,
        out_rows,
        (((0,), (0,)), ((), ())),
        precision=highest,
        preferred_element_type=jnp.float32,
    )
    mixed = (placed * weight[:, None]).astype(jnp.bfloat16)
    scaled = cotangent.astype(jnp.float32) * weight[:, None]
    dpicked_local = jnp.dot(
        chooser, scaled, precision=highest, preferred_element_type=jnp.float32
    ).astype(jnp.bfloat16)
    dpicked = gathered_copies(dpicked_local, "expert", 0)
    hidden_grad = jnp.dot(dpicked, full_down, preferred_element_type=jnp.float32)
    sigma_gate = jax.nn.sigmoid(gate_acts)
    dgate = (hidden_grad * up_acts * sigma_gate * (1.0 + gate_acts * (1.0 - sigma_gate))).astype(
        jnp.bfloat16
    )
    dup = (hidden_grad * gate_acts * sigma_gate).astype(jnp.bfloat16)
    group_total = lax.axis_size(DP)
    mine = jnp.arange(group_total, dtype=jnp.int32) == lax.axis_index(DP)
    active = 1.0 - jnp.sum(jnp.where(mine, join_groups, 0)).astype(jnp.float32)
    col_dims = (((0,), (0,)), ((), ()))

    def term_of(left, right):
        return active * lax.dot_general(left, right, col_dims, preferred_element_type=jnp.float32)

    summed = scatter_axes(
        jnp.concatenate(
            [term_of(picked, dgate), term_of(picked, dup), term_of(dpicked, hidden)], axis=1
        ),
        DP,
        (2, 0, 1),
        0,
    )
    grad_gate = summed[:, :slice_width]
    grad_up = summed[:, slice_width : 2 * slice_width]
    grad_down = summed[:, 2 * slice_width :]
    return (
        mixed,
        grad_gate.astype(jnp.bfloat16),
        grad_up.astype(jnp.bfloat16),
        grad_down.astype(jnp.bfloat16),
    )


def solution(mesh):
    split = Mesh(
        mesh.devices.reshape(16, 2, 2, mesh.shape["expert"]), ("dp_0", "dp_1", "dp_2", "expert")
    )
    placed = (
        P(DP_EXPERT, None),
        P(DP_EXPERT, None),
        P(DP_EXPERT, None),
        P(DP_EXPERT, None),
        P(),
        P(DP, "expert"),
        P(DP, "expert"),
        P(DP, "expert"),
    )
    return jax.shard_map(
        per_device,
        mesh=split,
        in_specs=placed,
        out_specs=(P(DP_EXPERT, None), P(DP, "expert"), P(DP, "expert"), P(DP, "expert")),
        check_vma=False,
    )
```

profile of v0, /device:TPU:6, one launch (start us, length us, event | category | flops | bytes accessed | tf_op | source)
XLA Modules:
  0.0 303.3 jit_solution(7285531849207102941)
XLA Ops:
  7.2 0.0 copy-start
  7.2 0.0 copy-start.1
  7.2 0.0 copy-start.2
  7.2 0.8 select_reduce_fusion
  8.0 0.1 copy.16
  8.1 0.2 reduce-window.8
  8.3 0.1 add_reduce_fusion
  8.4 1.6 convolution_convert_fusion.1
  10.1 16.7 %all_to_all.20 = bf16[8,16,2048]{2,1,0:T(8,128)(2,1)S(1)} all-to-all(bf16[8,16,2048]{2,1,0:T(8,128)(2,1)S(1)} %broadcast_in_dim.26), channel_id=1, replica_groups=mesh['dp_0'=16,'dp_1'=2,'dp_2'=2,'expert'=8] {'expert'}, dimensions={0} | all-to-all | bytes 1048576 | tf_op jit(solution)/shard_map/all_to_all | solution.py:13
  26.8 1.6 broadcast_in_dim.23
  28.3 16.2 %all-to-all-start.1 = ((bf16[64,32,128]{2,1,0:T(8,128)(2,1)}), bf16[64,32,128]{2,1,0:T(8,128)(2,1)S(1)}, u32[]{:S(2)}, u32[]{:S(2)}) async-start(bf16[64,32,128]{2,1,0:T(8,128)(2,1)} %broadcast_in_dim.23), calls=%async_computation.1 | async-start | bytes 1048576 | tf_op jit(solution)/shard_map/all_to_all | solution.py:13
  44.5 0.0 all-gather.2.cloned.1.call-start
  44.6 0.0 copy-done.1
  44.6 0.0 copy-done.2
  44.6 0.6 pad_maximum_fusion.1
  45.2 0.1 all-gather.2.cloned.1.call-update
  45.3 0.0 copy-done
  45.3 0.2 convolution_convert_fusion.2
  45.5 33.1 %all-to-all-done.1 = bf16[64,32,128]{2,1,0:T(8,128)(2,1)S(1)} async-done(((bf16[64,32,128]{2,1,0:T(8,128)(2,1)}), bf16[64,32,128]{2,1,0:T(8,128)(2,1)S(1)}, u32[]{:S(2)}, u32[]{:S(2)}) %all-to-all-start.1) | async-done | bytes 524320 | tf_op jit(solution)/shard_map/all_to_all | solution.py:13
  78.6 0.8 broadcast_in_dim.22
  79.4 5.6 %all-to-all-start = ((bf16[8,16,2048]{2,1,0:T(8,128)(2,1)}), bf16[8,16,2048]{2,1,0:T(8,128)(2,1)S(1)}, u32[]{:S(2)}, u32[]{:S(2)}) async-start(bf16[8,16,2048]{2,1,0:T(8,128)(2,1)} %broadcast_in_dim.22), calls=%async_computation | async-start | bytes 1048576 | tf_op jit(solution)/shard_map/all_to_all | solution.py:13
  85.0 0.0 reduce-scatter.4.cloned.1.call-start
  85.0 0.6 fusion.19
  86.3 0.3 fusion.23
  86.6 7.5 %all-to-all-done = bf16[8,16,2048]{2,1,0:T(8,128)(2,1)S(1)} async-done(((bf16[8,16,2048]{2,1,0:T(8,128)(2,1)}), bf16[8,16,2048]{2,1,0:T(8,128)(2,1)S(1)}, u32[]{:S(2)}, u32[]{:S(2)}) %all-to-all-start) | async-done | bytes 524320 | tf_op jit(solution)/shard_map/all_to_all | solution.py:13
  94.0 73.5 %all-gather.2.cloned.1.call-done = bf16[2048,256]{1,0:T(8,128)(2,1)} async-done(((bf16[32,256]{1,0:T(8,128)(2,1)}), bf16[2048,256]{1,0:T(8,128)(2,1)}) %all-gather.2.cloned.1.call-update) | async-done | bytes 1048592 | tf_op jit(solution)/shard_map/all_gather | solution.py:33
  167.5 1.3 fusion.5
  168.8 1.3 multiply_convert_fusion.2
  170.2 0.3 convolution_multiply_fusion
  170.5 0.4 convolution_multiply_fusion.1
  170.9 0.4 convolution_multiply_fusion.2
  171.3 2.1 pad_maximum_fusion
  173.3 3.5 %copy.17 = f32[2048,384]{1,0:T(8,128)} copy(f32[2048,384]{0,1:T(8,128)} %pad_maximum_fusion) | data formatting | bytes 6291456 | tf_op jit(solution)/shard_map/concatenate | solution.py:114
  176.9 3.9 %copy.18 = f32[2,16,2,32,384]{4,3,2,1,0:T(8,128)} copy(f32[2,16,2,32,384]{4,3,0,2,1:T(8,128)} %bitcast.25) | data formatting | bytes 6291456 | tf_op jit(solution)/shard_map/transpose | solution.py:50
  180.8 0.0 reduce-scatter.4.cloned.1.call-update
  180.8 0.0 reduce-scatter.6.cloned.1.call-start
  180.8 17.8 %reduce-scatter.4.cloned.1.call-done = f32[32,32,384]{2,1,0:T(8,128)} async-done(((f32[64,32,384]{2,1,0:T(8,128)}), f32[32,32,384]{2,1,0:T(8,128)}) %reduce-scatter.4.cloned.1.call-update) | async-done | bytes 1572880 | tf_op jit(solution)/shard_map/reduce_scatter | solution.py:53
  198.6 0.0 reduce-scatter.6.cloned.1.call-update
  198.6 0.0 reduce-scatter.8.cloned.1.call-start
  198.7 0.3 convolution_convert_fusion
  199.0 17.0 %all_to_all.21 = bf16[8,16,2048]{2,1,0:T(8,128)(2,1)S(1)} all-to-all(bf16[8,16,2048]{2,1,0:T(8,128)(2,1)S(1)} %bitcast.34), channel_id=1, replica_groups=mesh['dp_0'=16,'dp_1'=2,'dp_2'=2,'expert'=8] {'expert'}, dimensions={0} | all-to-all | bytes 1048576 | tf_op jit(solution)/shard_map/all_to_all | solution.py:43
  216.0 0.1 convert_reduce_fusion
  216.1 58.7 %reduce-scatter.6.cloned.1.call-done = f32[2,32,384]{2,1,0:T(8,128)} async-done(((f32[32,32,384]{2,1,0:T(8,128)}), f32[2,32,384]{2,1,0:T(8,128)}) %reduce-scatter.6.cloned.1.call-update) | async-done | bytes 98320 | tf_op jit(solution)/shard_map/reduce_scatter | solution.py:53
  274.8 0.0 reduce-scatter.8.cloned.1.call-update
  274.8 1.4 fusion
  276.2 19.1 %reduce-scatter.8.cloned.1.call-done = f32[1,32,384]{2,1,0:T(8,128)} async-done(((f32[2,32,384]{2,1,0:T(8,128)}), f32[1,32,384]{2,1,0:T(8,128)}) %reduce-scatter.8.cloned.1.call-update) | async-done | bytes 49168 | tf_op jit(solution)/shard_map/reduce_scatter | solution.py:53
  295.3 0.8 convert_bitcast_fusion
  296.2 0.6 fusion.22
  (5 shorter events, 0.1 us)
Async XLA Ops:
  7.2 38.1 %copy-start = (bf16[128,2048]{1,0:T(8,128)(2,1)S(1)}, bf16[128,2048]{1,0:T(8,128)(2,1)}, u32[]{:S(2)}) copy-start(bf16[128,2048]{1,0:T(8,128)(2,1)} %param.8) | copy-start | bytes 1572868
  7.2 37.4 %copy-start.1 = (bf16[32,128]{1,0:T(8,128)(2,1)S(1)}, bf16[32,128]{1,0:T(8,128)(2,1)}, u32[]{:S(2)}) copy-start(bf16[32,128]{1,0:T(8,128)(2,1)} %param.14) | copy-start | bytes 24580
  7.2 37.4 %copy-start.2 = (bf16[32,128]{1,0:T(8,128)(2,1)S(1)}, bf16[32,128]{1,0:T(8,128)(2,1)}, u32[]{:S(2)}) copy-start(bf16[32,128]{1,0:T(8,128)(2,1)} %param.13) | copy-start | bytes 24580
  8.1 76.9 %copy-start.3 = (s32[64]{0:T(128)S(1)}, s32[64]{0:T(128)}, u32[]{:S(2)}) copy-start(s32[64]{0:T(128)} %param.12) | copy-start | bytes 772
  28.3 50.3 %all-to-all-start.1 = ((bf16[64,32,128]{2,1,0:T(8,128)(2,1)}), bf16[64,32,128]{2,1,0:T(8,128)(2,1)S(1)}, u32[]{:S(2)}, u32[]{:S(2)}) async-start(bf16[64,32,128]{2,1,0:T(8,128)(2,1)} %broadcast_in_dim.23), calls=%async_computation.1 | async-start | bytes 1048576 | tf_op jit(solution)/shard_map/all_to_all | solution.py:13
  44.5 123.0 %all-gather.2.cloned.1.call-start = ((), (), s32[]{:S(2)}) async-start(), calls=%async_computation.7 | async-start | bytes 1064960 | tf_op jit(solution)/shard_map/all_gather | solution.py:33
  79.4 14.6 %all-to-all-start = ((bf16[8,16,2048]{2,1,0:T(8,128)(2,1)}), bf16[8,16,2048]{2,1,0:T(8,128)(2,1)S(1)}, u32[]{:S(2)}, u32[]{:S(2)}) async-start(bf16[8,16,2048]{2,1,0:T(8,128)(2,1)} %broadcast_in_dim.22), calls=%async_computation | async-start | bytes 1048576 | tf_op jit(solution)/shard_map/all_to_all | solution.py:13
  85.0 113.6 %reduce-scatter.4.cloned.1.call-start = ((), (), s32[]{:S(2)}) async-start(), calls=%async_computation.8 | async-start | bytes 4718592 | tf_op jit(solution)/shard_map/reduce_scatter | solution.py:53
  180.8 94.0 %reduce-scatter.6.cloned.1.call-start = ((), (), s32[]{:S(2)}) async-start(), calls=%async_computation.9 | async-start | bytes 1671168 | tf_op jit(solution)/shard_map/reduce_scatter | solution.py:53
  198.6 96.7 %reduce-scatter.8.cloned.1.call-start = ((), (), s32[]{:S(2)}) async-start(), calls=%async_computation.10 | async-start | bytes 147456 | tf_op jit(solution)/shard_map/reduce_scatter | solution.py:53
Sparse Core Ops, SparseCore 0:
  47.5 119.9 all-gather.1
  180.9 17.6 reduce-scatter.3
  201.7 73.0 reduce-scatter.5
  277.4 17.9 reduce-scatter.7
where the time goes:
time: 305 us; the launch traced here: 303 us
  waiting for transfers between devices  210 us (69%)
  blocking collectives  33.7 us (11%)
  starting transfers between devices  21.9 us (7%)
  between operations  14.5 us (5%)
  local copies, waits for them, and re-layouts  10.6 us (3%)
  matrix products  7.53 us (2%)
  other arithmetic  5.24 us (2%)
    reduce_scatter x3, waiting for transfers between devices, sum_in_order(): blocks = lax.psum_scatter(blocks, axes[k], scatter_dimension=0, tiled=True)  95.6 us
    all_gather x1, waiting for transfers between devices, side_by_side(): lax.all_gather(both, axis, axis=dim, tiled=True)  73.5 us
    all_to_all x2, waiting for transfers between devices, from_everyone(): return lax.all_to_all(copies, axis, split_axis=0, concat_axis=0, tiled=True)  40.6 us
    all_to_all x2, starting transfers between devices, from_everyone(): return lax.all_to_all(copies, axis, split_axis=0, concat_axis=0, tiled=True)  21.8 us
    all_to_all x1, blocking collectives, sent_and_summed(): lax.all_to_all(in_blocks(shard, dim, length), axis, 0, 0, tiled=True)  17 us
    all_to_all x1, blocking collectives, from_everyone(): return lax.all_to_all(copies, axis, split_axis=0, concat_axis=0, tiled=True)  16.7 us
  transfers between devices with their start and end apart: 6, of which 6 were waited for; matrix products, arithmetic and copies ran while one was open for 1% of the time, Pallas kernels for 0%

commit v1 on v0

v1 whole, which is shorter than its diff:
```python
import jax
import jax.numpy as jnp
from jax import lax
from jax.experimental import pallas as pl
from jax.experimental.pallas import tpu as pltpu
from jax.sharding import Mesh
from jax.sharding import PartitionSpec as P

AXES = ("z", "y", "c", "h", "x")
PLANE = ("y", "h", "x")
SWAP = ((0, 1), (1, 0))
VMEM_LIMIT = 40 * 1024 * 1024
PARAMS = pltpu.CompilerParams(vmem_limit_bytes=VMEM_LIMIT)
ROW_DIMS = (((0,), (0,)), ((), ()))
LANE_DIMS = (((1,), (1,)), ((), ()))


def whole(n):
    return [pl.BlockSpec(memory_space=pltpu.VMEM) for _ in range(n)]


def lanes(shape):
    return lax.broadcasted_iota(jnp.int32, shape, 1)


def halves_swapped(a):
    half = a.shape[1] // 2
    return pltpu.roll(a.astype(jnp.float32), half, 1)


def route_kernel(ids_ref, share_ref, tokens_ref, cot_ref, both_ref, place_ref, slot_weight_ref):
    count = ids_ref.shape[0]
    slots = both_ref.shape[0] // 2
    chosen = ids_ref[...] == 0
    routed = jnp.max(chosen.astype(jnp.float32), axis=1, keepdims=True)
    weight = jnp.sum(jnp.where(chosen, share_ref[...], 0.0), axis=1, keepdims=True)
    square = (count, count)
    below = lax.broadcasted_iota(jnp.int32, square, 0) >= lanes(square)
    before = jnp.dot(
        below.astype(jnp.bfloat16),
        jnp.broadcast_to(routed, square).astype(jnp.bfloat16),
        preferred_element_type=jnp.float32,
    )
    at_slot = (before - 1.0 == lanes(square).astype(jnp.float32)) & (routed > 0.0)
    place = at_slot.astype(jnp.float32)
    chooser = place.T[:slots].astype(jnp.bfloat16)
    slot_weight = jnp.sum((place * weight).T[:slots], axis=1, keepdims=True)
    picked = jnp.dot(chooser, tokens_ref[...], preferred_element_type=jnp.float32)
    dpicked = jnp.dot(chooser, cot_ref[...], preferred_element_type=jnp.float32) * slot_weight
    both_ref[:slots, :] = picked.astype(jnp.bfloat16)
    both_ref[slots:, :] = dpicked.astype(jnp.bfloat16)
    place_ref[...] = place.astype(jnp.bfloat16)
    slot_weight_ref[...] = jnp.broadcast_to(slot_weight, slot_weight_ref.shape)


def route(ids, share, tokens, cot):
    count, width = tokens.shape
    slots = count // 8
    return pl.pallas_call(
        route_kernel,
        out_shape=(
            jax.ShapeDtypeStruct((2 * slots, width), jnp.bfloat16),
            jax.ShapeDtypeStruct((count, count), jnp.bfloat16),
            jax.ShapeDtypeStruct((slots, 128), jnp.float32),
        ),
        in_specs=whole(4),
        out_specs=tuple(whole(3)),
        compiler_params=PARAMS,
        name="route",
    )(ids, share, tokens, cot)


def half_kernel(gate_ref, up_ref, mine_ref, other_ref):
    gate, up = gate_ref[...].astype(jnp.float32), up_ref[...].astype(jnp.float32)
    low = lanes(gate.shape) < gate.shape[1] // 2
    first = jnp.where(low, gate, halves_swapped(up)).astype(jnp.bfloat16)
    second = jnp.where(low, halves_swapped(gate), up).astype(jnp.bfloat16)
    top = lax.axis_index("y") == 0
    mine_ref[...] = jnp.where(top, first, second)
    other_ref[...] = jnp.where(top, second, first)


def split_columns(gate, up):
    return pl.pallas_call(
        half_kernel,
        out_shape=(jax.ShapeDtypeStruct(gate.shape, gate.dtype),) * 2,
        in_specs=whole(2),
        out_specs=tuple(whole(2)),
        name="split_columns",
    )(gate, up)


def pack_kernel(mine_ref, got_ref, down_ref, packed_ref):
    rows = mine_ref.shape[0]
    top = lax.axis_index("y") == 0
    mine, got = mine_ref[...], got_ref[:rows, :]
    packed_ref[:rows, :] = jnp.where(top, mine, got)
    packed_ref[rows : 2 * rows, :] = jnp.where(top, got, mine)
    down, their_down = down_ref[...].astype(jnp.float32), got_ref[rows:, :].astype(jnp.float32)
    low = lanes(down.shape) < down.shape[1] // 2
    if_top = jnp.where(low, down, halves_swapped(their_down))
    if_not = jnp.where(low, halves_swapped(their_down), down)
    packed_ref[2 * rows :, :] = jnp.where(top, if_top, if_not).astype(jnp.bfloat16)


def pack_shards(mine, got, down):
    rows, width = mine.shape
    return pl.pallas_call(
        pack_kernel,
        out_shape=jax.ShapeDtypeStruct((3 * rows, width), mine.dtype),
        in_specs=whole(3),
        out_specs=whole(1)[0],
        name="pack_shards",
    )(mine, got, down)


def expert_kernel(
    join_ref, both_ref, packed_ref, partial_ref, send_ref, keep_ref, gate_up, down, terms
):
    chips = packed_ref.shape[1]
    rows = packed_ref.shape[2] // 3
    width = packed_ref.shape[3]
    half = width // 2
    peers, slots = both_ref.shape[0], both_ref.shape[1] // 2
    depth = both_ref.shape[2]
    z, c = lax.axis_index("z"), lax.axis_index("c")
    for chip in range(chips):
        for core in range(2):
            block = packed_ref[core, chip, 2 * rows :, :].astype(jnp.float32)
            turned = pltpu.roll(block, half, 1)
            low = lanes(block.shape) < half
            doubled = (jnp.where(low, block, turned), jnp.where(low, turned, block))
            for y in range(2):
                at = ((chip * 2 + y) * 2 + core) * rows
                gate_up[at : at + rows, :] = packed_ref[core, chip, y * rows : (y + 1) * rows, :]
                down[at : at + rows, :] = doubled[y].astype(jnp.bfloat16)
    total = peers * slots
    picked = both_ref[:, :slots, :].reshape(total, depth)
    dpicked = both_ref[:, slots:, :].reshape(total, depth)
    acts = jnp.dot(picked, gate_up[...], preferred_element_type=jnp.float32)
    turned = pltpu.roll(acts, half, 1)
    low = lanes(acts.shape) < half
    gate, up = jnp.where(low, acts, turned), jnp.where(low, turned, acts)
    sigma = jax.nn.sigmoid(gate)
    hidden = gate * sigma * up
    hidden_half = hidden.astype(jnp.bfloat16)
    partial = lax.dot_general(
        jnp.where(low, hidden, 0.0).astype(jnp.bfloat16),
        down[...],
        LANE_DIMS,
        preferred_element_type=jnp.float32,
    )
    partial_ref[...] = partial.astype(jnp.bfloat16).reshape(partial_ref.shape)
    dhidden = jnp.dot(dpicked, down[...], preferred_element_type=jnp.float32)
    dgate = dhidden * up * sigma * (1.0 + gate * (1.0 - sigma))
    dup = dhidden * gate * sigma
    first = 1.0 - join_ref[(z * 2 + 0) * 2 + c].astype(jnp.float32)
    second = 1.0 - join_ref[(z * 2 + 1) * 2 + c].astype(jnp.float32)
    group = lax.broadcasted_iota(jnp.int32, acts.shape, 0) // (total // 2)
    active = jnp.where(group == 0, first, second)
    dacts = (jnp.where(low, dgate, dup) * active).astype(jnp.bfloat16)
    counted = (hidden_half.astype(jnp.float32) * active).astype(jnp.bfloat16)
    terms[0] = lax.dot_general(picked, dacts, ROW_DIMS, preferred_element_type=jnp.float32)
    terms[1] = lax.dot_general(dpicked, counted, ROW_DIMS, preferred_element_type=jnp.float32)
    half_rows = rows // 2
    low = lanes((half_rows, width)) < half
    for chip in range(chips):
        for y in range(2):
            base = (chip * 2 + y) * 2 * rows
            for which, ref in ((c, keep_ref), (1 - c, send_ref)):
                at = pl.multiple_of(base + which * rows, rows)
                ref[chip, y, :rows, :] = terms[0, pl.ds(at, rows), :].astype(ref.dtype)
                packed = jnp.where(
                    low,
                    terms[1, pl.ds(at, half_rows), :],
                    terms[1, pl.ds(at + half_rows, half_rows), :],
                )
                ref[chip, y, rows:, :] = packed.astype(ref.dtype)


def expert(join, both, packed):
    peers, doubled, depth = both.shape
    slots = doubled // 2
    _, chips, rows, width = packed.shape
    chunk = (chips, 2, rows // 2, width)
    return pl.pallas_call(
        expert_kernel,
        out_shape=(
            jax.ShapeDtypeStruct((peers, slots, depth), jnp.bfloat16),
            jax.ShapeDtypeStruct(chunk, jnp.bfloat16),
            jax.ShapeDtypeStruct(chunk, jnp.float32),
        ),
        in_specs=[pl.BlockSpec(memory_space=pltpu.SMEM), *whole(2)],
        out_specs=tuple(whole(3)),
        scratch_shapes=[
            pltpu.VMEM((depth, width), jnp.bfloat16),
            pltpu.VMEM((depth, width), jnp.bfloat16),
            pltpu.VMEM((2, depth, width), jnp.float32),
        ],
        compiler_params=PARAMS,
        name="expert",
    )(join, both, packed)


def mix_kernel(blocks_ref, place_ref, slot_weight_ref, mixed_ref):
    slots = blocks_ref.shape[1]
    total = blocks_ref[0].astype(jnp.float32)
    for k in range(1, blocks_ref.shape[0]):
        total += blocks_ref[k].astype(jnp.float32)
    weighted = (total * slot_weight_ref[:, :1]).astype(jnp.bfloat16)
    mixed_ref[...] = jnp.dot(
        place_ref[:, :slots], weighted, preferred_element_type=jnp.float32
    ).astype(jnp.bfloat16)


def mix(blocks, place, slot_weight):
    return pl.pallas_call(
        mix_kernel,
        out_shape=jax.ShapeDtypeStruct((place.shape[0], blocks.shape[2]), jnp.bfloat16),
        in_specs=whole(3),
        out_specs=whole(1)[0],
        compiler_params=PARAMS,
        name="mix",
    )(blocks, place, slot_weight)


def finish_kernel(blocks_ref, gate_ref, up_ref, down_ref):
    rows, width = gate_ref.shape
    half = width // 2
    sums = [blocks_ref[y].astype(jnp.float32) for y in range(2)]
    for k in range(2, blocks_ref.shape[0], 2):
        for y in range(2):
            sums[y] += blocks_ref[k + y].astype(jnp.float32)
    low = lanes(sums[0].shape) < half
    firsts = jnp.where(low, sums[0], pltpu.roll(sums[1], half, 1)).astype(jnp.bfloat16)
    seconds = jnp.where(low, pltpu.roll(sums[0], half, 1), sums[1]).astype(jnp.bfloat16)
    gate_ref[...] = firsts[:rows]
    up_ref[...] = seconds[:rows]
    down_ref[: rows // 2, :] = firsts[rows:]
    down_ref[rows // 2 :, :] = seconds[rows:]


def finish(blocks):
    _, packed_rows, width = blocks.shape
    shape = jax.ShapeDtypeStruct((packed_rows // 3 * 2, width), jnp.bfloat16)
    return pl.pallas_call(
        finish_kernel,
        out_shape=(shape,) * 3,
        in_specs=whole(1),
        out_specs=tuple(whole(3)),
        name="finish",
    )(blocks)


def per_device(tokens, cotangent, expert_ids, route_weights, join_groups, w_gate, w_up, w_down):
    plane = lax.axis_size(PLANE)
    chips = lax.axis_size("z")
    mine, other = split_columns(w_gate, w_up)
    got = lax.ppermute(jnp.concatenate([other, w_down]), "y", SWAP)
    both, place, slot_weight = route(expert_ids, route_weights, tokens, cotangent)
    packed = pack_shards(mine, got, w_down)
    copies = jnp.broadcast_to(both, (plane, *both.shape))
    rows_in = lax.all_to_all(copies, PLANE, 0, 0, tiled=True)
    along = lax.all_gather(packed, "z", axis=0, tiled=False)
    gathered = lax.all_gather(along, "c", axis=0, tiled=False)
    partial, send, keep = expert(join_groups, rows_in, gathered)
    blocks = lax.all_to_all(partial, PLANE, 0, 0, tiled=True)
    from_core = lax.ppermute(send, "c", SWAP)
    chip_sum = (keep + from_core.astype(jnp.float32)).astype(jnp.bfloat16)
    chip_sum = chip_sum.reshape(chips * 2, *chip_sum.shape[2:])
    pieces = lax.all_to_all(chip_sum, ("z", "y"), 0, 0, tiled=True)
    mixed = mix(blocks, place, slot_weight)
    return (mixed, *finish(pieces))


def solution(mesh):
    experts = mesh.shape["expert"]
    split = Mesh(mesh.devices.reshape(-1, 2, 2, 2, experts // 2), AXES)
    dp = ("z", "y", "c")
    tok, weight = P(AXES, None), P(dp, ("h", "x"))
    return jax.shard_map(
        per_device,
        mesh=split,
        in_specs=(tok, tok, tok, tok, P(), weight, weight, weight),
        out_specs=(tok, weight, weight, weight),
        check_vma=False,
    )
```

time: 305 us -> 146 us (0.48)
  the two profiles are of different devices: /device:TPU:6 before, /device:TPU:8 now
where the time goes in v1:
time: 146 us; the launch traced here: 145 us
  waiting for transfers between devices  54.3 us (37%)
  blocking collectives  38.7 us (27%)
  starting transfers between devices  32.1 us (22%)
  Pallas kernels  9.08 us (6%)
  local copies, waits for them, and re-layouts  8.5 us (6%)
  other arithmetic  1.55 us (1%)
    all_gather x1, blocking collectives, per_device(): along = lax.all_gather(packed, 'z', axis=0, tiled=False)  36.4 us
    all_to_all x1, waiting for transfers between devices, per_device(): pieces = lax.all_to_all(chip_sum, ('z', 'y'), 0, 0, tiled=True)  25 us
    ppermute x1, waiting for transfers between devices, per_device(): got = lax.ppermute(jnp.concatenate([other, w_down]), 'y', SWAP)  15.9 us
    all_to_all x1, waiting for transfers between devices, per_device(): blocks = lax.all_to_all(partial, PLANE, 0, 0, tiled=True)  11.7 us
    all_to_all x1, starting transfers between devices, per_device(): blocks = lax.all_to_all(partial, PLANE, 0, 0, tiled=True)  10 us
    all_to_all x1, starting transfers between devices, per_device(): rows_in = lax.all_to_all(copies, PLANE, 0, 0, tiled=True)  9.51 us
    all_to_all x1, starting transfers between devices, per_device(): pieces = lax.all_to_all(chip_sum, ('z', 'y'), 0, 0, tiled=True)  8.58 us
    unnamed x20, local copies, waits for them, and re-layouts  6.89 us
  transfers between devices with their start and end apart: 5, of which 4 were waited for; matrix products, arithmetic and copies ran while one was open for 1% of the time, Pallas kernels for 3%

profile of v1, /device:TPU:8, one launch (start us, length us, event | category | flops | bytes accessed | tf_op | source)
XLA Modules:
  0.0 144.9 jit_solution(10467882325451055840)
XLA Ops:
  0.6 0.8 copy.14.ids_ref
  1.4 0.8 copy.15.share_ref
  2.2 0.0 copy-start.3
  2.2 1.0 copy-done.3
  3.2 0.0 copy-start.4
  3.2 1.0 copy-done.4
  4.3 0.5 route.1
  4.8 1.6 %broadcast_in_dim.3 = bf16[16,32,2048]{2,1,0:T(8,128)(2,1)} broadcast(bf16[32,2048]{1,0:T(8,128)(2,1)S(1)} %get-tuple-element.15), dimensions={1,2} | broadcast | bytes 2228224 | tf_op jit(solution)/shard_map/broadcast_in_dim | solution.py:262
  6.4 0.0 copy-start.7
  6.4 0.0 copy-start.5
  6.4 9.5 %all-to-all-start = ((bf16[16,32,2048]{2,1,0:T(8,128)(2,1)}), bf16[16,32,2048]{2,1,0:T(8,128)(2,1)S(1)}, u32[]{:S(2)}, u32[]{:S(2)}) async-start(bf16[16,32,2048]{2,1,0:T(8,128)(2,1)} %broadcast_in_dim.3), calls=%async_computation | async-start | bytes 4194304 | tf_op jit(solution)/shard_map/all_to_all | solution.py:263
  15.9 1.4 split_columns.1
  17.3 0.0 copy-done.7
  17.3 0.7 pad_maximum_fusion
  18.0 2.1 %collective-permute-start = (bf16[64,128]{1,0:T(8,128)(2,1)S(1)}, bf16[64,128]{1,0:T(8,128)(2,1)S(1)}, u32[]{:S(2)}, u32[]{:S(2)}) collective-permute-start(bf16[64,128]{1,0:T(8,128)(2,1)S(1)} %pad_maximum_fusion), channel_id=1, source_target_pairs={{0,16},{16,0},{1,17},{17,1},{2,18},{18,2},{3,19},{19,3},{4,20},{20... | collective-permute-start | bytes 49160 | tf_op jit(solution)/shard_map/ppermute | solution.py:259
  20.1 15.9 %collective-permute-done.got_ref = bf16[64,128]{1,0:T(8,128)(2,1)S(1)} collective-permute-done((bf16[64,128]{1,0:T(8,128)(2,1)S(1)}, bf16[64,128]{1,0:T(8,128)(2,1)S(1)}, u32[]{:S(2)}, u32[]{:S(2)}) %collective-permute-start) | collective-permute-done | bytes 16416 | tf_op jit(solution)/shard_map/ppermute | solution.py:259
  36.0 0.0 copy-start.8
  36.0 0.6 copy-done.8
  36.6 1.4 pack_shards.1
  38.0 36.4 %all-gather = bf16[1536,128]{1,0:T(8,128)(2,1)S(1)} all-gather(bf16[96,128]{1,0:T(8,128)(2,1)} %pack_shards.1), channel_id=2, replica_groups=mesh['z'=16,'y'=2,'c'=2,'h'=2,'x'=4] {'z'}, dimensions={0}, use_global_device_ids=true | all-gather | bytes 417792 | tf_op jit(solution)/shard_map/all_gather | solution.py:264
  74.4 2.4 %all-gather.1 = bf16[32,96,128]{2,1,0:T(8,128)(2,1)S(1)} all-gather(bf16[16,96,128]{2,1,0:T(8,128)(2,1)S(1)} %bitcast.4), channel_id=3, replica_groups=mesh['z'=16,'y'=2,'c'=2,'h'=2,'x'=4] {'c'}, dimensions={0}, use_global_device_ids=true | all-gather | bytes 1179648 | tf_op jit(solution)/shard_map/all_gather | solution.py:265
  76.8 0.0 all-to-all-done.both_ref
  76.8 0.0 copy-done.5
  76.8 2.9 %expert.1 = (bf16[16,16,2048]{2,1,0:T(8,128)(2,1)S(1)}, bf16[16,2,48,128]{3,2,1,0:T(8,128)(2,1)S(1)}, f32[16,2,48,128]{3,2,1,0:T(8,128)S(1)}) custom-call(s32[64]{0:T(128)S(1)} %copy-done.5, bf16[16,32,2048]{2,1,0:T(8,128)(2,1)S(1)} %all-to-all-done.both_ref, bf16[2,16,96,128]{3,2,1,0:T(8,128)(2,1)S(1)} %bitcast.3), custom_call_target="tpu_custom_call" | custom-call | tf_op jit(solution)/shard_map/expert/pallas_call | solution.py:186
  79.7 0.0 copy-start
  79.7 1.0 copy-done
  80.7 0.0 copy-start.1
  80.7 0.9 copy-done.1
  81.6 0.0 copy-start.2
  81.6 10.0 %all-to-all-start.1 = ((bf16[16,16,2048]{2,1,0:T(8,128)(2,1)}), bf16[16,16,2048]{2,1,0:T(8,128)(2,1)S(1)}, u32[]{:S(2)}, u32[]{:S(2)}) async-start(bf16[16,16,2048]{2,1,0:T(8,128)(2,1)} %copy-done), calls=%async_computation.1 | async-start | bytes 2097152 | tf_op jit(solution)/shard_map/all_to_all | solution.py:267
  91.6 1.9 %collective-permute-start.1 = (bf16[16,2,48,128]{3,2,1,0:T(8,128)(2,1)S(1)}, bf16[16,2,48,128]{3,2,1,0:T(8,128)(2,1)S(1)}, u32[]{:S(2)}, u32[]{:S(2)}) collective-permute-start(bf16[16,2,48,128]{3,2,1,0:T(8,128)(2,1)S(1)} %get-tuple-element.22), channel_id=1, source_target_pairs={{0,8},{8,0},{1,9},{9,1},{2,10},{10,2},{3,11},{11,3},{4,12},{12,4},... | collective-permute-start | bytes 1179656 | tf_op jit(solution)/shard_map/ppermute | solution.py:268
  93.5 1.7 %collective-permute-done.1 = bf16[16,2,48,128]{3,2,1,0:T(8,128)(2,1)S(1)} collective-permute-done((bf16[16,2,48,128]{3,2,1,0:T(8,128)(2,1)S(1)}, bf16[16,2,48,128]{3,2,1,0:T(8,128)(2,1)S(1)}, u32[]{:S(2)}, u32[]{:S(2)}) %collective-permute-start.1) | collective-permute-done | bytes 393248 | tf_op jit(solution)/shard_map/ppermute | solution.py:268
  95.2 0.0 copy-done.2
  95.2 0.8 add_convert_fusion
  96.1 11.7 %all-to-all-done.1.blocks_ref = bf16[16,16,2048]{2,1,0:T(8,128)(2,1)S(1)} async-done(((bf16[16,16,2048]{2,1,0:T(8,128)(2,1)}), bf16[16,16,2048]{2,1,0:T(8,128)(2,1)S(1)}, u32[]{:S(2)}, u32[]{:S(2)}) %all-to-all-start.1) | async-done | bytes 1048608 | tf_op jit(solution)/shard_map/all_to_all | solution.py:267
  107.8 8.6 %all-to-all-start.2 = ((bf16[32,48,128]{2,1,0:T(8,128)(2,1)}), bf16[32,48,128]{2,1,0:T(8,128)(2,1)S(1)}, u32[]{:S(2)}, u32[]{:S(2)}) async-start(bf16[32,48,128]{2,1,0:T(8,128)(2,1)} %bitcast.2), calls=%async_computation.2 | async-start | bytes 786432 | tf_op jit(solution)/shard_map/all_to_all | solution.py:271
  116.4 1.2 mix.1
  117.5 25.0 %all-to-all-done.2.blocks_ref = bf16[32,48,128]{2,1,0:T(8,128)(2,1)S(1)} async-done(((bf16[32,48,128]{2,1,0:T(8,128)(2,1)}), bf16[32,48,128]{2,1,0:T(8,128)(2,1)S(1)}, u32[]{:S(2)}, u32[]{:S(2)}) %all-to-all-start.2) | async-done | bytes 393248 | tf_op jit(solution)/shard_map/all_to_all | solution.py:271
  142.5 0.0 copy-start.6
  142.5 0.8 copy-done.6
  143.2 1.7 %finish.1 = (bf16[32,128]{1,0:T(8,128)(2,1)}, bf16[32,128]{1,0:T(8,128)(2,1)}, bf16[32,128]{1,0:T(8,128)(2,1)}) custom-call(bf16[32,48,128]{2,1,0:T(8,128)(2,1)} %copy-done.6), custom_call_target="tpu_custom_call" | custom-call | tf_op jit(solution)/shard_map/finish/pallas_call | solution.py:246
Async XLA Ops:
  2.2 1.0 copy-start.3
  3.2 1.0 copy-start.4
  6.4 10.9 %copy-start.7 = (bf16[32,128]{1,0:T(8,128)(2,1)S(1)}, bf16[32,128]{1,0:T(8,128)(2,1)}, u32[]{:S(2)}) copy-start(bf16[32,128]{1,0:T(8,128)(2,1)} %down_ref.1) | copy-start | bytes 24580
  6.4 70.4 %copy-start.5 = (s32[64]{0:T(128)S(1)}, s32[64]{0:T(128)}, u32[]{:S(2)}) copy-start(s32[64]{0:T(128)} %join_ref.1) | copy-start | bytes 772
  6.4 70.4 %all-to-all-start = ((bf16[16,32,2048]{2,1,0:T(8,128)(2,1)}), bf16[16,32,2048]{2,1,0:T(8,128)(2,1)S(1)}, u32[]{:S(2)}, u32[]{:S(2)}) async-start(bf16[16,32,2048]{2,1,0:T(8,128)(2,1)} %broadcast_in_dim.3), calls=%async_computation | async-start | bytes 4194304 | tf_op jit(solution)/shard_map/all_to_all | solution.py:263
  18.0 18.0 %collective-permute-start = (bf16[64,128]{1,0:T(8,128)(2,1)S(1)}, bf16[64,128]{1,0:T(8,128)(2,1)S(1)}, u32[]{:S(2)}, u32[]{:S(2)}) collective-permute-start(bf16[64,128]{1,0:T(8,128)(2,1)S(1)} %pad_maximum_fusion), channel_id=1, source_target_pairs={{0,16},{16,0},{1,17},{17,1},{2,18},{18,2},{3,19},{19,3},{4,20},{20... | collective-permute-start | bytes 49160 | tf_op jit(solution)/shard_map/ppermute | solution.py:259
  36.0 0.6 copy-start.8
  79.7 1.0 copy-start
  80.7 0.9 copy-start.1
  81.6 13.6 %copy-start.2 = (f32[16,2,48,128]{3,2,1,0:T(8,128)S(1)}, f32[16,2,48,128]{3,2,1,0:T(8,128)}, u32[]{:S(2)}) copy-start(f32[16,2,48,128]{3,2,1,0:T(8,128)} %copy-done.1) | copy-start | bytes 2359300
  81.6 26.2 %all-to-all-start.1 = ((bf16[16,16,2048]{2,1,0:T(8,128)(2,1)}), bf16[16,16,2048]{2,1,0:T(8,128)(2,1)S(1)}, u32[]{:S(2)}, u32[]{:S(2)}) async-start(bf16[16,16,2048]{2,1,0:T(8,128)(2,1)} %copy-done), calls=%async_computation.1 | async-start | bytes 2097152 | tf_op jit(solution)/shard_map/all_to_all | solution.py:267
  91.6 3.6 %collective-permute-start.1 = (bf16[16,2,48,128]{3,2,1,0:T(8,128)(2,1)S(1)}, bf16[16,2,48,128]{3,2,1,0:T(8,128)(2,1)S(1)}, u32[]{:S(2)}, u32[]{:S(2)}) collective-permute-start(bf16[16,2,48,128]{3,2,1,0:T(8,128)(2,1)S(1)} %get-tuple-element.22), channel_id=1, source_target_pairs={{0,8},{8,0},{1,9},{9,1},{2,10},{10,2},{3,11},{11,3},{4,12},{12,4},... | collective-permute-start | bytes 1179656 | tf_op jit(solution)/shard_map/ppermute | solution.py:268
  107.8 34.7 %all-to-all-start.2 = ((bf16[32,48,128]{2,1,0:T(8,128)(2,1)}), bf16[32,48,128]{2,1,0:T(8,128)(2,1)S(1)}, u32[]{:S(2)}, u32[]{:S(2)}) async-start(bf16[32,48,128]{2,1,0:T(8,128)(2,1)} %bitcast.2), calls=%async_computation.2 | async-start | bytes 786432 | tf_op jit(solution)/shard_map/all_to_all | solution.py:271
  142.5 0.8 copy-start.6

commit v2 on v1

--- a/solution.py
+++ b/solution.py
@@ -7,10 +7,10 @@
 from jax.sharding import PartitionSpec as P
 
 AXES = ("z", "y", "c", "h", "x")
+RING = ("y", "h")
 PLANE = ("y", "h", "x")
+HBM = pl.BlockSpec(memory_space=pltpu.HBM)
 SWAP = ((0, 1), (1, 0))
-VMEM_LIMIT = 40 * 1024 * 1024
-PARAMS = pltpu.CompilerParams(vmem_limit_bytes=VMEM_LIMIT)
 ROW_DIMS = (((0,), (0,)), ((), ()))
 LANE_DIMS = (((1,), (1,)), ((), ()))
 
@@ -28,94 +28,131 @@
     return pltpu.roll(a.astype(jnp.float32), half, 1)
 
 
-def route_kernel(ids_ref, share_ref, tokens_ref, cot_ref, both_ref, place_ref, slot_weight_ref):
-    count = ids_ref.shape[0]
-    slots = both_ref.shape[0] // 2
+def params(mib):
+    return pltpu.CompilerParams(vmem_limit_bytes=mib * 1024 * 1024)
+
+
+def route_kernel(
+    ids_ref, share_ref, tokens_ref, cot_ref, copies_ref, chooser_ref, slot_weight_ref,
+    held_tokens, held_cot, both, in_sems, out_sem,
+):
+    count = ids_ref.shape[1]
+    slots = chooser_ref.shape[0]
+    reads = [
+        pltpu.make_async_copy(tokens_ref, held_tokens, in_sems.at[0]),
+        pltpu.make_async_copy(cot_ref, held_cot, in_sems.at[1]),
+    ]
+    for read in reads:
+        read.start()
     chosen = ids_ref[...] == 0
-    routed = jnp.max(chosen.astype(jnp.float32), axis=1, keepdims=True)
-    weight = jnp.sum(jnp.where(chosen, share_ref[...], 0.0), axis=1, keepdims=True)
+    routed = jnp.max(chosen.astype(jnp.float32), axis=0, keepdims=True)
+    weight = jnp.sum(jnp.where(chosen, share_ref[...], 0.0), axis=0, keepdims=True)
     square = (count, count)
-    below = lax.broadcasted_iota(jnp.int32, square, 0) >= lanes(square)
+    until = lax.broadcasted_iota(jnp.int32, square, 0) <= lanes(square)
     before = jnp.dot(
-        below.astype(jnp.bfloat16),
-        jnp.broadcast_to(routed, square).astype(jnp.bfloat16),
+        jnp.broadcast_to(routed, (slots, count)).astype(jnp.bfloat16),
+        until.astype(jnp.bfloat16),
         preferred_element_type=jnp.float32,
     )
-    at_slot = (before - 1.0 == lanes(square).astype(jnp.float32)) & (routed > 0.0)
-    place = at_slot.astype(jnp.float32)
-    chooser = place.T[:slots].astype(jnp.bfloat16)
-    slot_weight = jnp.sum((place * weight).T[:slots], axis=1, keepdims=True)
-    picked = jnp.dot(chooser, tokens_ref[...], preferred_element_type=jnp.float32)
-    dpicked = jnp.dot(chooser, cot_ref[...], preferred_element_type=jnp.float32) * slot_weight
-    both_ref[:slots, :] = picked.astype(jnp.bfloat16)
-    both_ref[slots:, :] = dpicked.astype(jnp.bfloat16)
-    place_ref[...] = place.astype(jnp.bfloat16)
+    slot = lax.broadcasted_iota(jnp.int32, (slots, count), 0).astype(jnp.float32)
+    place = jnp.where((before - 1.0 == slot) & (routed > 0.0), 1.0, 0.0)
+    chooser = place.astype(jnp.bfloat16)
+    slot_weight = jnp.sum(place * weight, axis=1, keepdims=True)
+    chooser_ref[...] = chooser
     slot_weight_ref[...] = jnp.broadcast_to(slot_weight, slot_weight_ref.shape)
-
-
-def route(ids, share, tokens, cot):
+    reads[0].wait()
+    picked = jnp.dot(chooser, held_tokens[...], preferred_element_type=jnp.float32)
+    both[:slots, :] = picked.astype(jnp.bfloat16)
+    reads[1].wait()
+    dpicked = jnp.dot(chooser, held_cot[...], preferred_element_type=jnp.float32) * slot_weight
+    both[slots:, :] = dpicked.astype(jnp.bfloat16)
+    writes = [
+        pltpu.make_async_copy(both, copies_ref.at[k], out_sem.at[k])
+        for k in range(copies_ref.shape[0])
+    ]
+    for write in writes:
+        write.start()
+    for write in writes:
+        write.wait()
+
+
+def route(ids, share, tokens, cot, peers):
     count, width = tokens.shape
     slots = count // 8
     return pl.pallas_call(
         route_kernel,
         out_shape=(
-            jax.ShapeDtypeStruct((2 * slots, width), jnp.bfloat16),
-            jax.ShapeDtypeStruct((count, count), jnp.bfloat16),
+            jax.ShapeDtypeStruct((peers, 2 * slots, width), jnp.bfloat16),
+            jax.ShapeDtypeStruct((slots, count), jnp.bfloat16),
             jax.ShapeDtypeStruct((slots, 128), jnp.float32),
         ),
-        in_specs=whole(4),
-        out_specs=tuple(whole(3)),
-        compiler_params=PARAMS,
+        in_specs=[*whole(2), HBM, HBM],
+        out_specs=(HBM, *whole(2)),
+        scratch_shapes=[
+            pltpu.VMEM((count, width), jnp.bfloat16),
+            pltpu.VMEM((count, width), jnp.bfloat16),
+            pltpu.VMEM((2 * slots, width), jnp.bfloat16),
+            pltpu.SemaphoreType.DMA((2,)),
+            pltpu.SemaphoreType.DMA((peers,)),
+        ],
+        compiler_params=params(56),
         name="route",
-    )(ids, share, tokens, cot)
-
-
-def half_kernel(gate_ref, up_ref, mine_ref, other_ref):
+    )(ids.T, share.T, tokens, cot)
+
+
+def half_kernel(gate_ref, up_ref, down_ref, mine_ref, other_ref):
     gate, up = gate_ref[...].astype(jnp.float32), up_ref[...].astype(jnp.float32)
+    rows = gate.shape[0]
     low = lanes(gate.shape) < gate.shape[1] // 2
     first = jnp.where(low, gate, halves_swapped(up)).astype(jnp.bfloat16)
     second = jnp.where(low, halves_swapped(gate), up).astype(jnp.bfloat16)
     top = lax.axis_index("y") == 0
-    mine_ref[...] = jnp.where(top, first, second)
-    other_ref[...] = jnp.where(top, second, first)
-
-
-def split_columns(gate, up):
+    mine_ref[:rows, :] = jnp.where(top, first, second)
+    mine_ref[rows:, :] = down_ref[...]
+    other_ref[:rows, :] = jnp.where(top, second, first)
+    other_ref[rows:, :] = down_ref[...]
+
+
+def split_columns(gate, up, down):
+    rows, width = gate.shape
     return pl.pallas_call(
         half_kernel,
-        out_shape=(jax.ShapeDtypeStruct(gate.shape, gate.dtype),) * 2,
-        in_specs=whole(2),
+        out_shape=(jax.ShapeDtypeStruct((2 * rows, width), gate.dtype),) * 2,
+        in_specs=whole(3),
         out_specs=tuple(whole(2)),
+        compiler_params=params(56),
         name="split_columns",
-    )(gate, up)
-
-
-def pack_kernel(mine_ref, got_ref, down_ref, packed_ref):
-    rows = mine_ref.shape[0]
+    )(gate, up, down)
+
+
+def pack_kernel(mine_ref, got_ref, packed_ref):
+    rows = mine_ref.shape[0] // 2
     top = lax.axis_index("y") == 0
-    mine, got = mine_ref[...], got_ref[:rows, :]
+    mine, got = mine_ref[:rows, :], got_ref[:rows, :]
     packed_ref[:rows, :] = jnp.where(top, mine, got)
     packed_ref[rows : 2 * rows, :] = jnp.where(top, got, mine)
-    down, their_down = down_ref[...].astype(jnp.float32), got_ref[rows:, :].astype(jnp.float32)
+    down, their_down = (ref[rows:, :].astype(jnp.float32) for ref in (mine_ref, got_ref))
     low = lanes(down.shape) < down.shape[1] // 2
     if_top = jnp.where(low, down, halves_swapped(their_down))
     if_not = jnp.where(low, halves_swapped(their_down), down)
     packed_ref[2 * rows :, :] = jnp.where(top, if_top, if_not).astype(jnp.bfloat16)
 
 
-def pack_shards(mine, got, down):
+def pack_shards(mine, got):
     rows, width = mine.shape
     return pl.pallas_call(
         pack_kernel,
-        out_shape=jax.ShapeDtypeStruct((3 * rows, width), mine.dtype),
-        in_specs=whole(3),
+        out_shape=jax.ShapeDtypeStruct((3 * rows // 2, width), mine.dtype),
+        in_specs=whole(2),
         out_specs=whole(1)[0],
+        compiler_params=params(56),
         name="pack_shards",
-    )(mine, got, down)
+    )(mine, got)
 
 
 def expert_kernel(
-    join_ref, both_ref, packed_ref, partial_ref, send_ref, keep_ref, gate_up, down, terms
+    join_ref, both_ref, packed_ref, partial_0, partial_1, partial_2, partial_3, send_ref, keep_ref,
+    gate_up, down, terms, partials,
 ):
     chips = packed_ref.shape[1]
     rows = packed_ref.shape[2] // 3
@@ -150,7 +187,13 @@
         LANE_DIMS,
         preferred_element_type=jnp.float32,
     )
-    partial_ref[...] = partial.astype(jnp.bfloat16).reshape(partial_ref.shape)
+    partials[...] = partial.reshape(partials.shape)
+    x, ring = lax.axis_index("x"), lax.axis_index("h") * 2 + lax.axis_index("y")
+    for step, ref in enumerate((partial_0, partial_1, partial_2, partial_3)):
+        for turn in range(4):
+            place = lax.rem(ring + turn, 4)
+            peer = (lax.rem(place, 2) * 2 + place // 2) * 4 + lax.rem(x + step, 4)
+            ref[turn] = partials[peer].astype(ref.dtype)
     dhidden = jnp.dot(dpicked, down[...], preferred_element_type=jnp.float32)
     dgate = dhidden * up * sigma * (1.0 + gate * (1.0 - sigma))
     dup = dhidden * gate * sigma
@@ -183,45 +226,66 @@
     slots = doubled // 2
     _, chips, rows, width = packed.shape
     chunk = (chips, 2, rows // 2, width)
+    quarter = jax.ShapeDtypeStruct((peers // 4, slots, depth), jnp.bfloat16)
     return pl.pallas_call(
         expert_kernel,
         out_shape=(
-            jax.ShapeDtypeStruct((peers, slots, depth), jnp.bfloat16),
+            quarter, quarter, quarter, quarter,
             jax.ShapeDtypeStruct(chunk, jnp.bfloat16),
             jax.ShapeDtypeStruct(chunk, jnp.float32),
         ),
         in_specs=[pl.BlockSpec(memory_space=pltpu.SMEM), *whole(2)],
-        out_specs=tuple(whole(3)),
+        out_specs=tuple(whole(6)),
         scratch_shapes=[
             pltpu.VMEM((depth, width), jnp.bfloat16),
             pltpu.VMEM((depth, width), jnp.bfloat16),
             pltpu.VMEM((2, depth, width), jnp.float32),
+            pltpu.VMEM((peers, slots, depth), jnp.float32),
         ],
-        compiler_params=PARAMS,
+        compiler_params=params(24),
         name="expert",
     )(join, both, packed)
 
 
-def mix_kernel(blocks_ref, place_ref, slot_weight_ref, mixed_ref):
-    slots = blocks_ref.shape[1]
-    total = blocks_ref[0].astype(jnp.float32)
-    for k in range(1, blocks_ref.shape[0]):
-        total += blocks_ref[k].astype(jnp.float32)
+def add_kernel(own_ref, *refs):
+    total = own_ref[...].astype(jnp.float32)
+    for ref in refs[:3]:
+        total += ref[...].astype(jnp.float32)
+    for k, ref in enumerate(refs[3:]):
+        ref[...] = total[k].astype(ref.dtype)
+
+
+def add_quarters(parts):
+    turns, slots, depth = parts[0].shape
+    return pl.pallas_call(
+        add_kernel,
+        out_shape=(jax.ShapeDtypeStruct((slots, depth), jnp.bfloat16),) * turns,
+        in_specs=whole(4),
+        out_specs=tuple(whole(turns)),
+        compiler_params=params(8),
+        name="add_quarters",
+    )(*parts)
+
+
+def mix_kernel(own_ref, first_ref, second_ref, third_ref, chooser_ref, slot_weight_ref, mixed_ref):
+    total = own_ref[...].astype(jnp.float32)
+    for ref in (first_ref, second_ref, third_ref):
+        total += ref[...].astype(jnp.float32)
     weighted = (total * slot_weight_ref[:, :1]).astype(jnp.bfloat16)
-    mixed_ref[...] = jnp.dot(
-        place_ref[:, :slots], weighted, preferred_element_type=jnp.float32
+    mixed_ref[...] = lax.dot_general(
+        chooser_ref[...], weighted, ROW_DIMS, preferred_element_type=jnp.float32
     ).astype(jnp.bfloat16)
 
 
-def mix(blocks, place, slot_weight):
+def mix(parts, chooser, slot_weight):
     return pl.pallas_call(
         mix_kernel,
-        out_shape=jax.ShapeDtypeStruct((place.shape[0], blocks.shape[2]), jnp.bfloat16),
-        in_specs=whole(3),
+        out_shape=jax.ShapeDtypeStruct((chooser.shape[1], parts[0].shape[1]), jnp.bfloat16),
+        in_specs=whole(6),
         out_specs=whole(1)[0],
-        compiler_params=PARAMS,
+        compiler_params=params(8),
         name="mix",
-    )(blocks, place, slot_weight)
+    )(*parts, chooser, slot_weight)
 
 
 def finish_kernel(blocks_ref, gate_ref, up_ref, down_ref):
@@ -248,28 +312,39 @@
         out_shape=(shape,) * 3,
         in_specs=whole(1),
         out_specs=tuple(whole(3)),
+        compiler_params=params(4),
         name="finish",
     )(blocks)
+
+
+def spread(parts, axes, ring):
+    came = [
+        lax.ppermute(part, axes, [(ring[i], ring[(i + k) % 4]) for i in range(4)])
+        for k, part in enumerate(parts)
+        if k
+    ]
+    return [parts[0], *came]
 
 
 def per_device(tokens, cotangent, expert_ids, route_weights, join_groups, w_gate, w_up, w_down):
     plane = lax.axis_size(PLANE)
     chips = lax.axis_size("z")
-    mine, other = split_columns(w_gate, w_up)
-    got = lax.ppermute(jnp.concatenate([other, w_down]), "y", SWAP)
-    both, place, slot_weight = route(expert_ids, route_weights, tokens, cotangent)
-    packed = pack_shards(mine, got, w_down)
-    copies = jnp.broadcast_to(both, (plane, *both.shape))
+    mine, other = split_columns(w_gate, w_up, w_down)
+    got = lax.ppermute(other, "y", SWAP)
+    copies, chooser, slot_weight = route(expert_ids, route_weights, tokens, cotangent, plane)
+    packed = pack_shards(mine, got)
+    packed, copies = lax.optimization_barrier((packed, copies))
     rows_in = lax.all_to_all(copies, PLANE, 0, 0, tiled=True)
     along = lax.all_gather(packed, "z", axis=0, tiled=False)
     gathered = lax.all_gather(along, "c", axis=0, tiled=False)
-    partial, send, keep = expert(join_groups, rows_in, gathered)
-    blocks = lax.all_to_all(partial, PLANE, 0, 0, tiled=True)
+    *partials, send, keep = expert(join_groups, rows_in, gathered)
     from_core = lax.ppermute(send, "c", SWAP)
     chip_sum = (keep + from_core.astype(jnp.float32)).astype(jnp.bfloat16)
     chip_sum = chip_sum.reshape(chips * 2, *chip_sum.shape[2:])
+    chip_sum, partials = lax.optimization_barrier((chip_sum, partials))
     pieces = lax.all_to_all(chip_sum, ("z", "y"), 0, 0, tiled=True)
-    mixed = mix(blocks, place, slot_weight)
+    quarters = add_quarters(spread(partials, "x", (0, 1, 2, 3)))
+    mixed = mix(spread(quarters, RING, (0, 2, 1, 3)), chooser, slot_weight)
     return (mixed, *finish(pieces))
 
 

time: 146 us -> 112 us (0.77)
  the two profiles are of different devices: /device:TPU:8 before, /device:TPU:6 now
where the time goes in v2:
time: 112 us; the launch traced here: 110 us
  starting transfers between devices  41.2 us (37%)
  blocking collectives  39.2 us (35%)
  waiting for transfers between devices  15.5 us (14%)
  Pallas kernels  12 us (11%)
    all_gather x1, blocking collectives, per_device(): along = lax.all_gather(packed, 'z', axis=0, tiled=False)  36.8 us
    ppermute x6, starting transfers between devices, spread(): lax.ppermute(part, axes, [(ring[i], ring[(i + k) % 4]) for i in range(4)])  19.5 us
    ppermute x6, waiting for transfers between devices, spread(): lax.ppermute(part, axes, [(ring[i], ring[(i + k) % 4]) for i in range(4)])  13.9 us
    all_to_all x1, starting transfers between devices, per_device(): pieces = lax.all_to_all(chip_sum, ('z', 'y'), 0, 0, tiled=True)  8.15 us
    all_to_all x1, starting transfers between devices, per_device(): rows_in = lax.all_to_all(copies, PLANE, 0, 0, tiled=True)  7.94 us
    pallas_call x1, Pallas kernels, route(): pl.pallas_call(route_kernel, out_shape=(jax.ShapeDtypeStruct((peers, 2 *...  4.21 us
    ppermute x1, starting transfers between devices, per_device(): got = lax.ppermute(other, 'y', SWAP)  3.47 us
    pallas_call x1, Pallas kernels, expert(): pl.pallas_call(expert_kernel, out_shape=(quarter, quarter, quarter, quart...  2.96 us
  transfers between devices with their start and end apart: 10, of which 5 were waited for; matrix products, arithmetic and copies ran while one was open for 0% of the time, Pallas kernels for 5%

profile of v2, /device:TPU:6, one launch (start us, length us, event | category | flops | bytes accessed | tf_op | source)
XLA Modules:
  0.0 110.1 jit_solution(15923901895989694189)
XLA Ops:
  0.6 1.4 %split_columns.1 = (bf16[64,128]{1,0:T(8,128)(2,1)}, bf16[64,128]{1,0:T(8,128)(2,1)}) custom-call(bf16[32,128]{1,0:T(8,128)(2,1)} %gate_ref.1, bf16[32,128]{1,0:T(8,128)(2,1)} %up_ref.1, bf16[32,128]{1,0:T(8,128)(2,1)} %down_ref.1), custom_call_target="tpu_custom_call" | custom-call | tf_op jit(solution)/shard_map/split_columns/pallas_call | solution.py:118
  2.1 3.5 %collective-permute-start = (bf16[64,128]{1,0:T(8,128)(2,1)}, bf16[64,128]{1,0:T(8,128)(2,1)S(1)}, u32[]{:S(2)}, u32[]{:S(2)}) collective-permute-start(bf16[64,128]{1,0:T(8,128)(2,1)} %get-tuple-element.30), channel_id=1, source_target_pairs={{0,16},{16,0},{1,17},{17,1},{2,18},{18,2},{3,19},{19,3},{4,20},{20... | collective-permute-start | bytes 49160 | tf_op jit(solution)/shard_map/ppermute | solution.py:333
  5.5 4.2 %route.1 = (bf16[16,32,2048]{2,1,0:T(8,128)(2,1)}, bf16[16,128]{1,0:T(8,128)(2,1)}, f32[16,128]{1,0:T(8,128)}) custom-call(s32[8,128]{1,0:T(8,128)} %bitcast.7, f32[8,128]{1,0:T(8,128)} %bitcast.8, bf16[128,2048]{1,0:T(8,128)(2,1)} %tokens_ref.1, bf16[128,2048]{1,0:T(8,128)(2,1)} %cot_ref.1), custom_call_target="tpu_custom_call" | custom-call | tf_op jit(solution)/shard_map/route/pallas_call | solution.py:82
  9.7 0.0 collective-permute-done.got_ref
  9.8 0.0 copy-start.6
  9.8 0.6 copy-done.6
  10.4 1.4 %pack_shards.1 = bf16[96,128]{1,0:T(8,128)(2,1)} custom-call(bf16[64,128]{1,0:T(8,128)(2,1)} %get-tuple-element.29.mine_ref, bf16[64,128]{1,0:T(8,128)(2,1)} %copy-done.6), custom_call_target="tpu_custom_call" | custom-call | tf_op jit(solution)/shard_map/pack_shards/pallas_call | solution.py:143
  11.8 0.0 copy-start.5
  11.8 0.0 copy-start.2
  11.8 7.9 %all-to-all-start = ((bf16[16,32,2048]{2,1,0:T(8,128)(2,1)}), bf16[16,32,2048]{2,1,0:T(8,128)(2,1)S(1)}, u32[]{:S(2)}, u32[]{:S(2)}) async-start(bf16[16,32,2048]{2,1,0:T(8,128)(2,1)} %get-tuple-element.32), calls=%async_computation | async-start | bytes 4194304 | tf_op jit(solution)/shard_map/all_to_all | solution.py:337
  19.7 0.0 copy-done.5
  19.7 36.8 %all-gather = bf16[1536,128]{1,0:T(8,128)(2,1)S(1)} all-gather(bf16[96,128]{1,0:T(8,128)(2,1)S(1)} %copy-done.5), channel_id=2, replica_groups=mesh['z'=16,'y'=2,'c'=2,'h'=2,'x'=4] {'z'}, dimensions={0}, use_global_device_ids=true | all-gather | bytes 417792 | tf_op jit(solution)/shard_map/all_gather | solution.py:338
  56.5 2.4 %all-gather.1 = bf16[32,96,128]{2,1,0:T(8,128)(2,1)S(1)} all-gather(bf16[16,96,128]{2,1,0:T(8,128)(2,1)S(1)} %bitcast.6), channel_id=3, replica_groups=mesh['z'=16,'y'=2,'c'=2,'h'=2,'x'=4] {'c'}, dimensions={0}, use_global_device_ids=true | all-gather | bytes 1179648 | tf_op jit(solution)/shard_map/all_gather | solution.py:339
  58.9 0.0 all-to-all-done.both_ref
  58.9 0.0 copy-done.2
  58.9 3.0 %expert.1 = (bf16[4,16,2048]{2,1,0:T(8,128)(2,1)S(1)}, bf16[4,16,2048]{2,1,0:T(8,128)(2,1)S(1)}, bf16[4,16,2048]{2,1,0:T(8,128)(2,1)S(1)}, bf16[4,16,2048]{2,1,0...) custom-call(s32[64]{0:T(128)S(1)} %copy-done.2, ...), custom_call_target="tpu_custom_call" | custom-call | tf_op jit(solution)/shard_map/expert/pallas_call | solution.py:230
  61.9 0.0 copy-start.3
  61.9 0.0 copy-start.4
  61.9 0.0 copy-start
  61.9 0.0 copy-start.1
  61.9 2.2 %collective-permute-start.1 = (bf16[16,2,48,128]{3,2,1,0:T(8,128)(2,1)S(1)}, bf16[16,2,48,128]{3,2,1,0:T(8,128)(2,1)S(1)}, u32[]{:S(2)}, u32[]{:S(2)}) collective-permute-start(bf16[16,2,48,128]{3,2,1,0:T(8,128)(2,1)S(1)} %get-tuple-element.35), channel_id=1, source_target_pairs={{0,8},{8,0},{1,9},{9,1},{2,10},{10,2},{3,11},{11,3},{4,12},{12,4},... | collective-permute-start | bytes 1179656 | tf_op jit(solution)/shard_map/ppermute | solution.py:341
  64.1 1.5 %collective-permute-done.1 = bf16[16,2,48,128]{3,2,1,0:T(8,128)(2,1)S(1)} collective-permute-done((bf16[16,2,48,128]{3,2,1,0:T(8,128)(2,1)S(1)}, bf16[16,2,48,128]{3,2,1,0:T(8,128)(2,1)S(1)}, u32[]{:S(2)}, u32[]{:S(2)}) %collective-permute-start.1) | collective-permute-done | bytes 393248 | tf_op jit(solution)/shard_map/ppermute | solution.py:341
  65.6 0.8 add_convert_fusion
  66.5 0.0 copy-done.3
  66.5 0.0 copy-done.4
  66.5 8.2 %all-to-all-start.1 = ((bf16[32,48,128]{2,1,0:T(8,128)(2,1)}), bf16[32,48,128]{2,1,0:T(8,128)(2,1)S(1)}, u32[]{:S(2)}, u32[]{:S(2)}) async-start(bf16[32,48,128]{2,1,0:T(8,128)(2,1)} %bitcast.4), calls=%async_computation.1 | async-start | bytes 786432 | tf_op jit(solution)/shard_map/all_to_all | solution.py:345
  74.7 2.2 %collective-permute-start.2 = (bf16[4,16,2048]{2,1,0:T(8,128)(2,1)}, bf16[4,16,2048]{2,1,0:T(8,128)(2,1)S(1)}, u32[]{:S(2)}, u32[]{:S(2)}) collective-permute-start(bf16[4,16,2048]{2,1,0:T(8,128)(2,1)} %copy-done.4), channel_id=1, source_target_pairs={{0,1},{1,2},{2,3},{3,0},{4,5},{5,6},{6,7},{7,4},{8,9},{9,10},{10,1... | collective-permute-start | bytes 786440 | tf_op jit(solution)/shard_map/ppermute | solution.py:322
  76.9 4.3 %collective-permute-start.3 = (bf16[4,16,2048]{2,1,0:T(8,128)(2,1)}, bf16[4,16,2048]{2,1,0:T(8,128)(2,1)S(1)}, u32[]{:S(2)}, u32[]{:S(2)}) collective-permute-start(bf16[4,16,2048]{2,1,0:T(8,128)(2,1)} %copy-done.3), channel_id=1, source_target_pairs={{0,2},{1,3},{2,0},{3,1},{4,6},{5,7},{6,4},{7,5},{8,10},{9,11},{10,... | collective-permute-start | bytes 786440 | tf_op jit(solution)/shard_map/ppermute | solution.py:322
  81.2 1.9 %collective-permute-start.4 = (bf16[4,16,2048]{2,1,0:T(8,128)(2,1)S(1)}, bf16[4,16,2048]{2,1,0:T(8,128)(2,1)S(1)}, u32[]{:S(2)}, u32[]{:S(2)}) collective-permute-start(bf16[4,16,2048]{2,1,0:T(8,128)(2,1)S(1)} %get-tuple-element.43), channel_id=1, source_target_pairs={{0,3},{1,0},{2,1},{3,2},{4,7},{5,4},{6,5},{7,6},{8,11},{9,8},{10,9... | collective-permute-start | bytes 786440 | tf_op jit(solution)/shard_map/ppermute | solution.py:322
  83.1 2.8 %collective-permute-done.2.refs_0_ = bf16[4,16,2048]{2,1,0:T(8,128)(2,1)S(1)} collective-permute-done((bf16[4,16,2048]{2,1,0:T(8,128)(2,1)}, bf16[4,16,2048]{2,1,0:T(8,128)(2,1)S(1)}, u32[]{:S(2)}, u32[]{:S(2)}) %collective-permute-start.2) | collective-permute-done | bytes 262176 | tf_op jit(solution)/shard_map/ppermute | solution.py:322
  85.9 3.8 %collective-permute-done.3.refs_1_ = bf16[4,16,2048]{2,1,0:T(8,128)(2,1)S(1)} collective-permute-done((bf16[4,16,2048]{2,1,0:T(8,128)(2,1)}, bf16[4,16,2048]{2,1,0:T(8,128)(2,1)S(1)}, u32[]{:S(2)}, u32[]{:S(2)}) %collective-permute-start.3) | collective-permute-done | bytes 262176 | tf_op jit(solution)/shard_map/ppermute | solution.py:322
  89.7 4.2 %collective-permute-done.4.refs_2_ = bf16[4,16,2048]{2,1,0:T(8,128)(2,1)S(1)} collective-permute-done((bf16[4,16,2048]{2,1,0:T(8,128)(2,1)S(1)}, bf16[4,16,2048]{2,1,0:T(8,128)(2,1)S(1)}, u32[]{:S(2)}, u32[]{:S(2)}) %collective-permute-start.4) | collective-permute-done | bytes 262176 | tf_op jit(solution)/shard_map/ppermute | solution.py:322
  93.9 0.1 add_quarters.1
  94.1 3.4 %collective-permute-start.5 = (bf16[16,2048]{1,0:T(8,128)(2,1)S(1)}, bf16[16,2048]{1,0:T(8,128)(2,1)S(1)}, u32[]{:S(2)}, u32[]{:S(2)}) collective-permute-start(bf16[16,2048]{1,0:T(8,128)(2,1)S(1)} %get-tuple-element.45), channel_id=1, source_target_pairs={{0,16},{16,4},{4,20},{20,0},{1,17},{17,5},{5,21},{21,1},{2,18},{18... | collective-permute-start | bytes 196616 | tf_op jit(solution)/shard_map/ppermute | solution.py:322
  97.5 4.6 %collective-permute-start.6 = (bf16[16,2048]{1,0:T(8,128)(2,1)S(1)}, bf16[16,2048]{1,0:T(8,128)(2,1)S(1)}, u32[]{:S(2)}, u32[]{:S(2)}) collective-permute-start(bf16[16,2048]{1,0:T(8,128)(2,1)S(1)} %get-tuple-element.46), channel_id=1, source_target_pairs={{0,4},{16,20},{4,0},{20,16},{1,5},{17,21},{5,1},{21,17},{2,6},{18,... | collective-permute-start | bytes 196616 | tf_op jit(solution)/shard_map/ppermute | solution.py:322
  102.1 3.0 %collective-permute-start.7 = (bf16[16,2048]{1,0:T(8,128)(2,1)S(1)}, bf16[16,2048]{1,0:T(8,128)(2,1)S(1)}, u32[]{:S(2)}, u32[]{:S(2)}) collective-permute-start(bf16[16,2048]{1,0:T(8,128)(2,1)S(1)} %get-tuple-element.47), channel_id=1, source_target_pairs={{0,20},{16,0},{4,16},{20,4},{1,21},{17,1},{5,17},{21,5},{2,22},{18... | collective-permute-start | bytes 196616 | tf_op jit(solution)/shard_map/ppermute | solution.py:322
  105.1 0.0 collective-permute-done.5.first_ref
  105.1 0.0 collective-permute-done.6.second_ref
  105.2 3.1 %collective-permute-done.7.third_ref = bf16[16,2048]{1,0:T(8,128)(2,1)S(1)} collective-permute-done((bf16[16,2048]{1,0:T(8,128)(2,1)S(1)}, bf16[16,2048]{1,0:T(8,128)(2,1)S(1)}, u32[]{:S(2)}, u32[]{:S(2)}) %collective-permute-start.7) | collective-permute-done | bytes 65568 | tf_op jit(solution)/shard_map/ppermute | solution.py:322
  108.3 0.0 copy-done
  108.3 0.0 copy-done.1
  108.3 1.1 %mix.1 = bf16[128,2048]{1,0:T(8,128)(2,1)} custom-call(bf16[16,2048]{1,0:T(8,128)(2,1)S(1)} %get-tuple-element.44.own_ref, bf16[16,2048]{1,0:T(8,128)(2,1)S(1)} %collective-permute-done.5.first_ref, bf16[16,2048]{1,0:T(8,128)(2,1)S(1)} %collective-permute-done.6.second_ref, bf16[16,2048]{1,0:T(8,128)(2,1)S(1)} %collective-permute-done.7.third_ref, ...), custom_call_target="tpu_custom_call" | custom-call | tf_op jit(solution)/shard_map/mix/pallas_call | solution.py:281
  109.4 0.0 all-to-all-done.1.blocks_ref
  109.4 0.7 finish.1
Async XLA Ops:
  2.1 7.7 %collective-permute-start = (bf16[64,128]{1,0:T(8,128)(2,1)}, bf16[64,128]{1,0:T(8,128)(2,1)S(1)}, u32[]{:S(2)}, u32[]{:S(2)}) collective-permute-start(bf16[64,128]{1,0:T(8,128)(2,1)} %get-tuple-element.30), channel_id=1, source_target_pairs={{0,16},{16,0},{1,17},{17,1},{2,18},{18,2},{3,19},{19,3},{4,20},{20... | collective-permute-start | bytes 49160 | tf_op jit(solution)/shard_map/ppermute | solution.py:333
  9.8 0.6 copy-start.6
  11.8 7.9 %copy-start.5 = (bf16[96,128]{1,0:T(8,128)(2,1)S(1)}, bf16[96,128]{1,0:T(8,128)(2,1)}, u32[]{:S(2)}) copy-start(bf16[96,128]{1,0:T(8,128)(2,1)} %pack_shards.1) | copy-start | bytes 73732
  11.8 47.1 %copy-start.2 = (s32[64]{0:T(128)S(1)}, s32[64]{0:T(128)}, u32[]{:S(2)}) copy-start(s32[64]{0:T(128)} %join_ref.1) | copy-start | bytes 772
  11.8 47.1 %all-to-all-start = ((bf16[16,32,2048]{2,1,0:T(8,128)(2,1)}), bf16[16,32,2048]{2,1,0:T(8,128)(2,1)S(1)}, u32[]{:S(2)}, u32[]{:S(2)}) async-start(bf16[16,32,2048]{2,1,0:T(8,128)(2,1)} %get-tuple-element.32), calls=%async_computation | async-start | bytes 4194304 | tf_op jit(solution)/shard_map/all_to_all | solution.py:337
  61.9 4.6 %copy-start.3 = (bf16[4,16,2048]{2,1,0:T(8,128)(2,1)}, bf16[4,16,2048]{2,1,0:T(8,128)(2,1)S(1)}, u32[]{:S(2)}) copy-start(bf16[4,16,2048]{2,1,0:T(8,128)(2,1)S(1)} %get-tuple-element.42) | copy-start | bytes 786436
  61.9 4.6 %copy-start.4 = (bf16[4,16,2048]{2,1,0:T(8,128)(2,1)}, bf16[4,16,2048]{2,1,0:T(8,128)(2,1)S(1)}, u32[]{:S(2)}) copy-start(bf16[4,16,2048]{2,1,0:T(8,128)(2,1)S(1)} %get-tuple-element.41) | copy-start | bytes 786436
  61.9 46.4 %copy-start = (f32[16,128]{1,0:T(8,128)S(1)}, f32[16,128]{1,0:T(8,128)}, u32[]{:S(2)}) copy-start(f32[16,128]{1,0:T(8,128)} %get-tuple-element.49.slot_weight_ref) | copy-start | bytes 24580
  61.9 46.4 %copy-start.1 = (bf16[16,128]{1,0:T(8,128)(2,1)S(1)}, bf16[16,128]{1,0:T(8,128)(2,1)}, u32[]{:S(2)}) copy-start(bf16[16,128]{1,0:T(8,128)(2,1)} %get-tuple-element.48.chooser_ref) | copy-start | bytes 12292
  61.9 3.7 %collective-permute-start.1 = (bf16[16,2,48,128]{3,2,1,0:T(8,128)(2,1)S(1)}, bf16[16,2,48,128]{3,2,1,0:T(8,128)(2,1)S(1)}, u32[]{:S(2)}, u32[]{:S(2)}) collective-permute-start(bf16[16,2,48,128]{3,2,1,0:T(8,128)(2,1)S(1)} %get-tuple-element.35), channel_id=1, source_target_pairs={{0,8},{8,0},{1,9},{9,1},{2,10},{10,2},{3,11},{11,3},{4,12},{12,4},... | collective-permute-start | bytes 1179656 | tf_op jit(solution)/shard_map/ppermute | solution.py:341
  66.5 42.9 %all-to-all-start.1 = ((bf16[32,48,128]{2,1,0:T(8,128)(2,1)}), bf16[32,48,128]{2,1,0:T(8,128)(2,1)S(1)}, u32[]{:S(2)}, u32[]{:S(2)}) async-start(bf16[32,48,128]{2,1,0:T(8,128)(2,1)} %bitcast.4), calls=%async_computation.1 | async-start | bytes 786432 | tf_op jit(solution)/shard_map/all_to_all | solution.py:345
  74.7 11.3 %collective-permute-start.2 = (bf16[4,16,2048]{2,1,0:T(8,128)(2,1)}, bf16[4,16,2048]{2,1,0:T(8,128)(2,1)S(1)}, u32[]{:S(2)}, u32[]{:S(2)}) collective-permute-start(bf16[4,16,2048]{2,1,0:T(8,128)(2,1)} %copy-done.4), channel_id=1, source_target_pairs={{0,1},{1,2},{2,3},{3,0},{4,5},{5,6},{6,7},{7,4},{8,9},{9,10},{10,1... | collective-permute-start | bytes 786440 | tf_op jit(solution)/shard_map/ppermute | solution.py:322
  76.9 12.8 %collective-permute-start.3 = (bf16[4,16,2048]{2,1,0:T(8,128)(2,1)}, bf16[4,16,2048]{2,1,0:T(8,128)(2,1)S(1)}, u32[]{:S(2)}, u32[]{:S(2)}) collective-permute-start(bf16[4,16,2048]{2,1,0:T(8,128)(2,1)} %copy-done.3), channel_id=1, source_target_pairs={{0,2},{1,3},{2,0},{3,1},{4,6},{5,7},{6,4},{7,5},{8,10},{9,11},{10,... | collective-permute-start | bytes 786440 | tf_op jit(solution)/shard_map/ppermute | solution.py:322
  81.2 12.8 %collective-permute-start.4 = (bf16[4,16,2048]{2,1,0:T(8,128)(2,1)S(1)}, bf16[4,16,2048]{2,1,0:T(8,128)(2,1)S(1)}, u32[]{:S(2)}, u32[]{:S(2)}) collective-permute-start(bf16[4,16,2048]{2,1,0:T(8,128)(2,1)S(1)} %get-tuple-element.43), channel_id=1, source_target_pairs={{0,3},{1,0},{2,1},{3,2},{4,7},{5,4},{6,5},{7,6},{8,11},{9,8},{10,9... | collective-permute-start | bytes 786440 | tf_op jit(solution)/shard_map/ppermute | solution.py:322
  94.1 11.1 %collective-permute-start.5 = (bf16[16,2048]{1,0:T(8,128)(2,1)S(1)}, bf16[16,2048]{1,0:T(8,128)(2,1)S(1)}, u32[]{:S(2)}, u32[]{:S(2)}) collective-permute-start(bf16[16,2048]{1,0:T(8,128)(2,1)S(1)} %get-tuple-element.45), channel_id=1, source_target_pairs={{0,16},{16,4},{4,20},{20,0},{1,17},{17,5},{5,21},{21,1},{2,18},{18... | collective-permute-start | bytes 196616 | tf_op jit(solution)/shard_map/ppermute | solution.py:322
  97.5 7.7 %collective-permute-start.6 = (bf16[16,2048]{1,0:T(8,128)(2,1)S(1)}, bf16[16,2048]{1,0:T(8,128)(2,1)S(1)}, u32[]{:S(2)}, u32[]{:S(2)}) collective-permute-start(bf16[16,2048]{1,0:T(8,128)(2,1)S(1)} %get-tuple-element.46), channel_id=1, source_target_pairs={{0,4},{16,20},{4,0},{20,16},{1,5},{17,21},{5,1},{21,17},{2,6},{18,... | collective-permute-start | bytes 196616 | tf_op jit(solution)/shard_map/ppermute | solution.py:322
  102.1 6.2 %collective-permute-start.7 = (bf16[16,2048]{1,0:T(8,128)(2,1)S(1)}, bf16[16,2048]{1,0:T(8,128)(2,1)S(1)}, u32[]{:S(2)}, u32[]{:S(2)}) collective-permute-start(bf16[16,2048]{1,0:T(8,128)(2,1)S(1)} %get-tuple-element.47), channel_id=1, source_target_pairs={{0,20},{16,0},{4,16},{20,4},{1,21},{17,1},{5,17},{21,5},{2,22},{18... | collective-permute-start | bytes 196616 | tf_op jit(solution)/shard_map/ppermute | solution.py:322

commit v3 on v2

--- a/solution.py
+++ b/solution.py
@@ -34,44 +34,56 @@
 
 def route_kernel(
     ids_ref, share_ref, tokens_ref, cot_ref, copies_ref, chooser_ref, slot_weight_ref,
-    held_tokens, held_cot, both, in_sems, out_sem,
+    held_ids, held_share, held_tokens, held_cot, both, chooser, weights, in_sems, out_sems, own_sems,
 ):
     count = ids_ref.shape[1]
     slots = chooser_ref.shape[0]
+    peers = copies_ref.shape[0]
+    pairs = (
+        (ids_ref, held_ids), (share_ref, held_share), (tokens_ref, held_tokens), (cot_ref, held_cot)
+    )
     reads = [
-        pltpu.make_async_copy(tokens_ref, held_tokens, in_sems.at[0]),
-        pltpu.make_async_copy(cot_ref, held_cot, in_sems.at[1]),
+        pltpu.make_async_copy(src, dst, in_sems.at[k]) for k, (src, dst) in enumerate(pairs)
     ]
     for read in reads:
         read.start()
-    chosen = ids_ref[...] == 0
-    routed = jnp.max(chosen.astype(jnp.float32), axis=0, keepdims=True)
-    weight = jnp.sum(jnp.where(chosen, share_ref[...], 0.0), axis=0, keepdims=True)
     square = (count, count)
     until = lax.broadcasted_iota(jnp.int32, square, 0) <= lanes(square)
+    until = until.astype(jnp.bfloat16)
+    slot = lax.broadcasted_iota(jnp.int32, (slots, count), 0).astype(jnp.float32)
+    reads[0].wait()
+    reads[1].wait()
+    chosen = held_ids[...] == 0
+    routed = jnp.max(chosen.astype(jnp.float32), axis=0, keepdims=True)
+    weight = jnp.sum(jnp.where(chosen, held_share[...], 0.0), axis=0, keepdims=True)
     before = jnp.dot(
         jnp.broadcast_to(routed, (slots, count)).astype(jnp.bfloat16),
-        until.astype(jnp.bfloat16),
+        until,
         preferred_element_type=jnp.float32,
     )
-    slot = lax.broadcasted_iota(jnp.int32, (slots, count), 0).astype(jnp.float32)
     place = jnp.where((before - 1.0 == slot) & (routed > 0.0), 1.0, 0.0)
-    chooser = place.astype(jnp.bfloat16)
     slot_weight = jnp.sum(place * weight, axis=1, keepdims=True)
-    chooser_ref[...] = chooser
-    slot_weight_ref[...] = jnp.broadcast_to(slot_weight, slot_weight_ref.shape)
-    reads[0].wait()
-    picked = jnp.dot(chooser, held_tokens[...], preferred_element_type=jnp.float32)
-    both[:slots, :] = picked.astype(jnp.bfloat16)
-    reads[1].wait()
-    dpicked = jnp.dot(chooser, held_cot[...], preferred_element_type=jnp.float32) * slot_weight
-    both[slots:, :] = dpicked.astype(jnp.bfloat16)
+    chooser[...] = place.astype(jnp.bfloat16)
+    weights[...] = jnp.broadcast_to(slot_weight, weights.shape)
     writes = [
-        pltpu.make_async_copy(both, copies_ref.at[k], out_sem.at[k])
-        for k in range(copies_ref.shape[0])
+        pltpu.make_async_copy(chooser, chooser_ref, own_sems.at[0]),
+        pltpu.make_async_copy(weights, slot_weight_ref, own_sems.at[1]),
     ]
     for write in writes:
         write.start()
+    for part, held in enumerate((held_tokens, held_cot)):
+        reads[2 + part].wait()
+        rows = jnp.dot(chooser[...], held[...], preferred_element_type=jnp.float32)
+        both[part] = (rows * slot_weight if part else rows).astype(jnp.bfloat16)
+        for k in range(peers):
+            writes.append(
+                pltpu.make_async_copy(
+                    both.at[part],
+                    copies_ref.at[k, pl.ds(part * slots, slots), :],
+                    out_sems.at[part, k],
+                )
+            )
+            writes[-1].start()
     for write in writes:
         write.wait()
 
@@ -79,6 +91,7 @@
 def route(ids, share, tokens, cot, peers):
     count, width = tokens.shape
     slots = count // 8
+    top = ids.shape[1]
     return pl.pallas_call(
         route_kernel,
         out_shape=(
@@ -86,68 +99,55 @@
             jax.ShapeDtypeStruct((slots, count), jnp.bfloat16),
             jax.ShapeDtypeStruct((slots, 128), jnp.float32),
         ),
-        in_specs=[*whole(2), HBM, HBM],
-        out_specs=(HBM, *whole(2)),
+        in_specs=[HBM] * 4,
+        out_specs=(HBM,) * 3,
         scratch_shapes=[
+            pltpu.VMEM((top, count), jnp.int32),
+            pltpu.VMEM((top, count), jnp.float32),
             pltpu.VMEM((count, width), jnp.bfloat16),
             pltpu.VMEM((count, width), jnp.bfloat16),
-            pltpu.VMEM((2 * slots, width), jnp.bfloat16),
+            pltpu.VMEM((2, slots, width), jnp.bfloat16),
+            pltpu.VMEM((slots, count), jnp.bfloat16),
+            pltpu.VMEM((slots, 128), jnp.float32),
+            pltpu.SemaphoreType.DMA((4,)),
+            pltpu.SemaphoreType.DMA((2, peers)),
             pltpu.SemaphoreType.DMA((2,)),
-            pltpu.SemaphoreType.DMA((peers,)),
         ],
         compiler_params=params(56),
         name="route",
     )(ids.T, share.T, tokens, cot)
 
 
-def half_kernel(gate_ref, up_ref, down_ref, mine_ref, other_ref):
-    gate, up = gate_ref[...].astype(jnp.float32), up_ref[...].astype(jnp.float32)
-    rows = gate.shape[0]
-    low = lanes(gate.shape) < gate.shape[1] // 2
-    first = jnp.where(low, gate, halves_swapped(up)).astype(jnp.bfloat16)
-    second = jnp.where(low, halves_swapped(gate), up).astype(jnp.bfloat16)
+def pack_kernel(own_ref, got_ref, packed_ref):
+    rows, width = own_ref.shape[1:]
+    low = lanes((rows, width)) < width // 2
     top = lax.axis_index("y") == 0
-    mine_ref[:rows, :] = jnp.where(top, first, second)
-    mine_ref[rows:, :] = down_ref[...]
-    other_ref[:rows, :] = jnp.where(top, second, first)
-    other_ref[rows:, :] = down_ref[...]
-
-
-def split_columns(gate, up, down):
-    rows, width = gate.shape
-    return pl.pallas_call(
-        half_kernel,
-        out_shape=(jax.ShapeDtypeStruct((2 * rows, width), gate.dtype),) * 2,
-        in_specs=whole(3),
-        out_specs=tuple(whole(2)),
-        compiler_params=params(56),
-        name="split_columns",
-    )(gate, up, down)
-
-
-def pack_kernel(mine_ref, got_ref, packed_ref):
-    rows = mine_ref.shape[0] // 2
-    top = lax.axis_index("y") == 0
-    mine, got = mine_ref[:rows, :], got_ref[:rows, :]
+
+    def half_of(left, right):
+        left, right = left.astype(jnp.float32), right.astype(jnp.float32)
+        if_top = jnp.where(low, left, halves_swapped(right))
+        return jnp.where(top, if_top, jnp.where(low, halves_swapped(left), right)).astype(jnp.bfloat16)
+
+    mine = half_of(own_ref[0], own_ref[1])
+    got = half_of(got_ref[0], got_ref[1])
+    down, their_down = own_ref[2], got_ref[2]
     packed_ref[:rows, :] = jnp.where(top, mine, got)
     packed_ref[rows : 2 * rows, :] = jnp.where(top, got, mine)
-    down, their_down = (ref[rows:, :].astype(jnp.float32) for ref in (mine_ref, got_ref))
-    low = lanes(down.shape) < down.shape[1] // 2
-    if_top = jnp.where(low, down, halves_swapped(their_down))
-    if_not = jnp.where(low, halves_swapped(their_down), down)
-    packed_ref[2 * rows :, :] = jnp.where(top, if_top, if_not).astype(jnp.bfloat16)
-
-
-def pack_shards(mine, got):
-    rows, width = mine.shape
+    packed_ref[2 * rows :, :] = half_of(
+        jnp.where(top, down, their_down), jnp.where(top, their_down, down)
+    )
+
+
+def pack_shards(own, got):
+    _, rows, width = own.shape
     return pl.pallas_call(
         pack_kernel,
-        out_shape=jax.ShapeDtypeStruct((3 * rows // 2, width), mine.dtype),
+        out_shape=jax.ShapeDtypeStruct((3 * rows, width), own.dtype),
         in_specs=whole(2),
         out_specs=whole(1)[0],
-        compiler_params=params(56),
+        compiler_params=params(2),
         name="pack_shards",
-    )(mine, got)
+    )(own, got)
 
 
 def expert_kernel(
@@ -329,21 +329,22 @@
 def per_device(tokens, cotangent, expert_ids, route_weights, join_groups, w_gate, w_up, w_down):
     plane = lax.axis_size(PLANE)
     chips = lax.axis_size("z")
-    mine, other = split_columns(w_gate, w_up, w_down)
-    got = lax.ppermute(other, "y", SWAP)
+    own = jnp.stack([w_gate, w_up, w_down])
+    got = lax.ppermute(own, "y", SWAP)
     copies, chooser, slot_weight = route(expert_ids, route_weights, tokens, cotangent, plane)
-    packed = pack_shards(mine, got)
+    packed = pack_shards(own, got)
     packed, copies = lax.optimization_barrier((packed, copies))
     rows_in = lax.all_to_all(copies, PLANE, 0, 0, tiled=True)
     along = lax.all_gather(packed, "z", axis=0, tiled=False)
     gathered = lax.all_gather(along, "c", axis=0, tiled=False)
     *partials, send, keep = expert(join_groups, rows_in, gathered)
     from_core = lax.ppermute(send, "c", SWAP)
+    own, right, across, left = spread(partials, "x", (0, 1, 2, 3))
     chip_sum = (keep + from_core.astype(jnp.float32)).astype(jnp.bfloat16)
     chip_sum = chip_sum.reshape(chips * 2, *chip_sum.shape[2:])
-    chip_sum, partials = lax.optimization_barrier((chip_sum, partials))
+    chip_sum, right, left = lax.optimization_barrier((chip_sum, right, left))
     pieces = lax.all_to_all(chip_sum, ("z", "y"), 0, 0, tiled=True)
-    quarters = add_quarters(spread(partials, "x", (0, 1, 2, 3)))
+    quarters = add_quarters((own, right, across, left))
     mixed = mix(spread(quarters, RING, (0, 2, 1, 3)), chooser, slot_weight)
     return (mixed, *finish(pieces))
 

time: 112 us -> 110 us (0.982); the launches traced: 110 us -> 109 us
  Pallas kernels: 12 us -> 7.91 us
  waiting for transfers between devices: 15.5 us -> 18.3 us
  starting transfers between devices: 41.2 us -> 42.4 us
    ppermute x6, waiting for transfers between devices: 13.9 us -> 17.5 us  [spread(): lax.ppermute(part, axes, [(ring[i], ring[(i + k) % 4]) for i in range(4)])]
    pallas_call x2 -> x1, Pallas kernels: 2.84 us -> 0.09 us  [pack_shards(): pl.pallas_call(pack_kernel, out_shape=jax.ShapeDtypeStruct((3 * rows, wid...]
    ppermute x1, waiting for transfers between devices: 1.52 us -> 0.01 us  [per_device(): from_core = lax.ppermute(send, 'c', SWAP)]
    pallas_call x1, Pallas kernels: 4.21 us -> 2.88 us  [route(): pl.pallas_call(route_kernel, out_shape=(jax.ShapeDtypeStruct((peers, 2 *...]
  transfers between devices with their start and end apart: 10 -> 10, of which waited for: 5 -> 6; matrix products, arithmetic and copies ran while one was open for 0% -> 1% of each run, Pallas kernels for 5% -> 4%
where the time goes in v3:
time: 110 us; the launch traced here: 109 us
  starting transfers between devices  42.4 us (39%)
  blocking collectives  38.3 us (35%)
  waiting for transfers between devices  18.3 us (17%)
  Pallas kernels  7.91 us (7%)
  other arithmetic  1.58 us (1%)
    all_gather x1, blocking collectives, per_device(): along = lax.all_gather(packed, 'z', axis=0, tiled=False)  35.9 us
    ppermute x6, starting transfers between devices, spread(): lax.ppermute(part, axes, [(ring[i], ring[(i + k) % 4]) for i in range(4)])  20 us
    ppermute x6, waiting for transfers between devices, spread(): lax.ppermute(part, axes, [(ring[i], ring[(i + k) % 4]) for i in range(4)])  17.5 us
    all_to_all x1, starting transfers between devices, per_device(): rows_in = lax.all_to_all(copies, PLANE, 0, 0, tiled=True)  8.71 us
    all_to_all x1, starting transfers between devices, per_device(): pieces = lax.all_to_all(chip_sum, ('z', 'y'), 0, 0, tiled=True)  8.13 us
    ppermute x1, starting transfers between devices, per_device(): got = lax.ppermute(own, 'y', SWAP)  3.47 us
    pallas_call x1, Pallas kernels, expert(): pl.pallas_call(expert_kernel, out_shape=(quarter, quarter, quarter, quart...  2.96 us
    pallas_call x1, Pallas kernels, route(): pl.pallas_call(route_kernel, out_shape=(jax.ShapeDtypeStruct((peers, 2 *...  2.88 us
  transfers between devices with their start and end apart: 10, of which 6 were waited for; matrix products, arithmetic and copies ran while one was open for 1% of the time, Pallas kernels for 4%

profile of v3, /device:TPU:6, one launch (start us, length us, event | category | flops | bytes accessed | tf_op | source)
XLA Modules:
  0.0 109.2 jit_solution(13458679799842746685)
XLA Ops:
  0.6 0.7 pad_maximum_fusion.own_ref
  1.4 3.5 %collective-permute-start = (bf16[3,32,128]{2,1,0:T(8,128)(2,1)S(1)}, bf16[3,32,128]{2,1,0:T(8,128)(2,1)S(1)}, u32[]{:S(2)}, u32[]{:S(2)}) collective-permute-start(bf16[3,32,128]{2,1,0:T(8,128)(2,1)S(1)} %pad_maximum_fusion.own_ref), channel_id=1, source_target_pairs={{0,16},{16,0},{1,17},{17,1},{2,18},{18,2},{3,19},{19,3},{4,20},{20... | collective-permute-start | bytes 73736 | tf_op jit(solution)/shard_map/ppermute | solution.py:333
  4.8 2.9 %route.1 = (bf16[16,32,2048]{2,1,0:T(8,128)(2,1)}, bf16[16,128]{1,0:T(8,128)(2,1)}, f32[16,128]{1,0:T(8,128)}) custom-call(s32[8,128]{1,0:T(8,128)} %bitcast.13, f32[8,128]{1,0:T(8,128)} %bitcast.14, bf16[128,2048]{1,0:T(8,128)(2,1)} %tokens_ref.1, bf16[128,2048]{1,0:T(8,128)(2,1)} %cot_ref.1), custom_call_target="tpu_custom_call" | custom-call | tf_op jit(solution)/shard_map/route/pallas_call | solution.py:95
  7.7 0.0 collective-permute-done.got_ref
  7.7 0.1 pack_shards.1
  7.8 0.0 copy-start.2
  7.9 8.7 %all-to-all-start = ((bf16[16,32,2048]{2,1,0:T(8,128)(2,1)}), bf16[16,32,2048]{2,1,0:T(8,128)(2,1)S(1)}, u32[]{:S(2)}, u32[]{:S(2)}) async-start(bf16[16,32,2048]{2,1,0:T(8,128)(2,1)} %get-tuple-element.26), calls=%async_computation | async-start | bytes 4194304 | tf_op jit(solution)/shard_map/all_to_all | solution.py:337
  16.6 35.9 %all-gather = bf16[1536,128]{1,0:T(8,128)(2,1)S(1)} all-gather(bf16[96,128]{1,0:T(8,128)(2,1)S(1)} %pack_shards.1), channel_id=2, replica_groups=mesh['z'=16,'y'=2,'c'=2,'h'=2,'x'=4] {'z'}, dimensions={0}, use_global_device_ids=true | all-gather | bytes 417792 | tf_op jit(solution)/shard_map/all_gather | solution.py:338
  52.5 2.4 %all-gather.1 = bf16[32,96,128]{2,1,0:T(8,128)(2,1)S(1)} all-gather(bf16[16,96,128]{2,1,0:T(8,128)(2,1)S(1)} %bitcast.9), channel_id=3, replica_groups=mesh['z'=16,'y'=2,'c'=2,'h'=2,'x'=4] {'c'}, dimensions={0}, use_global_device_ids=true | all-gather | bytes 1179648 | tf_op jit(solution)/shard_map/all_gather | solution.py:339
  54.8 0.0 all-to-all-done.both_ref
  54.8 0.0 copy-done.2
  54.8 3.0 %expert.1 = (bf16[4,16,2048]{2,1,0:T(8,128)(2,1)S(1)}, bf16[4,16,2048]{2,1,0:T(8,128)(2,1)S(1)}, bf16[4,16,2048]{2,1,0:T(8,128)(2,1)S(1)}, bf16[4,16,2048]{2,1,0...) custom-call(s32[64]{0:T(128)S(1)} %copy-done.2, ...), custom_call_target="tpu_custom_call" | custom-call | tf_op jit(solution)/shard_map/expert/pallas_call | solution.py:230
  57.8 0.0 copy-start
  57.8 0.0 copy-start.1
  57.8 2.1 %collective-permute-start.1 = (bf16[16,2,48,128]{3,2,1,0:T(8,128)(2,1)S(1)}, bf16[16,2,48,128]{3,2,1,0:T(8,128)(2,1)S(1)}, u32[]{:S(2)}, u32[]{:S(2)}) collective-permute-start(bf16[16,2,48,128]{3,2,1,0:T(8,128)(2,1)S(1)} %get-tuple-element.30), channel_id=1, source_target_pairs={{0,8},{8,0},{1,9},{9,1},{2,10},{10,2},{3,11},{11,3},{4,12},{12,4},... | collective-permute-start | bytes 1179656 | tf_op jit(solution)/shard_map/ppermute | solution.py:341
  59.9 2.2 %collective-permute-start.2 = (bf16[4,16,2048]{2,1,0:T(8,128)(2,1)S(1)}, bf16[4,16,2048]{2,1,0:T(8,128)(2,1)S(1)}, u32[]{:S(2)}, u32[]{:S(2)}) collective-permute-start(bf16[4,16,2048]{2,1,0:T(8,128)(2,1)S(1)} %get-tuple-element.31), channel_id=1, source_target_pairs={{0,1},{1,2},{2,3},{3,0},{4,5},{5,6},{6,7},{7,4},{8,9},{9,10},{10,1... | collective-permute-start | bytes 786440 | tf_op jit(solution)/shard_map/ppermute | solution.py:322
  62.2 3.6 %collective-permute-start.3 = (bf16[4,16,2048]{2,1,0:T(8,128)(2,1)S(1)}, bf16[4,16,2048]{2,1,0:T(8,128)(2,1)S(1)}, u32[]{:S(2)}, u32[]{:S(2)}) collective-permute-start(bf16[4,16,2048]{2,1,0:T(8,128)(2,1)S(1)} %get-tuple-element.32), channel_id=1, source_target_pairs={{0,3},{1,0},{2,1},{3,2},{4,7},{5,4},{6,5},{7,6},{8,11},{9,8},{10,9... | collective-permute-start | bytes 786440 | tf_op jit(solution)/shard_map/ppermute | solution.py:322
  65.8 0.0 collective-permute-done.1
  65.8 0.8 add_convert_fusion
  66.6 3.7 %collective-permute-done.2.refs_0_ = bf16[4,16,2048]{2,1,0:T(8,128)(2,1)S(1)} collective-permute-done((bf16[4,16,2048]{2,1,0:T(8,128)(2,1)S(1)}, bf16[4,16,2048]{2,1,0:T(8,128)(2,1)S(1)}, u32[]{:S(2)}, u32[]{:S(2)}) %collective-permute-start.2) | collective-permute-done | bytes 262176 | tf_op jit(solution)/shard_map/ppermute | solution.py:322
  70.4 3.2 %collective-permute-done.3.refs_2_ = bf16[4,16,2048]{2,1,0:T(8,128)(2,1)S(1)} collective-permute-done((bf16[4,16,2048]{2,1,0:T(8,128)(2,1)S(1)}, bf16[4,16,2048]{2,1,0:T(8,128)(2,1)S(1)}, u32[]{:S(2)}, u32[]{:S(2)}) %collective-permute-start.3) | collective-permute-done | bytes 262176 | tf_op jit(solution)/shard_map/ppermute | solution.py:322
  73.5 8.1 %all-to-all-start.1 = ((bf16[32,48,128]{2,1,0:T(8,128)(2,1)}), bf16[32,48,128]{2,1,0:T(8,128)(2,1)S(1)}, u32[]{:S(2)}, u32[]{:S(2)}) async-start(bf16[32,48,128]{2,1,0:T(8,128)(2,1)} %bitcast.7), calls=%async_computation.1 | async-start | bytes 786432 | tf_op jit(solution)/shard_map/all_to_all | solution.py:346
  81.7 3.1 %collective-permute-start.4 = (bf16[4,16,2048]{2,1,0:T(8,128)(2,1)S(1)}, bf16[4,16,2048]{2,1,0:T(8,128)(2,1)S(1)}, u32[]{:S(2)}, u32[]{:S(2)}) collective-permute-start(bf16[4,16,2048]{2,1,0:T(8,128)(2,1)S(1)} %get-tuple-element.34), channel_id=1, source_target_pairs={{0,2},{1,3},{2,0},{3,1},{4,6},{5,7},{6,4},{7,5},{8,10},{9,11},{10,... | collective-permute-start | bytes 786440 | tf_op jit(solution)/shard_map/ppermute | solution.py:322
  84.8 7.5 %collective-permute-done.4.refs_1_ = bf16[4,16,2048]{2,1,0:T(8,128)(2,1)S(1)} collective-permute-done((bf16[4,16,2048]{2,1,0:T(8,128)(2,1)S(1)}, bf16[4,16,2048]{2,1,0:T(8,128)(2,1)S(1)}, u32[]{:S(2)}, u32[]{:S(2)}) %collective-permute-start.4) | collective-permute-done | bytes 262176 | tf_op jit(solution)/shard_map/ppermute | solution.py:322
  92.2 0.1 add_quarters.1
  92.4 3.4 %collective-permute-start.5 = (bf16[16,2048]{1,0:T(8,128)(2,1)S(1)}, bf16[16,2048]{1,0:T(8,128)(2,1)S(1)}, u32[]{:S(2)}, u32[]{:S(2)}) collective-permute-start(bf16[16,2048]{1,0:T(8,128)(2,1)S(1)} %get-tuple-element.37), channel_id=1, source_target_pairs={{0,16},{16,4},{4,20},{20,0},{1,17},{17,5},{5,21},{21,1},{2,18},{18... | collective-permute-start | bytes 196616 | tf_op jit(solution)/shard_map/ppermute | solution.py:322
  95.8 4.6 %collective-permute-start.6 = (bf16[16,2048]{1,0:T(8,128)(2,1)S(1)}, bf16[16,2048]{1,0:T(8,128)(2,1)S(1)}, u32[]{:S(2)}, u32[]{:S(2)}) collective-permute-start(bf16[16,2048]{1,0:T(8,128)(2,1)S(1)} %get-tuple-element.38), channel_id=1, source_target_pairs={{0,4},{16,20},{4,0},{20,16},{1,5},{17,21},{5,1},{21,17},{2,6},{18,... | collective-permute-start | bytes 196616 | tf_op jit(solution)/shard_map/ppermute | solution.py:322
  100.4 3.0 %collective-permute-start.7 = (bf16[16,2048]{1,0:T(8,128)(2,1)S(1)}, bf16[16,2048]{1,0:T(8,128)(2,1)S(1)}, u32[]{:S(2)}, u32[]{:S(2)}) collective-permute-start(bf16[16,2048]{1,0:T(8,128)(2,1)S(1)} %get-tuple-element.39), channel_id=1, source_target_pairs={{0,20},{16,0},{4,16},{20,4},{1,21},{17,1},{5,17},{21,5},{2,22},{18... | collective-permute-start | bytes 196616 | tf_op jit(solution)/shard_map/ppermute | solution.py:322
  103.4 0.0 collective-permute-done.5.first_ref
  103.5 0.2 collective-permute-done.6.second_ref
  103.7 2.9 %collective-permute-done.7.third_ref = bf16[16,2048]{1,0:T(8,128)(2,1)S(1)} collective-permute-done((bf16[16,2048]{1,0:T(8,128)(2,1)S(1)}, bf16[16,2048]{1,0:T(8,128)(2,1)S(1)}, u32[]{:S(2)}, u32[]{:S(2)}) %collective-permute-start.7) | collective-permute-done | bytes 65568 | tf_op jit(solution)/shard_map/ppermute | solution.py:322
  106.6 0.0 copy-done
  106.6 0.0 copy-done.1
  106.6 1.1 %mix.1 = bf16[128,2048]{1,0:T(8,128)(2,1)} custom-call(bf16[16,2048]{1,0:T(8,128)(2,1)S(1)} %get-tuple-element.36.own_ref, bf16[16,2048]{1,0:T(8,128)(2,1)S(1)} %collective-permute-done.5.first_ref, bf16[16,2048]{1,0:T(8,128)(2,1)S(1)} %collective-permute-done.6.second_ref, bf16[16,2048]{1,0:T(8,128)(2,1)S(1)} %collective-permute-done.7.third_ref, ...), custom_call_target="tpu_custom_call" | custom-call | tf_op jit(solution)/shard_map/mix/pallas_call | solution.py:281
  107.7 0.8 all-to-all-done.1.blocks_ref
  108.5 0.7 finish.1
Async XLA Ops:
  1.4 6.4 %collective-permute-start = (bf16[3,32,128]{2,1,0:T(8,128)(2,1)S(1)}, bf16[3,32,128]{2,1,0:T(8,128)(2,1)S(1)}, u32[]{:S(2)}, u32[]{:S(2)}) collective-permute-start(bf16[3,32,128]{2,1,0:T(8,128)(2,1)S(1)} %pad_maximum_fusion.own_ref), channel_id=1, source_target_pairs={{0,16},{16,0},{1,17},{17,1},{2,18},{18,2},{3,19},{19,3},{4,20},{20... | collective-permute-start | bytes 73736 | tf_op jit(solution)/shard_map/ppermute | solution.py:333
  7.8 47.0 %copy-start.2 = (s32[64]{0:T(128)S(1)}, s32[64]{0:T(128)}, u32[]{:S(2)}) copy-start(s32[64]{0:T(128)} %join_ref.1) | copy-start | bytes 772
  7.9 47.0 %all-to-all-start = ((bf16[16,32,2048]{2,1,0:T(8,128)(2,1)}), bf16[16,32,2048]{2,1,0:T(8,128)(2,1)S(1)}, u32[]{:S(2)}, u32[]{:S(2)}) async-start(bf16[16,32,2048]{2,1,0:T(8,128)(2,1)} %get-tuple-element.26), calls=%async_computation | async-start | bytes 4194304 | tf_op jit(solution)/shard_map/all_to_all | solution.py:337
  57.8 48.8 %copy-start = (f32[16,128]{1,0:T(8,128)S(1)}, f32[16,128]{1,0:T(8,128)}, u32[]{:S(2)}) copy-start(f32[16,128]{1,0:T(8,128)} %get-tuple-element.41.slot_weight_ref) | copy-start | bytes 24580
  57.8 48.8 %copy-start.1 = (bf16[16,128]{1,0:T(8,128)(2,1)S(1)}, bf16[16,128]{1,0:T(8,128)(2,1)}, u32[]{:S(2)}) copy-start(bf16[16,128]{1,0:T(8,128)(2,1)} %get-tuple-element.40.chooser_ref) | copy-start | bytes 12292
  57.8 8.0 %collective-permute-start.1 = (bf16[16,2,48,128]{3,2,1,0:T(8,128)(2,1)S(1)}, bf16[16,2,48,128]{3,2,1,0:T(8,128)(2,1)S(1)}, u32[]{:S(2)}, u32[]{:S(2)}) collective-permute-start(bf16[16,2,48,128]{3,2,1,0:T(8,128)(2,1)S(1)} %get-tuple-element.30), channel_id=1, source_target_pairs={{0,8},{8,0},{1,9},{9,1},{2,10},{10,2},{3,11},{11,3},{4,12},{12,4},... | collective-permute-start | bytes 1179656 | tf_op jit(solution)/shard_map/ppermute | solution.py:341
  59.9 10.4 %collective-permute-start.2 = (bf16[4,16,2048]{2,1,0:T(8,128)(2,1)S(1)}, bf16[4,16,2048]{2,1,0:T(8,128)(2,1)S(1)}, u32[]{:S(2)}, u32[]{:S(2)}) collective-permute-start(bf16[4,16,2048]{2,1,0:T(8,128)(2,1)S(1)} %get-tuple-element.31), channel_id=1, source_target_pairs={{0,1},{1,2},{2,3},{3,0},{4,5},{5,6},{6,7},{7,4},{8,9},{9,10},{10,1... | collective-permute-start | bytes 786440 | tf_op jit(solution)/shard_map/ppermute | solution.py:322
  62.2 11.4 %collective-permute-start.3 = (bf16[4,16,2048]{2,1,0:T(8,128)(2,1)S(1)}, bf16[4,16,2048]{2,1,0:T(8,128)(2,1)S(1)}, u32[]{:S(2)}, u32[]{:S(2)}) collective-permute-start(bf16[4,16,2048]{2,1,0:T(8,128)(2,1)S(1)} %get-tuple-element.32), channel_id=1, source_target_pairs={{0,3},{1,0},{2,1},{3,2},{4,7},{5,4},{6,5},{7,6},{8,11},{9,8},{10,9... | collective-permute-start | bytes 786440 | tf_op jit(solution)/shard_map/ppermute | solution.py:322
  73.5 35.0 %all-to-all-start.1 = ((bf16[32,48,128]{2,1,0:T(8,128)(2,1)}), bf16[32,48,128]{2,1,0:T(8,128)(2,1)S(1)}, u32[]{:S(2)}, u32[]{:S(2)}) async-start(bf16[32,48,128]{2,1,0:T(8,128)(2,1)} %bitcast.7), calls=%async_computation.1 | async-start | bytes 786432 | tf_op jit(solution)/shard_map/all_to_all | solution.py:346
  81.7 10.6 %collective-permute-start.4 = (bf16[4,16,2048]{2,1,0:T(8,128)(2,1)S(1)}, bf16[4,16,2048]{2,1,0:T(8,128)(2,1)S(1)}, u32[]{:S(2)}, u32[]{:S(2)}) collective-permute-start(bf16[4,16,2048]{2,1,0:T(8,128)(2,1)S(1)} %get-tuple-element.34), channel_id=1, source_target_pairs={{0,2},{1,3},{2,0},{3,1},{4,6},{5,7},{6,4},{7,5},{8,10},{9,11},{10,... | collective-permute-start | bytes 786440 | tf_op jit(solution)/shard_map/ppermute | solution.py:322
  92.4 11.1 %collective-permute-start.5 = (bf16[16,2048]{1,0:T(8,128)(2,1)S(1)}, bf16[16,2048]{1,0:T(8,128)(2,1)S(1)}, u32[]{:S(2)}, u32[]{:S(2)}) collective-permute-start(bf16[16,2048]{1,0:T(8,128)(2,1)S(1)} %get-tuple-element.37), channel_id=1, source_target_pairs={{0,16},{16,4},{4,20},{20,0},{1,17},{17,5},{5,21},{21,1},{2,18},{18... | collective-permute-start | bytes 196616 | tf_op jit(solution)/shard_map/ppermute | solution.py:322
  95.8 7.9 %collective-permute-start.6 = (bf16[16,2048]{1,0:T(8,128)(2,1)S(1)}, bf16[16,2048]{1,0:T(8,128)(2,1)S(1)}, u32[]{:S(2)}, u32[]{:S(2)}) collective-permute-start(bf16[16,2048]{1,0:T(8,128)(2,1)S(1)} %get-tuple-element.38), channel_id=1, source_target_pairs={{0,4},{16,20},{4,0},{20,16},{1,5},{17,21},{5,1},{21,17},{2,6},{18,... | collective-permute-start | bytes 196616 | tf_op jit(solution)/shard_map/ppermute | solution.py:322
  100.4 6.2 %collective-permute-start.7 = (bf16[16,2048]{1,0:T(8,128)(2,1)S(1)}, bf16[16,2048]{1,0:T(8,128)(2,1)S(1)}, u32[]{:S(2)}, u32[]{:S(2)}) collective-permute-start(bf16[16,2048]{1,0:T(8,128)(2,1)S(1)} %get-tuple-element.39), channel_id=1, source_target_pairs={{0,20},{16,0},{4,16},{20,4},{1,21},{17,1},{5,17},{21,5},{2,22},{18... | collective-permute-start | bytes 196616 | tf_op jit(solution)/shard_map/ppermute | solution.py:322

commit v4 on v3

--- a/solution.py
+++ b/solution.py
@@ -7,7 +7,6 @@
 from jax.sharding import PartitionSpec as P
 
 AXES = ("z", "y", "c", "h", "x")
-RING = ("y", "h")
 PLANE = ("y", "h", "x")
 HBM = pl.BlockSpec(memory_space=pltpu.HBM)
 SWAP = ((0, 1), (1, 0))
@@ -130,19 +129,17 @@
 
     mine = half_of(own_ref[0], own_ref[1])
     got = half_of(got_ref[0], got_ref[1])
-    down, their_down = own_ref[2], got_ref[2]
     packed_ref[:rows, :] = jnp.where(top, mine, got)
     packed_ref[rows : 2 * rows, :] = jnp.where(top, got, mine)
-    packed_ref[2 * rows :, :] = half_of(
-        jnp.where(top, down, their_down), jnp.where(top, their_down, down)
-    )
+    packed_ref[2 * rows : 3 * rows, :] = jnp.where(top, own_ref[2], got_ref[2])
+    packed_ref[3 * rows :, :] = jnp.where(top, got_ref[2], own_ref[2])
 
 
 def pack_shards(own, got):
     _, rows, width = own.shape
     return pl.pallas_call(
         pack_kernel,
-        out_shape=jax.ShapeDtypeStruct((3 * rows, width), own.dtype),
+        out_shape=jax.ShapeDtypeStruct((4 * rows, width), own.dtype),
         in_specs=whole(2),
         out_specs=whole(1)[0],
         compiler_params=params(2),
@@ -151,26 +148,21 @@
 
 
 def expert_kernel(
-    join_ref, both_ref, packed_ref, partial_0, partial_1, partial_2, partial_3, send_ref, keep_ref,
-    gate_up, down, terms, partials,
+    join_ref, both_ref, own_ref, got_ref, hidden_send_ref, hidden_keep_ref, down, send_ref, keep_ref,
+    gate_up, terms, hiddens,
 ):
-    chips = packed_ref.shape[1]
-    rows = packed_ref.shape[2] // 3
-    width = packed_ref.shape[3]
+    chips, rows, width = own_ref.shape
+    rows = rows // 4
     half = width // 2
     peers, slots = both_ref.shape[0], both_ref.shape[1] // 2
     depth = both_ref.shape[2]
-    z, c = lax.axis_index("z"), lax.axis_index("c")
-    for chip in range(chips):
-        for core in range(2):
-            block = packed_ref[core, chip, 2 * rows :, :].astype(jnp.float32)
-            turned = pltpu.roll(block, half, 1)
-            low = lanes(block.shape) < half
-            doubled = (jnp.where(low, block, turned), jnp.where(low, turned, block))
-            for y in range(2):
-                at = ((chip * 2 + y) * 2 + core) * rows
-                gate_up[at : at + rows, :] = packed_ref[core, chip, y * rows : (y + 1) * rows, :]
-                down[at : at + rows, :] = doubled[y].astype(jnp.bfloat16)
+    z, y, c = lax.axis_index("z"), lax.axis_index("y"), lax.axis_index("c")
+    for core, ref in ((c, own_ref), (1 - c, got_ref)):
+        for chip in range(chips):
+            for k in range(2):
+                at = pl.multiple_of((chip * 2 + k) * 2 * rows + core * rows, rows)
+                gate_up[pl.ds(at, rows), :] = ref[chip, k * rows : (k + 1) * rows, :]
+                down[pl.ds(at, rows), :] = ref[chip, (2 + k) * rows : (3 + k) * rows, :]
     total = peers * slots
     picked = both_ref[:, :slots, :].reshape(total, depth)
     dpicked = both_ref[:, slots:, :].reshape(total, depth)
@@ -180,71 +172,89 @@
     gate, up = jnp.where(low, acts, turned), jnp.where(low, turned, acts)
     sigma = jax.nn.sigmoid(gate)
     hidden = gate * sigma * up
-    hidden_half = hidden.astype(jnp.bfloat16)
-    partial = lax.dot_general(
-        jnp.where(low, hidden, 0.0).astype(jnp.bfloat16),
-        down[...],
-        LANE_DIMS,
-        preferred_element_type=jnp.float32,
-    )
-    partials[...] = partial.reshape(partials.shape)
-    x, ring = lax.axis_index("x"), lax.axis_index("h") * 2 + lax.axis_index("y")
-    for step, ref in enumerate((partial_0, partial_1, partial_2, partial_3)):
-        for turn in range(4):
-            place = lax.rem(ring + turn, 4)
-            peer = (lax.rem(place, 2) * 2 + place // 2) * 4 + lax.rem(x + step, 4)
-            ref[turn] = partials[peer].astype(ref.dtype)
+    mine = (lanes(acts.shape) >= half) == (y == 1)
+    hiddens[...] = jnp.where(mine, hidden, 0.0)
+    group_rows = total // 2
+    hidden_send_ref[...] = hiddens[pl.ds((1 - y) * group_rows, group_rows), :].astype(jnp.bfloat16)
+    hidden_keep_ref[...] = hiddens[pl.ds(y * group_rows, group_rows), :].astype(jnp.bfloat16)
     dhidden = jnp.dot(dpicked, down[...], preferred_element_type=jnp.float32)
+    dhidden = jnp.where(mine, dhidden, pltpu.roll(dhidden, half, 1))
     dgate = dhidden * up * sigma * (1.0 + gate * (1.0 - sigma))
     dup = dhidden * gate * sigma
     first = 1.0 - join_ref[(z * 2 + 0) * 2 + c].astype(jnp.float32)
     second = 1.0 - join_ref[(z * 2 + 1) * 2 + c].astype(jnp.float32)
-    group = lax.broadcasted_iota(jnp.int32, acts.shape, 0) // (total // 2)
+    group = lax.broadcasted_iota(jnp.int32, acts.shape, 0) // group_rows
     active = jnp.where(group == 0, first, second)
     dacts = (jnp.where(low, dgate, dup) * active).astype(jnp.bfloat16)
-    counted = (hidden_half.astype(jnp.float32) * active).astype(jnp.bfloat16)
+    counted = (hidden.astype(jnp.bfloat16).astype(jnp.float32) * active).astype(jnp.bfloat16)
     terms[0] = lax.dot_general(picked, dacts, ROW_DIMS, preferred_element_type=jnp.float32)
     terms[1] = lax.dot_general(dpicked, counted, ROW_DIMS, preferred_element_type=jnp.float32)
     half_rows = rows // 2
     low = lanes((half_rows, width)) < half
     for chip in range(chips):
-        for y in range(2):
-            base = (chip * 2 + y) * 2 * rows
+        for k in range(2):
+            base = (chip * 2 + k) * 2 * rows
             for which, ref in ((c, keep_ref), (1 - c, send_ref)):
                 at = pl.multiple_of(base + which * rows, rows)
-                ref[chip, y, :rows, :] = terms[0, pl.ds(at, rows), :].astype(ref.dtype)
+                ref[chip, k, :rows, :] = terms[0, pl.ds(at, rows), :].astype(ref.dtype)
                 packed = jnp.where(
                     low,
                     terms[1, pl.ds(at, half_rows), :],
                     terms[1, pl.ds(at + half_rows, half_rows), :],
                 )
-                ref[chip, y, rows:, :] = packed.astype(ref.dtype)
-
-
-def expert(join, both, packed):
+                ref[chip, k, rows:, :] = packed.astype(ref.dtype)
+
+
+def expert(join, both, own, got):
     peers, doubled, depth = both.shape
     slots = doubled // 2
-    _, chips, rows, width = packed.shape
-    chunk = (chips, 2, rows // 2, width)
-    quarter = jax.ShapeDtypeStruct((peers // 4, slots, depth), jnp.bfloat16)
+    chips, rows, width = own.shape
+    chunk = (chips, 2, rows // 8 * 3, width)
+    hidden = jax.ShapeDtypeStruct((peers * slots // 2, width), jnp.bfloat16)
     return pl.pallas_call(
         expert_kernel,
         out_shape=(
-            quarter, quarter, quarter, quarter,
+            hidden,
+            hidden,
+            jax.ShapeDtypeStruct((depth, width), jnp.bfloat16),
             jax.ShapeDtypeStruct(chunk, jnp.bfloat16),
             jax.ShapeDtypeStruct(chunk, jnp.float32),
         ),
-        in_specs=[pl.BlockSpec(memory_space=pltpu.SMEM), *whole(2)],
-        out_specs=tuple(whole(6)),
+        in_specs=[pl.BlockSpec(memory_space=pltpu.SMEM), *whole(3)],
+        out_specs=tuple(whole(5)),
         scratch_shapes=[
             pltpu.VMEM((depth, width), jnp.bfloat16),
-            pltpu.VMEM((depth, width), jnp.bfloat16),
             pltpu.VMEM((2, depth, width), jnp.float32),
-            pltpu.VMEM((peers, slots, depth), jnp.float32),
+            pltpu.VMEM((peers * slots, width), jnp.float32),
         ],
         compiler_params=params(24),
         name="expert",
-    )(join, both, packed)
+    )(join, both, own, got)
+
+
+def partial_kernel(keep_ref, got_ref, down_ref, partial_0, partial_1, partial_2, partial_3, partials):
+    partial = lax.dot_general(
+        keep_ref[...] + got_ref[...], down_ref[...], LANE_DIMS, preferred_element_type=jnp.float32
+    )
+    partials[...] = partial.reshape(partials.shape)
+    h, x = lax.axis_index("h"), lax.axis_index("x")
+    for step, ref in enumerate((partial_0, partial_1, partial_2, partial_3)):
+        for turn in range(2):
+            peer = lax.rem(h + turn, 2) * 4 + lax.rem(x + step, 4)
+            ref[turn] = partials[peer].astype(ref.dtype)
+
+
+def partial_rows(keep, got, down, peers):
+    slots, depth = keep.shape[0] // peers, down.shape[0]
+    return pl.pallas_call(
+        partial_kernel,
+        out_shape=(jax.ShapeDtypeStruct((2, slots, depth), jnp.bfloat16),) * 4,
+        in_specs=whole(3),
+        out_specs=tuple(whole(4)),
+        scratch_shapes=[pltpu.VMEM((peers, slots, depth), jnp.float32)],
+        compiler_params=params(8),
+        name="partial_rows",
+    )(keep, got, down)
 
 
 def add_kernel(own_ref, *refs):
@@ -255,7 +265,7 @@
         ref[...] = total[k].astype(ref.dtype)
 
 
-def add_quarters(parts):
+def add_turns(parts):
     turns, slots, depth = parts[0].shape
     return pl.pallas_call(
         add_kernel,
@@ -263,29 +273,27 @@
         in_specs=whole(4),
         out_specs=tuple(whole(turns)),
         compiler_params=params(8),
-        name="add_quarters",
+        name="add_turns",
     )(*parts)
 
 
-def mix_kernel(own_ref, first_ref, second_ref, third_ref, chooser_ref, slot_weight_ref, mixed_ref):
-    total = own_ref[...].astype(jnp.float32)
-    for ref in (first_ref, second_ref, third_ref):
-        total += ref[...].astype(jnp.float32)
+def mix_kernel(own_ref, got_ref, chooser_ref, slot_weight_ref, mixed_ref):
+    total = own_ref[...].astype(jnp.float32) + got_ref[...].astype(jnp.float32)
     weighted = (total * slot_weight_ref[:, :1]).astype(jnp.bfloat16)
     mixed_ref[...] = lax.dot_general(
         chooser_ref[...], weighted, ROW_DIMS, preferred_element_type=jnp.float32
     ).astype(jnp.bfloat16)
 
 
-def mix(parts, chooser, slot_weight):
+def mix(own, got, chooser, slot_weight):
     return pl.pallas_call(
         mix_kernel,
-        out_shape=jax.ShapeDtypeStruct((chooser.shape[1], parts[0].shape[1]), jnp.bfloat16),
-        in_specs=whole(6),
+        out_shape=jax.ShapeDtypeStruct((chooser.shape[1], own.shape[1]), jnp.bfloat16),
+        in_specs=whole(4),
         out_specs=whole(1)[0],
         compiler_params=params(8),
         name="mix",
-    )(*parts, chooser, slot_weight)
+    )(own, got, chooser, slot_weight)
 
 
 def finish_kernel(blocks_ref, gate_ref, up_ref, down_ref):
@@ -317,9 +325,9 @@
     )(blocks)
 
 
-def spread(parts, axes, ring):
+def spread(parts, axis):
     came = [
-        lax.ppermute(part, axes, [(ring[i], ring[(i + k) % 4]) for i in range(4)])
+        lax.ppermute(part, axis, [(i, (i + k) % 4) for i in range(4)])
         for k, part in enumerate(parts)
         if k
     ]
@@ -327,25 +335,27 @@
 
 
 def per_device(tokens, cotangent, expert_ids, route_weights, join_groups, w_gate, w_up, w_down):
-    plane = lax.axis_size(PLANE)
     chips = lax.axis_size("z")
     own = jnp.stack([w_gate, w_up, w_down])
     got = lax.ppermute(own, "y", SWAP)
-    copies, chooser, slot_weight = route(expert_ids, route_weights, tokens, cotangent, plane)
+    copies, chooser, slot_weight = route(
+        expert_ids, route_weights, tokens, cotangent, lax.axis_size(PLANE)
+    )
     packed = pack_shards(own, got)
     packed, copies = lax.optimization_barrier((packed, copies))
     rows_in = lax.all_to_all(copies, PLANE, 0, 0, tiled=True)
     along = lax.all_gather(packed, "z", axis=0, tiled=False)
-    gathered = lax.all_gather(along, "c", axis=0, tiled=False)
-    *partials, send, keep = expert(join_groups, rows_in, gathered)
+    other = lax.ppermute(along, "c", SWAP)
+    hidden_send, hidden, down, send, keep = expert(join_groups, rows_in, along, other)
     from_core = lax.ppermute(send, "c", SWAP)
-    own, right, across, left = spread(partials, "x", (0, 1, 2, 3))
+    hidden_got = lax.ppermute(hidden_send, "y", SWAP)
     chip_sum = (keep + from_core.astype(jnp.float32)).astype(jnp.bfloat16)
     chip_sum = chip_sum.reshape(chips * 2, *chip_sum.shape[2:])
-    chip_sum, right, left = lax.optimization_barrier((chip_sum, right, left))
+    chip_sum, hidden_got = lax.optimization_barrier((chip_sum, hidden_got))
     pieces = lax.all_to_all(chip_sum, ("z", "y"), 0, 0, tiled=True)
-    quarters = add_quarters((own, right, across, left))
-    mixed = mix(spread(quarters, RING, (0, 2, 1, 3)), chooser, slot_weight)
+    partials = partial_rows(hidden, hidden_got, down, lax.axis_size(("h", "x")))
+    mine, theirs = add_turns(spread(partials, "x"))
+    mixed = mix(mine, lax.ppermute(theirs, "h", SWAP), chooser, slot_weight)
     return (mixed, *finish(pieces))
 
 

time: 110 us -> 106 us (0.964)
  waiting for transfers between devices: 18.3 us -> 15.5 us
  local copies, waits for them, and re-layouts: 0.02 us -> 1.85 us
  starting transfers between devices: 42.4 us -> 40.8 us
  blocking collectives: 38.3 us -> 36.7 us
    ppermute x6, waiting for transfers between devices: 17.5 us -> 12.8 us  [the longest x3 6.14 us: spread(): lax.ppermute(part, axis, [(i, (i + k) % 4) for i in range(4)])]
    all_gather x1 -> x0, blocking collectives: 2.36 us -> none  [per_device(): gathered = lax.all_gather(along, 'c', axis=0, tiled=False)]
    all_to_all x1, waiting for transfers between devices: 0.82 us -> 2.69 us  [per_device(): pieces = lax.all_to_all(chip_sum, ('z', 'y'), 0, 0, tiled=True)]
    unnamed x6 -> x10, local copies, waits for them, and re-layouts: 0.02 us -> 1.85 us
    ppermute x6, starting transfers between devices: 20 us -> 18.5 us  [the longest x3 8.59 us: spread(): lax.ppermute(part, axis, [(i, (i + k) % 4) for i in range(4)])]
    pallas_call x3 -> x4, Pallas kernels: 3.18 us -> 3.29 us  [the longest x1 2.78 us: expert(): pl.pallas_call(expert_kernel, out_shape=(hidden, hidden, jax.ShapeDtypeSt...]
where the time goes in v4:
time: 106 us; the launch traced here: 105 us
  starting transfers between devices  40.8 us (38%)
  blocking collectives  36.7 us (35%)
  waiting for transfers between devices  15.5 us (15%)
  Pallas kernels  8.02 us (8%)
  local copies, waits for them, and re-layouts  1.85 us (2%)
  other arithmetic  1.58 us (1%)
    all_gather x1, blocking collectives, per_device(): along = lax.all_gather(packed, 'z', axis=0, tiled=False)  36.7 us
    all_to_all x1, starting transfers between devices, per_device(): rows_in = lax.all_to_all(copies, PLANE, 0, 0, tiled=True)  8.71 us
    ppermute x3, starting transfers between devices, spread(): lax.ppermute(part, axis, [(i, (i + k) % 4) for i in range(4)])  8.59 us
    all_to_all x1, starting transfers between devices, per_device(): pieces = lax.all_to_all(chip_sum, ('z', 'y'), 0, 0, tiled=True)  8.02 us
    ppermute x3, waiting for transfers between devices, spread(): lax.ppermute(part, axis, [(i, (i + k) % 4) for i in range(4)])  6.14 us
    ppermute x1, starting transfers between devices, per_device(): mixed = mix(mine, lax.ppermute(theirs, 'h', SWAP), chooser, slot_weight)  4.6 us
    ppermute x1, starting transfers between devices, per_device(): got = lax.ppermute(own, 'y', SWAP)  3.47 us
    ppermute x1, starting transfers between devices, per_device(): hidden_got = lax.ppermute(hidden_send, 'y', SWAP)  3.37 us
  transfers between devices with their start and end apart: 10, of which 6 were waited for; matrix products, arithmetic and copies ran while one was open for 1% of the time, Pallas kernels for 4%

profile of v4, /device:TPU:6, one launch (start us, length us, event | category | flops | bytes accessed | tf_op | source)
XLA Modules:
  0.0 105.2 jit_solution(1184678713861096931)
XLA Ops:
  0.6 0.7 pad_maximum_fusion.own_ref
  1.4 3.5 %collective-permute-start = (bf16[3,32,128]{2,1,0:T(8,128)(2,1)S(1)}, bf16[3,32,128]{2,1,0:T(8,128)(2,1)S(1)}, u32[]{:S(2)}, u32[]{:S(2)}) collective-permute-start(bf16[3,32,128]{2,1,0:T(8,128)(2,1)S(1)} %pad_maximum_fusion.own_ref), channel_id=1, source_target_pairs={{0,16},{16,0},{1,17},{17,1},{2,18},{18,2},{3,19},{19,3},{4,20},{20... | collective-permute-start | bytes 73736 | tf_op jit(solution)/shard_map/ppermute | solution.py:340
  4.8 2.9 %route.1 = (bf16[16,32,2048]{2,1,0:T(8,128)(2,1)}, bf16[16,128]{1,0:T(8,128)(2,1)}, f32[16,128]{1,0:T(8,128)}) custom-call(s32[8,128]{1,0:T(8,128)} %bitcast.12, f32[8,128]{1,0:T(8,128)} %bitcast.13, bf16[128,2048]{1,0:T(8,128)(2,1)} %tokens_ref.1, bf16[128,2048]{1,0:T(8,128)(2,1)} %cot_ref.1), custom_call_target="tpu_custom_call" | custom-call | tf_op jit(solution)/shard_map/route/pallas_call | solution.py:94
  7.7 0.0 collective-permute-done.got_ref
  7.7 0.1 pack_shards.1
  7.8 0.0 copy-start.4
  7.8 8.7 %all-to-all-start = ((bf16[16,32,2048]{2,1,0:T(8,128)(2,1)}), bf16[16,32,2048]{2,1,0:T(8,128)(2,1)S(1)}, u32[]{:S(2)}, u32[]{:S(2)}) async-start(bf16[16,32,2048]{2,1,0:T(8,128)(2,1)} %get-tuple-element.26), calls=%async_computation | async-start | bytes 4194304 | tf_op jit(solution)/shard_map/all_to_all | solution.py:346
  16.6 36.7 %all-gather = bf16[2048,128]{1,0:T(8,128)(2,1)S(1)} all-gather(bf16[128,128]{1,0:T(8,128)(2,1)S(1)} %pack_shards.1), channel_id=2, replica_groups=mesh['z'=16,'y'=2,'c'=2,'h'=2,'x'=4] {'z'}, dimensions={0}, use_global_device_ids=true | all-gather | bytes 557056 | tf_op jit(solution)/shard_map/all_gather | solution.py:347
  53.3 1.9 %collective-permute-start.1 = (bf16[16,128,128]{2,1,0:T(8,128)(2,1)S(1)}, bf16[16,128,128]{2,1,0:T(8,128)(2,1)S(1)}, u32[]{:S(2)}, u32[]{:S(2)}) collective-permute-start(bf16[16,128,128]{2,1,0:T(8,128)(2,1)S(1)} %bitcast.7), channel_id=1, source_target_pairs={{0,8},{8,0},{1,9},{9,1},{2,10},{10,2},{3,11},{11,3},{4,12},{12,4},... | collective-permute-start | bytes 1572872 | tf_op jit(solution)/shard_map/ppermute | solution.py:348
  55.2 1.9 %collective-permute-done.1.got_ref = bf16[16,128,128]{2,1,0:T(8,128)(2,1)S(1)} collective-permute-done((bf16[16,128,128]{2,1,0:T(8,128)(2,1)S(1)}, bf16[16,128,128]{2,1,0:T(8,128)(2,1)S(1)}, u32[]{:S(2)}, u32[]{:S(2)}) %collective-permute-start.1) | collective-permute-done | bytes 524320 | tf_op jit(solution)/shard_map/ppermute | solution.py:348
  57.1 0.0 copy-start
  57.1 0.8 copy-done
  57.9 0.0 all-to-all-done.both_ref
  57.9 0.0 copy-done.4
  57.9 0.0 copy-start.1
  57.9 1.0 copy-done.1
  58.9 2.8 %expert.1 = (bf16[128,128]{1,0:T(8,128)(2,1)S(1)}, bf16[128,128]{1,0:T(8,128)(2,1)S(1)}, bf16[2048,128]{1,0:T(8,128)(2,1)S(1)}, bf16[16,2,48,128]{3,2,1,0:T(8,128)(2,1)S(1)}, f32[16,2,48,128]{3,2,1,0:T(8,128)S(1)}) custom-call(s32[64]{0:T(128)S(1)} %copy-done.4, bf16[16,32,2048]{2,1,0:T(8,128)(2,1)S(1)} %all-to-all-done.both_ref, ...), custom_call_target="tpu_custom_call" | custom-call | tf_op jit(solution)/shard_map/expert/pallas_call | solution.py:214
  61.7 0.0 copy-start.2
  61.7 0.0 copy-start.3
  61.7 2.1 %collective-permute-start.2 = (bf16[16,2,48,128]{3,2,1,0:T(8,128)(2,1)S(1)}, bf16[16,2,48,128]{3,2,1,0:T(8,128)(2,1)S(1)}, u32[]{:S(2)}, u32[]{:S(2)}) collective-permute-start(bf16[16,2,48,128]{3,2,1,0:T(8,128)(2,1)S(1)} %get-tuple-element.30), channel_id=1, source_target_pairs={{0,8},{8,0},{1,9},{9,1},{2,10},{10,2},{3,11},{11,3},{4,12},{12,4},... | collective-permute-start | bytes 1179656 | tf_op jit(solution)/shard_map/ppermute | solution.py:350
  63.8 3.4 %collective-permute-start.3 = (bf16[128,128]{1,0:T(8,128)(2,1)S(1)}, bf16[128,128]{1,0:T(8,128)(2,1)S(1)}, u32[]{:S(2)}, u32[]{:S(2)}) collective-permute-start(bf16[128,128]{1,0:T(8,128)(2,1)S(1)} %get-tuple-element.31), channel_id=1, source_target_pairs={{0,16},{16,0},{1,17},{17,1},{2,18},{18,2},{3,19},{19,3},{4,20},{20... | collective-permute-start | bytes 98312 | tf_op jit(solution)/shard_map/ppermute | solution.py:351
  67.2 0.0 collective-permute-done.2
  67.2 0.8 add_convert_fusion
  68.1 1.6 %collective-permute-done.3.got_ref = bf16[128,128]{1,0:T(8,128)(2,1)S(1)} collective-permute-done((bf16[128,128]{1,0:T(8,128)(2,1)S(1)}, bf16[128,128]{1,0:T(8,128)(2,1)S(1)}, u32[]{:S(2)}, u32[]{:S(2)}) %collective-permute-start.3) | collective-permute-done | bytes 32800 | tf_op jit(solution)/shard_map/ppermute | solution.py:351
  69.6 8.0 %all-to-all-start.1 = ((bf16[32,48,128]{2,1,0:T(8,128)(2,1)}), bf16[32,48,128]{2,1,0:T(8,128)(2,1)S(1)}, u32[]{:S(2)}, u32[]{:S(2)}) async-start(bf16[32,48,128]{2,1,0:T(8,128)(2,1)} %bitcast.6), calls=%async_computation.1 | async-start | bytes 786432 | tf_op jit(solution)/shard_map/all_to_all | solution.py:355
  77.7 0.4 partial_rows.1
  78.0 2.2 %collective-permute-start.4 = (bf16[2,16,2048]{2,1,0:T(8,128)(2,1)S(1)}, bf16[2,16,2048]{2,1,0:T(8,128)(2,1)S(1)}, u32[]{:S(2)}, u32[]{:S(2)}) collective-permute-start(bf16[2,16,2048]{2,1,0:T(8,128)(2,1)S(1)} %get-tuple-element.35), channel_id=1, source_target_pairs={{0,1},{1,2},{2,3},{3,0},{4,5},{5,6},{6,7},{7,4},{8,9},{9,10},{10,1... | collective-permute-start | bytes 393224 | tf_op jit(solution)/shard_map/ppermute | solution.py:330
  80.3 4.4 %collective-permute-start.5 = (bf16[2,16,2048]{2,1,0:T(8,128)(2,1)S(1)}, bf16[2,16,2048]{2,1,0:T(8,128)(2,1)S(1)}, u32[]{:S(2)}, u32[]{:S(2)}) collective-permute-start(bf16[2,16,2048]{2,1,0:T(8,128)(2,1)S(1)} %get-tuple-element.36), channel_id=1, source_target_pairs={{0,2},{1,3},{2,0},{3,1},{4,6},{5,7},{6,4},{7,5},{8,10},{9,11},{10,... | collective-permute-start | bytes 393224 | tf_op jit(solution)/shard_map/ppermute | solution.py:330
  84.7 1.9 %collective-permute-start.6 = (bf16[2,16,2048]{2,1,0:T(8,128)(2,1)S(1)}, bf16[2,16,2048]{2,1,0:T(8,128)(2,1)S(1)}, u32[]{:S(2)}, u32[]{:S(2)}) collective-permute-start(bf16[2,16,2048]{2,1,0:T(8,128)(2,1)S(1)} %get-tuple-element.37), channel_id=1, source_target_pairs={{0,3},{1,0},{2,1},{3,2},{4,7},{5,4},{6,5},{7,6},{8,11},{9,8},{10,9... | collective-permute-start | bytes 393224 | tf_op jit(solution)/shard_map/ppermute | solution.py:330
  86.6 0.0 collective-permute-done.4.refs_0_
  86.7 2.0 %collective-permute-done.5.refs_1_ = bf16[2,16,2048]{2,1,0:T(8,128)(2,1)S(1)} collective-permute-done((bf16[2,16,2048]{2,1,0:T(8,128)(2,1)S(1)}, bf16[2,16,2048]{2,1,0:T(8,128)(2,1)S(1)}, u32[]{:S(2)}, u32[]{:S(2)}) %collective-permute-start.5) | collective-permute-done | bytes 131104 | tf_op jit(solution)/shard_map/ppermute | solution.py:330
  88.6 4.2 %collective-permute-done.6.refs_2_ = bf16[2,16,2048]{2,1,0:T(8,128)(2,1)S(1)} collective-permute-done((bf16[2,16,2048]{2,1,0:T(8,128)(2,1)S(1)}, bf16[2,16,2048]{2,1,0:T(8,128)(2,1)S(1)}, u32[]{:S(2)}, u32[]{:S(2)}) %collective-permute-start.6) | collective-permute-done | bytes 131104 | tf_op jit(solution)/shard_map/ppermute | solution.py:330
  92.8 0.1 add_turns.1
  92.9 4.6 %collective-permute-start.7 = (bf16[16,2048]{1,0:T(8,128)(2,1)S(1)}, bf16[16,2048]{1,0:T(8,128)(2,1)S(1)}, u32[]{:S(2)}, u32[]{:S(2)}) collective-permute-start(bf16[16,2048]{1,0:T(8,128)(2,1)S(1)} %get-tuple-element.39), channel_id=1, source_target_pairs={{0,4},{4,0},{1,5},{5,1},{2,6},{6,2},{3,7},{7,3},{8,12},{12,8},{9,1... | collective-permute-start | bytes 196616 | tf_op jit(solution)/shard_map/ppermute | solution.py:358
  97.5 3.2 %collective-permute-done.7.got_ref = bf16[16,2048]{1,0:T(8,128)(2,1)S(1)} collective-permute-done((bf16[16,2048]{1,0:T(8,128)(2,1)S(1)}, bf16[16,2048]{1,0:T(8,128)(2,1)S(1)}, u32[]{:S(2)}, u32[]{:S(2)}) %collective-permute-start.7) | collective-permute-done | bytes 65568 | tf_op jit(solution)/shard_map/ppermute | solution.py:358
  100.7 0.0 copy-done.2
  100.7 0.0 copy-done.3
  100.7 1.1 %mix.1 = bf16[128,2048]{1,0:T(8,128)(2,1)} custom-call(bf16[16,2048]{1,0:T(8,128)(2,1)S(1)} %get-tuple-element.38.own_ref, bf16[16,2048]{1,0:T(8,128)(2,1)S(1)} %collective-permute-done.7.got_ref, bf16[16,128]{1,0:T(8,128)(2,1)S(1)} %copy-done.3, f32[16,128]{1,0:T(8,128)S(1)} %copy-done.2), custom_call_target="tpu_custom_call" | custom-call | tf_op jit(solution)/shard_map/mix/pallas_call | solution.py:289
  101.8 2.7 %all-to-all-done.1.blocks_ref = bf16[32,48,128]{2,1,0:T(8,128)(2,1)S(1)} async-done(((bf16[32,48,128]{2,1,0:T(8,128)(2,1)}), bf16[32,48,128]{2,1,0:T(8,128)(2,1)S(1)}, u32[]{:S(2)}, u32[]{:S(2)}) %all-to-all-start.1) | async-done | bytes 393248 | tf_op jit(solution)/shard_map/all_to_all | solution.py:355
  104.5 0.7 finish.1
Async XLA Ops:
  1.4 6.4 %collective-permute-start = (bf16[3,32,128]{2,1,0:T(8,128)(2,1)S(1)}, bf16[3,32,128]{2,1,0:T(8,128)(2,1)S(1)}, u32[]{:S(2)}, u32[]{:S(2)}) collective-permute-start(bf16[3,32,128]{2,1,0:T(8,128)(2,1)S(1)} %pad_maximum_fusion.own_ref), channel_id=1, source_target_pairs={{0,16},{16,0},{1,17},{17,1},{2,18},{18,2},{3,19},{19,3},{4,20},{20... | collective-permute-start | bytes 73736 | tf_op jit(solution)/shard_map/ppermute | solution.py:340
  7.8 50.1 %copy-start.4 = (s32[64]{0:T(128)S(1)}, s32[64]{0:T(128)}, u32[]{:S(2)}) copy-start(s32[64]{0:T(128)} %join_ref.1) | copy-start | bytes 772
  7.8 50.0 %all-to-all-start = ((bf16[16,32,2048]{2,1,0:T(8,128)(2,1)}), bf16[16,32,2048]{2,1,0:T(8,128)(2,1)S(1)}, u32[]{:S(2)}, u32[]{:S(2)}) async-start(bf16[16,32,2048]{2,1,0:T(8,128)(2,1)} %get-tuple-element.26), calls=%async_computation | async-start | bytes 4194304 | tf_op jit(solution)/shard_map/all_to_all | solution.py:346
  53.3 3.8 %collective-permute-start.1 = (bf16[16,128,128]{2,1,0:T(8,128)(2,1)S(1)}, bf16[16,128,128]{2,1,0:T(8,128)(2,1)S(1)}, u32[]{:S(2)}, u32[]{:S(2)}) collective-permute-start(bf16[16,128,128]{2,1,0:T(8,128)(2,1)S(1)} %bitcast.7), channel_id=1, source_target_pairs={{0,8},{8,0},{1,9},{9,1},{2,10},{10,2},{3,11},{11,3},{4,12},{12,4},... | collective-permute-start | bytes 1572872 | tf_op jit(solution)/shard_map/ppermute | solution.py:348
  57.1 0.8 copy-start
  57.9 1.0 copy-start.1
  61.7 38.9 %copy-start.2 = (f32[16,128]{1,0:T(8,128)S(1)}, f32[16,128]{1,0:T(8,128)}, u32[]{:S(2)}) copy-start(f32[16,128]{1,0:T(8,128)} %get-tuple-element.41.slot_weight_ref) | copy-start | bytes 24580
  61.7 38.9 %copy-start.3 = (bf16[16,128]{1,0:T(8,128)(2,1)S(1)}, bf16[16,128]{1,0:T(8,128)(2,1)}, u32[]{:S(2)}) copy-start(bf16[16,128]{1,0:T(8,128)(2,1)} %get-tuple-element.40.chooser_ref) | copy-start | bytes 12292
  61.7 5.5 %collective-permute-start.2 = (bf16[16,2,48,128]{3,2,1,0:T(8,128)(2,1)S(1)}, bf16[16,2,48,128]{3,2,1,0:T(8,128)(2,1)S(1)}, u32[]{:S(2)}, u32[]{:S(2)}) collective-permute-start(bf16[16,2,48,128]{3,2,1,0:T(8,128)(2,1)S(1)} %get-tuple-element.30), channel_id=1, source_target_pairs={{0,8},{8,0},{1,9},{9,1},{2,10},{10,2},{3,11},{11,3},{4,12},{12,4},... | collective-permute-start | bytes 1179656 | tf_op jit(solution)/shard_map/ppermute | solution.py:350
  63.8 5.8 %collective-permute-start.3 = (bf16[128,128]{1,0:T(8,128)(2,1)S(1)}, bf16[128,128]{1,0:T(8,128)(2,1)S(1)}, u32[]{:S(2)}, u32[]{:S(2)}) collective-permute-start(bf16[128,128]{1,0:T(8,128)(2,1)S(1)} %get-tuple-element.31), channel_id=1, source_target_pairs={{0,16},{16,0},{1,17},{17,1},{2,18},{18,2},{3,19},{19,3},{4,20},{20... | collective-permute-start | bytes 98312 | tf_op jit(solution)/shard_map/ppermute | solution.py:351
  69.6 34.8 %all-to-all-start.1 = ((bf16[32,48,128]{2,1,0:T(8,128)(2,1)}), bf16[32,48,128]{2,1,0:T(8,128)(2,1)S(1)}, u32[]{:S(2)}, u32[]{:S(2)}) async-start(bf16[32,48,128]{2,1,0:T(8,128)(2,1)} %bitcast.6), calls=%async_computation.1 | async-start | bytes 786432 | tf_op jit(solution)/shard_map/all_to_all | solution.py:355
  78.0 8.6 %collective-permute-start.4 = (bf16[2,16,2048]{2,1,0:T(8,128)(2,1)S(1)}, bf16[2,16,2048]{2,1,0:T(8,128)(2,1)S(1)}, u32[]{:S(2)}, u32[]{:S(2)}) collective-permute-start(bf16[2,16,2048]{2,1,0:T(8,128)(2,1)S(1)} %get-tuple-element.35), channel_id=1, source_target_pairs={{0,1},{1,2},{2,3},{3,0},{4,5},{5,6},{6,7},{7,4},{8,9},{9,10},{10,1... | collective-permute-start | bytes 393224 | tf_op jit(solution)/shard_map/ppermute | solution.py:330
  80.3 8.4 %collective-permute-start.5 = (bf16[2,16,2048]{2,1,0:T(8,128)(2,1)S(1)}, bf16[2,16,2048]{2,1,0:T(8,128)(2,1)S(1)}, u32[]{:S(2)}, u32[]{:S(2)}) collective-permute-start(bf16[2,16,2048]{2,1,0:T(8,128)(2,1)S(1)} %get-tuple-element.36), channel_id=1, source_target_pairs={{0,2},{1,3},{2,0},{3,1},{4,6},{5,7},{6,4},{7,5},{8,10},{9,11},{10,... | collective-permute-start | bytes 393224 | tf_op jit(solution)/shard_map/ppermute | solution.py:330
  84.7 8.1 %collective-permute-start.6 = (bf16[2,16,2048]{2,1,0:T(8,128)(2,1)S(1)}, bf16[2,16,2048]{2,1,0:T(8,128)(2,1)S(1)}, u32[]{:S(2)}, u32[]{:S(2)}) collective-permute-start(bf16[2,16,2048]{2,1,0:T(8,128)(2,1)S(1)} %get-tuple-element.37), channel_id=1, source_target_pairs={{0,3},{1,0},{2,1},{3,2},{4,7},{5,4},{6,5},{7,6},{8,11},{9,8},{10,9... | collective-permute-start | bytes 393224 | tf_op jit(solution)/shard_map/ppermute | solution.py:330
  92.9 7.8 %collective-permute-start.7 = (bf16[16,2048]{1,0:T(8,128)(2,1)S(1)}, bf16[16,2048]{1,0:T(8,128)(2,1)S(1)}, u32[]{:S(2)}, u32[]{:S(2)}) collective-permute-start(bf16[16,2048]{1,0:T(8,128)(2,1)S(1)} %get-tuple-element.39), channel_id=1, source_target_pairs={{0,4},{4,0},{1,5},{5,1},{2,6},{6,2},{3,7},{7,3},{8,12},{12,8},{9,1... | collective-permute-start | bytes 196616 | tf_op jit(solution)/shard_map/ppermute | solution.py:358

commit v5 on v4

--- a/solution.py
+++ b/solution.py
@@ -6,10 +6,10 @@
 from jax.sharding import Mesh
 from jax.sharding import PartitionSpec as P
 
-AXES = ("z", "y", "c", "h", "x")
+AXES = ("zh", "zl", "y", "c", "h", "x")
+Z = ("zh", "zl")
 PLANE = ("y", "h", "x")
 HBM = pl.BlockSpec(memory_space=pltpu.HBM)
-SWAP = ((0, 1), (1, 0))
 ROW_DIMS = (((0,), (0,)), ((), ()))
 LANE_DIMS = (((1,), (1,)), ((), ()))
 
@@ -156,7 +156,7 @@
     half = width // 2
     peers, slots = both_ref.shape[0], both_ref.shape[1] // 2
     depth = both_ref.shape[2]
-    z, y, c = lax.axis_index("z"), lax.axis_index("y"), lax.axis_index("c")
+    z, y, c = lax.axis_index(Z), lax.axis_index("y"), lax.axis_index("c")
     for core, ref in ((c, own_ref), (1 - c, got_ref)):
         for chip in range(chips):
             for k in range(2):
@@ -194,22 +194,23 @@
     for chip in range(chips):
         for k in range(2):
             base = (chip * 2 + k) * 2 * rows
+            away = jnp.bitwise_xor(chip % 2, lax.rem(z, 2))
             for which, ref in ((c, keep_ref), (1 - c, send_ref)):
                 at = pl.multiple_of(base + which * rows, rows)
-                ref[chip, k, :rows, :] = terms[0, pl.ds(at, rows), :].astype(ref.dtype)
+                ref[away, chip // 2, k, :rows, :] = terms[0, pl.ds(at, rows), :].astype(ref.dtype)
                 packed = jnp.where(
                     low,
                     terms[1, pl.ds(at, half_rows), :],
                     terms[1, pl.ds(at + half_rows, half_rows), :],
                 )
-                ref[chip, k, rows:, :] = packed.astype(ref.dtype)
+                ref[away, chip // 2, k, rows:, :] = packed.astype(ref.dtype)
 
 
 def expert(join, both, own, got):
     peers, doubled, depth = both.shape
     slots = doubled // 2
     chips, rows, width = own.shape
-    chunk = (chips, 2, rows // 8 * 3, width)
+    chunk = (2, chips // 2, 2, rows // 8 * 3, width)
     hidden = jax.ShapeDtypeStruct((peers * slots // 2, width), jnp.bfloat16)
     return pl.pallas_call(
         expert_kernel,
@@ -232,53 +233,58 @@
     )(join, both, own, got)
 
 
-def partial_kernel(keep_ref, got_ref, down_ref, partial_0, partial_1, partial_2, partial_3, partials):
+def partial_kernel(keep_ref, got_ref, down_ref, mine_ref, theirs_ref, partials):
     partial = lax.dot_general(
         keep_ref[...] + got_ref[...], down_ref[...], LANE_DIMS, preferred_element_type=jnp.float32
     )
     partials[...] = partial.reshape(partials.shape)
     h, x = lax.axis_index("h"), lax.axis_index("x")
-    for step, ref in enumerate((partial_0, partial_1, partial_2, partial_3)):
-        for turn in range(2):
-            peer = lax.rem(h + turn, 2) * 4 + lax.rem(x + step, 4)
-            ref[turn] = partials[peer].astype(ref.dtype)
+    for low, ref in enumerate((mine_ref, theirs_ref)):
+        for high in range(2):
+            for row in range(2):
+                peer = jnp.bitwise_xor(h, row) * 4 + jnp.bitwise_xor(x, 2 * high + low)
+                ref[2 * high + row] = partials[peer].astype(ref.dtype)
 
 
 def partial_rows(keep, got, down, peers):
     slots, depth = keep.shape[0] // peers, down.shape[0]
     return pl.pallas_call(
         partial_kernel,
-        out_shape=(jax.ShapeDtypeStruct((2, slots, depth), jnp.bfloat16),) * 4,
+        out_shape=(
+            jax.ShapeDtypeStruct((peers // 2, slots, depth), jnp.float32),
+            jax.ShapeDtypeStruct((peers // 2, slots, depth), jnp.bfloat16),
+        ),
         in_specs=whole(3),
-        out_specs=tuple(whole(4)),
+        out_specs=tuple(whole(2)),
         scratch_shapes=[pltpu.VMEM((peers, slots, depth), jnp.float32)],
         compiler_params=params(8),
         name="partial_rows",
     )(keep, got, down)
 
 
-def add_kernel(own_ref, *refs):
-    total = own_ref[...].astype(jnp.float32)
-    for ref in refs[:3]:
-        total += ref[...].astype(jnp.float32)
-    for k, ref in enumerate(refs[3:]):
-        ref[...] = total[k].astype(ref.dtype)
-
-
-def add_turns(parts):
-    turns, slots, depth = parts[0].shape
+def add_kernel(keep_ref, got_ref, mine_ref, theirs_ref):
+    half = mine_ref.shape[0]
+    mine_ref[...] = keep_ref[:half] + got_ref[:half].astype(jnp.float32)
+    theirs_ref[...] = (keep_ref[half:] + got_ref[half:].astype(jnp.float32)).astype(jnp.bfloat16)
+
+
+def add_halves(keep, got):
+    half = (keep.shape[0] // 2, *keep.shape[1:])
     return pl.pallas_call(
         add_kernel,
-        out_shape=(jax.ShapeDtypeStruct((slots, depth), jnp.bfloat16),) * turns,
-        in_specs=whole(4),
-        out_specs=tuple(whole(turns)),
+        out_shape=(
+            jax.ShapeDtypeStruct(half, jnp.float32),
+            jax.ShapeDtypeStruct(half, jnp.bfloat16),
+        ),
+        in_specs=whole(2),
+        out_specs=tuple(whole(2)),
         compiler_params=params(8),
-        name="add_turns",
-    )(*parts)
+        name="add_halves",
+    )(keep, got)
 
 
 def mix_kernel(own_ref, got_ref, chooser_ref, slot_weight_ref, mixed_ref):
-    total = own_ref[...].astype(jnp.float32) + got_ref[...].astype(jnp.float32)
+    total = own_ref[0] + got_ref[0].astype(jnp.float32)
     weighted = (total * slot_weight_ref[:, :1]).astype(jnp.bfloat16)
     mixed_ref[...] = lax.dot_general(
         chooser_ref[...], weighted, ROW_DIMS, preferred_element_type=jnp.float32
@@ -288,7 +294,7 @@
 def mix(own, got, chooser, slot_weight):
     return pl.pallas_call(
         mix_kernel,
-        out_shape=jax.ShapeDtypeStruct((chooser.shape[1], own.shape[1]), jnp.bfloat16),
+        out_shape=jax.ShapeDtypeStruct((chooser.shape[1], own.shape[2]), jnp.bfloat16),
         in_specs=whole(4),
         out_specs=whole(1)[0],
         compiler_params=params(8),
@@ -325,44 +331,43 @@
     )(blocks)
 
 
-def spread(parts, axis):
-    came = [
-        lax.ppermute(part, axis, [(i, (i + k) % 4) for i in range(4)])
-        for k, part in enumerate(parts)
-        if k
-    ]
-    return [parts[0], *came]
+def swapped(part, axis, distance=1):
+    size = lax.axis_size(axis)
+    return lax.ppermute(part, axis, [(i, i ^ distance) for i in range(size)])
 
 
 def per_device(tokens, cotangent, expert_ids, route_weights, join_groups, w_gate, w_up, w_down):
-    chips = lax.axis_size("z")
     own = jnp.stack([w_gate, w_up, w_down])
-    got = lax.ppermute(own, "y", SWAP)
+    got = swapped(own, "y")
     copies, chooser, slot_weight = route(
         expert_ids, route_weights, tokens, cotangent, lax.axis_size(PLANE)
     )
     packed = pack_shards(own, got)
     packed, copies = lax.optimization_barrier((packed, copies))
     rows_in = lax.all_to_all(copies, PLANE, 0, 0, tiled=True)
-    along = lax.all_gather(packed, "z", axis=0, tiled=False)
-    other = lax.ppermute(along, "c", SWAP)
+    along = lax.all_gather(packed, Z, axis=0, tiled=False)
+    along, rows_in = lax.optimization_barrier((along, rows_in))
+    other = swapped(along, "c")
     hidden_send, hidden, down, send, keep = expert(join_groups, rows_in, along, other)
-    from_core = lax.ppermute(send, "c", SWAP)
-    hidden_got = lax.ppermute(hidden_send, "y", SWAP)
-    chip_sum = (keep + from_core.astype(jnp.float32)).astype(jnp.bfloat16)
-    chip_sum = chip_sum.reshape(chips * 2, *chip_sum.shape[2:])
-    chip_sum, hidden_got = lax.optimization_barrier((chip_sum, hidden_got))
-    pieces = lax.all_to_all(chip_sum, ("z", "y"), 0, 0, tiled=True)
-    partials = partial_rows(hidden, hidden_got, down, lax.axis_size(("h", "x")))
-    mine, theirs = add_turns(spread(partials, "x"))
-    mixed = mix(mine, lax.ppermute(theirs, "h", SWAP), chooser, slot_weight)
+    from_core = swapped(send, "c")
+    hidden_got = swapped(hidden_send, "y")
+    keep, to_pair = add_halves(keep, from_core)
+    from_pair = swapped(to_pair, "zl")
+    partial, partial_send = partial_rows(hidden, hidden_got, down, lax.axis_size(("h", "x")))
+    pair_sum = (keep + from_pair.astype(jnp.float32)).astype(jnp.bfloat16)
+    pair_sum = pair_sum.reshape(-1, *pair_sum.shape[3:])
+    pair_sum, partial_send = lax.optimization_barrier((pair_sum, partial_send))
+    pieces = lax.all_to_all(pair_sum, ("zh", "y"), 0, 0, tiled=True)
+    partial, partial_send = add_halves(partial, swapped(partial_send, "x"))
+    partial, partial_send = add_halves(partial, swapped(partial_send, "x", 2))
+    mixed = mix(partial, swapped(partial_send, "h"), chooser, slot_weight)
     return (mixed, *finish(pieces))
 
 
 def solution(mesh):
     experts = mesh.shape["expert"]
-    split = Mesh(mesh.devices.reshape(-1, 2, 2, 2, experts // 2), AXES)
-    dp = ("z", "y", "c")
+    split = Mesh(mesh.devices.reshape(-1, 2, 2, 2, 2, experts // 2), AXES)
+    dp = ("zh", "zl", "y", "c")
     tok, weight = P(AXES, None), P(dp, ("h", "x"))
     return jax.shard_map(
         per_device,

time: 106 us -> 108 us (1.019)
  waiting for transfers between devices: 15.5 us -> 20.9 us
  local copies, waits for them, and re-layouts: 1.85 us -> 0.02 us
    ppermute x8, waiting for transfers between devices: 12.8 us -> 20.9 us  [swapped(): return lax.ppermute(part, axis, [(i, i ^ distance) for i in range(size)])]
    all_to_all x1, waiting for transfers between devices: 2.69 us -> 0.01 us  [per_device(): pieces = lax.all_to_all(pair_sum, ('zh', 'y'), 0, 0, tiled=True)]
    unnamed x10 -> x6, local copies, waits for them, and re-layouts: 1.85 us -> 0.02 us
  transfers between devices with their start and end apart: 10 -> 10, of which waited for: 6 -> 7; matrix products, arithmetic and copies ran while one was open for 1% -> 0% of each run, Pallas kernels for 4% -> 4%
where the time goes in v5:
time: 108 us
  starting transfers between devices  40 us (37%)
  blocking collectives  36.7 us (34%)
  waiting for transfers between devices  20.9 us (19%)
  Pallas kernels  7.64 us (7%)
  other arithmetic  1.44 us (1%)
    all_gather x1, blocking collectives, per_device(): along = lax.all_gather(packed, Z, axis=0, tiled=False)  36.7 us
    ppermute x8, starting transfers between devices, swapped(): return lax.ppermute(part, axis, [(i, i ^ distance) for i in range(size)])  23.4 us
    ppermute x8, waiting for transfers between devices, swapped(): return lax.ppermute(part, axis, [(i, i ^ distance) for i in range(size)])  20.9 us
    all_to_all x1, starting transfers between devices, per_device(): rows_in = lax.all_to_all(copies, PLANE, 0, 0, tiled=True)  8.71 us
    all_to_all x1, starting transfers between devices, per_device(): pieces = lax.all_to_all(pair_sum, ('zh', 'y'), 0, 0, tiled=True)  7.91 us
    pallas_call x1, Pallas kernels, route(): pl.pallas_call(route_kernel, out_shape=(jax.ShapeDtypeStruct((peers, 2 *...  2.88 us
    pallas_call x1, Pallas kernels, expert(): pl.pallas_call(expert_kernel, out_shape=(hidden, hidden, jax.ShapeDtypeSt...  2.35 us
  transfers between devices with their start and end apart: 10, of which 7 were waited for; matrix products, arithmetic and copies ran while one was open for 0% of the time, Pallas kernels for 4%

profile of v5, /device:TPU:6, one launch (start us, length us, event | category | flops | bytes accessed | tf_op | source)
XLA Modules:
  0.0 107.5 jit_solution(9219996847305380157)
XLA Ops:
  0.6 0.7 pad_maximum_fusion.own_ref
  1.4 3.5 %collective-permute-start = (bf16[3,32,128]{2,1,0:T(8,128)(2,1)S(1)}, bf16[3,32,128]{2,1,0:T(8,128)(2,1)S(1)}, u32[]{:S(2)}, u32[]{:S(2)}) collective-permute-start(bf16[3,32,128]{2,1,0:T(8,128)(2,1)S(1)} %pad_maximum_fusion.own_ref), channel_id=1, source_target_pairs={{0,16},{16,0},{1,17},{17,1},{2,18},{18,2},{3,19},{19,3},{4,20},{20... | collective-permute-start | bytes 73736 | tf_op jit(solution)/shard_map/ppermute | solution.py:336
  4.8 2.9 %route.1 = (bf16[16,32,2048]{2,1,0:T(8,128)(2,1)}, bf16[16,128]{1,0:T(8,128)(2,1)}, f32[16,128]{1,0:T(8,128)}) custom-call(s32[8,128]{1,0:T(8,128)} %bitcast.12, f32[8,128]{1,0:T(8,128)} %bitcast.13, bf16[128,2048]{1,0:T(8,128)(2,1)} %tokens_ref.1, bf16[128,2048]{1,0:T(8,128)(2,1)} %cot_ref.1), custom_call_target="tpu_custom_call" | custom-call | tf_op jit(solution)/shard_map/route/pallas_call | solution.py:94
  7.7 0.0 collective-permute-done.got_ref
  7.7 0.1 pack_shards.1
  7.8 0.0 copy-start.2
  7.8 8.7 %all-to-all-start = ((bf16[16,32,2048]{2,1,0:T(8,128)(2,1)}), bf16[16,32,2048]{2,1,0:T(8,128)(2,1)S(1)}, u32[]{:S(2)}, u32[]{:S(2)}) async-start(bf16[16,32,2048]{2,1,0:T(8,128)(2,1)} %get-tuple-element.31), calls=%async_computation | async-start | bytes 4194304 | tf_op jit(solution)/shard_map/all_to_all | solution.py:347
  16.6 36.7 %all-gather = bf16[2048,128]{1,0:T(8,128)(2,1)S(1)} all-gather(bf16[128,128]{1,0:T(8,128)(2,1)S(1)} %pack_shards.1), channel_id=2, replica_groups=mesh['zh'=8,'zl'=2,'y'=2,'c'=2,'h'=2,'x'=4] {'zh','zl'}, dimensions={0}, use_global_device_ids=true | all-gather | bytes 557056 | tf_op jit(solution)/shard_map/all_gather | solution.py:348
  53.3 0.0 all-to-all-done.both_ref
  53.3 1.9 %collective-permute-start.1 = (bf16[16,128,128]{2,1,0:T(8,128)(2,1)S(1)}, bf16[16,128,128]{2,1,0:T(8,128)(2,1)S(1)}, u32[]{:S(2)}, u32[]{:S(2)}) collective-permute-start(bf16[16,128,128]{2,1,0:T(8,128)(2,1)S(1)} %bitcast.7), channel_id=1, source_target_pairs={{0,8},{8,0},{1,9},{9,1},{2,10},{10,2},{3,11},{11,3},{4,12},{12,4},... | collective-permute-start | bytes 1572872 | tf_op jit(solution)/shard_map/ppermute | solution.py:336
  55.2 1.9 %collective-permute-done.1.got_ref = bf16[16,128,128]{2,1,0:T(8,128)(2,1)S(1)} collective-permute-done((bf16[16,128,128]{2,1,0:T(8,128)(2,1)S(1)}, bf16[16,128,128]{2,1,0:T(8,128)(2,1)S(1)}, u32[]{:S(2)}, u32[]{:S(2)}) %collective-permute-start.1) | collective-permute-done | bytes 524320 | tf_op jit(solution)/shard_map/ppermute | solution.py:336
  57.1 0.0 copy-done.2
  57.1 2.3 %expert.1 = (bf16[128,128]{1,0:T(8,128)(2,1)S(1)}, bf16[128,128]{1,0:T(8,128)(2,1)S(1)}, bf16[2048,128]{1,0:T(8,128)(2,1)S(1)}, bf16[2,8,2,48,128]{4,3,2,1,0:T(8,128)(2,1)S(1)}, f32[2,8,2,48,128]{4,3,2,1,0:T(8,128)S(1)}) custom-call(s32[64]{0:T(128)S(1)} %copy-done.2, bf16[16,32,2048]{2,1,0:T(8,128)(2,1)S(1)} %all-to-all-done.both_ref, ...), custom_call_target="tpu_custom_call" | custom-call | tf_op jit(solution)/shard_map/expert/pallas_call | solution.py:215
  59.5 0.0 copy-start
  59.5 0.0 copy-start.1
  59.5 2.0 %collective-permute-start.3 = (bf16[2,8,2,48,128]{4,3,2,1,0:T(8,128)(2,1)S(1)}, bf16[2,8,2,48,128]{4,3,2,1,0:T(8,128)(2,1)S(1)}, u32[]{:S(2)}, u32[]{:S(2)}) collective-permute-start(bf16[2,8,2,48,128]{4,3,2,1,0:T(8,128)(2,1)S(1)} %get-tuple-element.39), channel_id=1, source_target_pairs={{0,8},{8,0},{1,9},{9,1},{2,10},{10,2},{3,11},{11,3},{4,12},{12,4},... | collective-permute-start | bytes 1179656 | tf_op jit(solution)/shard_map/ppermute | solution.py:336
  61.5 1.6 %collective-permute-done.3.got_ref = bf16[2,8,2,48,128]{4,3,2,1,0:T(8,128)(2,1)S(1)} collective-permute-done((bf16[2,8,2,48,128]{4,3,2,1,0:T(8,128)(2,1)S(1)}, bf16[2,8,2,48,128]{4,3,2,1,0:T(8,128)(2,1)S(1)}, u32[]{:S(2)}, u32[]{:S(2)}) %collective-permute-start.3) | collective-permute-done | bytes 393248 | tf_op jit(solution)/shard_map/ppermute | solution.py:336
  63.1 0.1 add_halves.3
  63.2 1.9 %collective-permute-start.4 = (bf16[1,8,2,48,128]{4,3,2,1,0:T(8,128)(2,1)S(1)}, bf16[1,8,2,48,128]{4,3,2,1,0:T(8,128)(2,1)S(1)}, u32[]{:S(2)}, u32[]{:S(2)}) collective-permute-start(bf16[1,8,2,48,128]{4,3,2,1,0:T(8,128)(2,1)S(1)} %get-tuple-element.41), channel_id=1, source_target_pairs={{0,32},{32,0},{1,33},{33,1},{2,34},{34,2},{3,35},{35,3},{4,36},{36... | collective-permute-start | bytes 589832 | tf_op jit(solution)/shard_map/ppermute | solution.py:336
  65.1 3.4 %collective-permute-start.2 = (bf16[128,128]{1,0:T(8,128)(2,1)S(1)}, bf16[128,128]{1,0:T(8,128)(2,1)S(1)}, u32[]{:S(2)}, u32[]{:S(2)}) collective-permute-start(bf16[128,128]{1,0:T(8,128)(2,1)S(1)} %get-tuple-element.35), channel_id=1, source_target_pairs={{0,16},{16,0},{1,17},{17,1},{2,18},{18,2},{3,19},{19,3},{4,20},{20... | collective-permute-start | bytes 98312 | tf_op jit(solution)/shard_map/ppermute | solution.py:336
  68.5 2.4 %collective-permute-done.2.got_ref = bf16[128,128]{1,0:T(8,128)(2,1)S(1)} collective-permute-done((bf16[128,128]{1,0:T(8,128)(2,1)S(1)}, bf16[128,128]{1,0:T(8,128)(2,1)S(1)}, u32[]{:S(2)}, u32[]{:S(2)}) %collective-permute-start.2) | collective-permute-done | bytes 32800 | tf_op jit(solution)/shard_map/ppermute | solution.py:336
  70.9 0.4 partial_rows.1
  71.3 0.7 collective-permute-done.4
  72.0 0.7 add_convert_fusion
  72.7 7.9 %all-to-all-start.1 = ((bf16[16,48,128]{2,1,0:T(8,128)(2,1)}), bf16[16,48,128]{2,1,0:T(8,128)(2,1)S(1)}, u32[]{:S(2)}, u32[]{:S(2)}) async-start(bf16[16,48,128]{2,1,0:T(8,128)(2,1)} %bitcast.6), calls=%async_computation.1 | async-start | bytes 393216 | tf_op jit(solution)/shard_map/all_to_all | solution.py:360
  80.6 2.8 %collective-permute-start.5 = (bf16[4,16,2048]{2,1,0:T(8,128)(2,1)S(1)}, bf16[4,16,2048]{2,1,0:T(8,128)(2,1)S(1)}, u32[]{:S(2)}, u32[]{:S(2)}) collective-permute-start(bf16[4,16,2048]{2,1,0:T(8,128)(2,1)S(1)} %get-tuple-element.43), channel_id=1, source_target_pairs={{0,1},{1,0},{2,3},{3,2},{4,5},{5,4},{6,7},{7,6},{8,9},{9,8},{10,11... | collective-permute-start | bytes 786440 | tf_op jit(solution)/shard_map/ppermute | solution.py:336
  83.4 6.2 %collective-permute-done.5.got_ref = bf16[4,16,2048]{2,1,0:T(8,128)(2,1)S(1)} collective-permute-done((bf16[4,16,2048]{2,1,0:T(8,128)(2,1)S(1)}, bf16[4,16,2048]{2,1,0:T(8,128)(2,1)S(1)}, u32[]{:S(2)}, u32[]{:S(2)}) %collective-permute-start.5) | collective-permute-done | bytes 262176 | tf_op jit(solution)/shard_map/ppermute | solution.py:336
  89.6 0.1 add_halves.4
  89.6 3.3 %collective-permute-start.6 = (bf16[2,16,2048]{2,1,0:T(8,128)(2,1)S(1)}, bf16[2,16,2048]{2,1,0:T(8,128)(2,1)S(1)}, u32[]{:S(2)}, u32[]{:S(2)}) collective-permute-start(bf16[2,16,2048]{2,1,0:T(8,128)(2,1)S(1)} %get-tuple-element.45), channel_id=1, source_target_pairs={{0,2},{1,3},{2,0},{3,1},{4,6},{5,7},{6,4},{7,5},{8,10},{9,11},{10,... | collective-permute-start | bytes 393224 | tf_op jit(solution)/shard_map/ppermute | solution.py:336
  93.0 5.1 %collective-permute-done.6.got_ref = bf16[2,16,2048]{2,1,0:T(8,128)(2,1)S(1)} collective-permute-done((bf16[2,16,2048]{2,1,0:T(8,128)(2,1)S(1)}, bf16[2,16,2048]{2,1,0:T(8,128)(2,1)S(1)}, u32[]{:S(2)}, u32[]{:S(2)}) %collective-permute-start.6) | collective-permute-done | bytes 131104 | tf_op jit(solution)/shard_map/ppermute | solution.py:336
  98.0 4.6 %collective-permute-start.7 = (bf16[1,16,2048]{2,1,0:T(8,128)(2,1)S(1)}, bf16[1,16,2048]{2,1,0:T(8,128)(2,1)S(1)}, u32[]{:S(2)}, u32[]{:S(2)}) collective-permute-start(bf16[1,16,2048]{2,1,0:T(8,128)(2,1)S(1)} %get-tuple-element.47), channel_id=1, source_target_pairs={{0,4},{4,0},{1,5},{5,1},{2,6},{6,2},{3,7},{7,3},{8,12},{12,8},{9,1... | collective-permute-start | bytes 196616 | tf_op jit(solution)/shard_map/ppermute | solution.py:336
  102.6 3.1 %collective-permute-done.7.got_ref = bf16[1,16,2048]{2,1,0:T(8,128)(2,1)S(1)} collective-permute-done((bf16[1,16,2048]{2,1,0:T(8,128)(2,1)S(1)}, bf16[1,16,2048]{2,1,0:T(8,128)(2,1)S(1)}, u32[]{:S(2)}, u32[]{:S(2)}) %collective-permute-start.7) | collective-permute-done | bytes 65568 | tf_op jit(solution)/shard_map/ppermute | solution.py:336
  105.7 0.0 copy-done
  105.7 0.0 copy-done.1
  105.7 1.1 %mix.1 = bf16[128,2048]{1,0:T(8,128)(2,1)} custom-call(f32[1,16,2048]{2,1,0:T(8,128)S(1)} %get-tuple-element.46.own_ref, bf16[1,16,2048]{2,1,0:T(8,128)(2,1)S(1)} %collective-permute-done.7.got_ref, bf16[16,128]{1,0:T(8,128)(2,1)S(1)} %copy-done.1, f32[16,128]{1,0:T(8,128)S(1)} %copy-done), custom_call_target="tpu_custom_call" | custom-call | tf_op jit(solution)/shard_map/mix/pallas_call | solution.py:295
  106.8 0.0 all-to-all-done.1.blocks_ref
  106.8 0.7 finish.1
  (1 shorter events, 0.0 us)
Async XLA Ops:
  1.4 6.4 %collective-permute-start = (bf16[3,32,128]{2,1,0:T(8,128)(2,1)S(1)}, bf16[3,32,128]{2,1,0:T(8,128)(2,1)S(1)}, u32[]{:S(2)}, u32[]{:S(2)}) collective-permute-start(bf16[3,32,128]{2,1,0:T(8,128)(2,1)S(1)} %pad_maximum_fusion.own_ref), channel_id=1, source_target_pairs={{0,16},{16,0},{1,17},{17,1},{2,18},{18,2},{3,19},{19,3},{4,20},{20... | collective-permute-start | bytes 73736 | tf_op jit(solution)/shard_map/ppermute | solution.py:336
  7.8 49.3 %copy-start.2 = (s32[64]{0:T(128)S(1)}, s32[64]{0:T(128)}, u32[]{:S(2)}) copy-start(s32[64]{0:T(128)} %join_ref.1) | copy-start | bytes 772
  7.8 45.5 %all-to-all-start = ((bf16[16,32,2048]{2,1,0:T(8,128)(2,1)}), bf16[16,32,2048]{2,1,0:T(8,128)(2,1)S(1)}, u32[]{:S(2)}, u32[]{:S(2)}) async-start(bf16[16,32,2048]{2,1,0:T(8,128)(2,1)} %get-tuple-element.31), calls=%async_computation | async-start | bytes 4194304 | tf_op jit(solution)/shard_map/all_to_all | solution.py:347
  53.3 3.8 %collective-permute-start.1 = (bf16[16,128,128]{2,1,0:T(8,128)(2,1)S(1)}, bf16[16,128,128]{2,1,0:T(8,128)(2,1)S(1)}, u32[]{:S(2)}, u32[]{:S(2)}) collective-permute-start(bf16[16,128,128]{2,1,0:T(8,128)(2,1)S(1)} %bitcast.7), channel_id=1, source_target_pairs={{0,8},{8,0},{1,9},{9,1},{2,10},{10,2},{3,11},{11,3},{4,12},{12,4},... | collective-permute-start | bytes 1572872 | tf_op jit(solution)/shard_map/ppermute | solution.py:336
  59.5 46.2 %copy-start = (f32[16,128]{1,0:T(8,128)S(1)}, f32[16,128]{1,0:T(8,128)}, u32[]{:S(2)}) copy-start(f32[16,128]{1,0:T(8,128)} %get-tuple-element.49.slot_weight_ref) | copy-start | bytes 24580
  59.5 46.2 %copy-start.1 = (bf16[16,128]{1,0:T(8,128)(2,1)S(1)}, bf16[16,128]{1,0:T(8,128)(2,1)}, u32[]{:S(2)}) copy-start(bf16[16,128]{1,0:T(8,128)(2,1)} %get-tuple-element.48.chooser_ref) | copy-start | bytes 12292
  59.5 3.6 %collective-permute-start.3 = (bf16[2,8,2,48,128]{4,3,2,1,0:T(8,128)(2,1)S(1)}, bf16[2,8,2,48,128]{4,3,2,1,0:T(8,128)(2,1)S(1)}, u32[]{:S(2)}, u32[]{:S(2)}) collective-permute-start(bf16[2,8,2,48,128]{4,3,2,1,0:T(8,128)(2,1)S(1)} %get-tuple-element.39), channel_id=1, source_target_pairs={{0,8},{8,0},{1,9},{9,1},{2,10},{10,2},{3,11},{11,3},{4,12},{12,4},... | collective-permute-start | bytes 1179656 | tf_op jit(solution)/shard_map/ppermute | solution.py:336
  63.2 8.8 %collective-permute-start.4 = (bf16[1,8,2,48,128]{4,3,2,1,0:T(8,128)(2,1)S(1)}, bf16[1,8,2,48,128]{4,3,2,1,0:T(8,128)(2,1)S(1)}, u32[]{:S(2)}, u32[]{:S(2)}) collective-permute-start(bf16[1,8,2,48,128]{4,3,2,1,0:T(8,128)(2,1)S(1)} %get-tuple-element.41), channel_id=1, source_target_pairs={{0,32},{32,0},{1,33},{33,1},{2,34},{34,2},{3,35},{35,3},{4,36},{36... | collective-permute-start | bytes 589832 | tf_op jit(solution)/shard_map/ppermute | solution.py:336
  65.1 5.8 %collective-permute-start.2 = (bf16[128,128]{1,0:T(8,128)(2,1)S(1)}, bf16[128,128]{1,0:T(8,128)(2,1)S(1)}, u32[]{:S(2)}, u32[]{:S(2)}) collective-permute-start(bf16[128,128]{1,0:T(8,128)(2,1)S(1)} %get-tuple-element.35), channel_id=1, source_target_pairs={{0,16},{16,0},{1,17},{17,1},{2,18},{18,2},{3,19},{19,3},{4,20},{20... | collective-permute-start | bytes 98312 | tf_op jit(solution)/shard_map/ppermute | solution.py:336
  72.7 34.1 %all-to-all-start.1 = ((bf16[16,48,128]{2,1,0:T(8,128)(2,1)}), bf16[16,48,128]{2,1,0:T(8,128)(2,1)S(1)}, u32[]{:S(2)}, u32[]{:S(2)}) async-start(bf16[16,48,128]{2,1,0:T(8,128)(2,1)} %bitcast.6), calls=%async_computation.1 | async-start | bytes 393216 | tf_op jit(solution)/shard_map/all_to_all | solution.py:360
  80.6 9.0 %collective-permute-start.5 = (bf16[4,16,2048]{2,1,0:T(8,128)(2,1)S(1)}, bf16[4,16,2048]{2,1,0:T(8,128)(2,1)S(1)}, u32[]{:S(2)}, u32[]{:S(2)}) collective-permute-start(bf16[4,16,2048]{2,1,0:T(8,128)(2,1)S(1)} %get-tuple-element.43), channel_id=1, source_target_pairs={{0,1},{1,0},{2,3},{3,2},{4,5},{5,4},{6,7},{7,6},{8,9},{9,8},{10,11... | collective-permute-start | bytes 786440 | tf_op jit(solution)/shard_map/ppermute | solution.py:336
  89.6 8.4 %collective-permute-start.6 = (bf16[2,16,2048]{2,1,0:T(8,128)(2,1)S(1)}, bf16[2,16,2048]{2,1,0:T(8,128)(2,1)S(1)}, u32[]{:S(2)}, u32[]{:S(2)}) collective-permute-start(bf16[2,16,2048]{2,1,0:T(8,128)(2,1)S(1)} %get-tuple-element.45), channel_id=1, source_target_pairs={{0,2},{1,3},{2,0},{3,1},{4,6},{5,7},{6,4},{7,5},{8,10},{9,11},{10,... | collective-permute-start | bytes 393224 | tf_op jit(solution)/shard_map/ppermute | solution.py:336
  98.0 7.7 %collective-permute-start.7 = (bf16[1,16,2048]{2,1,0:T(8,128)(2,1)S(1)}, bf16[1,16,2048]{2,1,0:T(8,128)(2,1)S(1)}, u32[]{:S(2)}, u32[]{:S(2)}) collective-permute-start(bf16[1,16,2048]{2,1,0:T(8,128)(2,1)S(1)} %get-tuple-element.47), channel_id=1, source_target_pairs={{0,4},{4,0},{1,5},{5,1},{2,6},{6,2},{3,7},{7,3},{8,12},{12,8},{9,1... | collective-permute-start | bytes 196616 | tf_op jit(solution)/shard_map/ppermute | solution.py:336

commit v6 on v5

--- a/solution.py
+++ b/solution.py
@@ -349,16 +349,18 @@
     along, rows_in = lax.optimization_barrier((along, rows_in))
     other = swapped(along, "c")
     hidden_send, hidden, down, send, keep = expert(join_groups, rows_in, along, other)
+    hidden_got = swapped(hidden_send, "y")
     from_core = swapped(send, "c")
-    hidden_got = swapped(hidden_send, "y")
+    partial, partial_send = partial_rows(hidden, hidden_got, down, lax.axis_size(("h", "x")))
+    from_core, partial_send = lax.optimization_barrier((from_core, partial_send))
+    partial_got = swapped(partial_send, "x")
     keep, to_pair = add_halves(keep, from_core)
     from_pair = swapped(to_pair, "zl")
-    partial, partial_send = partial_rows(hidden, hidden_got, down, lax.axis_size(("h", "x")))
     pair_sum = (keep + from_pair.astype(jnp.float32)).astype(jnp.bfloat16)
     pair_sum = pair_sum.reshape(-1, *pair_sum.shape[3:])
-    pair_sum, partial_send = lax.optimization_barrier((pair_sum, partial_send))
+    pair_sum, partial_got = lax.optimization_barrier((pair_sum, partial_got))
     pieces = lax.all_to_all(pair_sum, ("zh", "y"), 0, 0, tiled=True)
-    partial, partial_send = add_halves(partial, swapped(partial_send, "x"))
+    partial, partial_send = add_halves(partial, partial_got)
     partial, partial_send = add_halves(partial, swapped(partial_send, "x", 2))
     mixed = mix(partial, swapped(partial_send, "h"), chooser, slot_weight)
     return (mixed, *finish(pieces))

time: 108 us -> 107 us (level); the launches traced: 108 us -> 105 us
  waiting for transfers between devices: 20.9 us -> 18.2 us
    ppermute x8, waiting for transfers between devices: 20.9 us -> 18.2 us  [swapped(): return lax.ppermute(part, axis, [(i, i ^ distance) for i in range(size)])]
  transfers between devices with their start and end apart: 10 -> 10, of which waited for: 7 -> 6; matrix products, arithmetic and copies ran while one was open for 0% -> 1% of each run, Pallas kernels for 4% -> 4%
where the time goes in v6:
time: 107 us; the launch traced here: 105 us
  starting transfers between devices  40.5 us (38%)
  blocking collectives  36.7 us (34%)
  waiting for transfers between devices  18.2 us (17%)
  Pallas kernels  7.63 us (7%)
  other arithmetic  1.44 us (1%)
    all_gather x1, blocking collectives, per_device(): along = lax.all_gather(packed, Z, axis=0, tiled=False)  36.7 us
    ppermute x8, starting transfers between devices, swapped(): return lax.ppermute(part, axis, [(i, i ^ distance) for i in range(size)])  23.5 us
    ppermute x8, waiting for transfers between devices, swapped(): return lax.ppermute(part, axis, [(i, i ^ distance) for i in range(size)])  18.2 us
    all_to_all x1, starting transfers between devices, per_device(): rows_in = lax.all_to_all(copies, PLANE, 0, 0, tiled=True)  8.71 us
    all_to_all x1, starting transfers between devices, per_device(): pieces = lax.all_to_all(pair_sum, ('zh', 'y'), 0, 0, tiled=True)  8.35 us
    pallas_call x1, Pallas kernels, route(): pl.pallas_call(route_kernel, out_shape=(jax.ShapeDtypeStruct((peers, 2 *...  2.88 us
    pallas_call x1, Pallas kernels, expert(): pl.pallas_call(expert_kernel, out_shape=(hidden, hidden, jax.ShapeDtypeSt...  2.34 us
  transfers between devices with their start and end apart: 10, of which 6 were waited for; matrix products, arithmetic and copies ran while one was open for 1% of the time, Pallas kernels for 4%

profile of v6, /device:TPU:6, one launch (start us, length us, event | category | flops | bytes accessed | tf_op | source)
XLA Modules:
  0.0 105.3 jit_solution(423158874303861727)
XLA Ops:
  0.6 0.7 pad_maximum_fusion.own_ref
  1.4 3.5 %collective-permute-start = (bf16[3,32,128]{2,1,0:T(8,128)(2,1)S(1)}, bf16[3,32,128]{2,1,0:T(8,128)(2,1)S(1)}, u32[]{:S(2)}, u32[]{:S(2)}) collective-permute-start(bf16[3,32,128]{2,1,0:T(8,128)(2,1)S(1)} %pad_maximum_fusion.own_ref), channel_id=1, source_target_pairs={{0,16},{16,0},{1,17},{17,1},{2,18},{18,2},{3,19},{19,3},{4,20},{20... | collective-permute-start | bytes 73736 | tf_op jit(solution)/shard_map/ppermute | solution.py:336
  4.8 2.9 %route.1 = (bf16[16,32,2048]{2,1,0:T(8,128)(2,1)}, bf16[16,128]{1,0:T(8,128)(2,1)}, f32[16,128]{1,0:T(8,128)}) custom-call(s32[8,128]{1,0:T(8,128)} %bitcast.12, f32[8,128]{1,0:T(8,128)} %bitcast.13, bf16[128,2048]{1,0:T(8,128)(2,1)} %tokens_ref.1, bf16[128,2048]{1,0:T(8,128)(2,1)} %cot_ref.1), custom_call_target="tpu_custom_call" | custom-call | tf_op jit(solution)/shard_map/route/pallas_call | solution.py:94
  7.7 0.0 collective-permute-done.got_ref
  7.7 0.1 pack_shards.1
  7.8 0.0 copy-start.2
  7.8 8.7 %all-to-all-start = ((bf16[16,32,2048]{2,1,0:T(8,128)(2,1)}), bf16[16,32,2048]{2,1,0:T(8,128)(2,1)S(1)}, u32[]{:S(2)}, u32[]{:S(2)}) async-start(bf16[16,32,2048]{2,1,0:T(8,128)(2,1)} %get-tuple-element.33), calls=%async_computation | async-start | bytes 4194304 | tf_op jit(solution)/shard_map/all_to_all | solution.py:347
  16.6 36.7 %all-gather = bf16[2048,128]{1,0:T(8,128)(2,1)S(1)} all-gather(bf16[128,128]{1,0:T(8,128)(2,1)S(1)} %pack_shards.1), channel_id=2, replica_groups=mesh['zh'=8,'zl'=2,'y'=2,'c'=2,'h'=2,'x'=4] {'zh','zl'}, dimensions={0}, use_global_device_ids=true | all-gather | bytes 557056 | tf_op jit(solution)/shard_map/all_gather | solution.py:348
  53.3 0.0 all-to-all-done.both_ref
  53.3 1.9 %collective-permute-start.1 = (bf16[16,128,128]{2,1,0:T(8,128)(2,1)S(1)}, bf16[16,128,128]{2,1,0:T(8,128)(2,1)S(1)}, u32[]{:S(2)}, u32[]{:S(2)}) collective-permute-start(bf16[16,128,128]{2,1,0:T(8,128)(2,1)S(1)} %bitcast.7), channel_id=1, source_target_pairs={{0,8},{8,0},{1,9},{9,1},{2,10},{10,2},{3,11},{11,3},{4,12},{12,4},... | collective-permute-start | bytes 1572872 | tf_op jit(solution)/shard_map/ppermute | solution.py:336
  55.2 1.9 %collective-permute-done.1.got_ref = bf16[16,128,128]{2,1,0:T(8,128)(2,1)S(1)} collective-permute-done((bf16[16,128,128]{2,1,0:T(8,128)(2,1)S(1)}, bf16[16,128,128]{2,1,0:T(8,128)(2,1)S(1)}, u32[]{:S(2)}, u32[]{:S(2)}) %collective-permute-start.1) | collective-permute-done | bytes 524320 | tf_op jit(solution)/shard_map/ppermute | solution.py:336
  57.1 0.0 copy-done.2
  57.1 2.3 %expert.1 = (bf16[128,128]{1,0:T(8,128)(2,1)S(1)}, bf16[128,128]{1,0:T(8,128)(2,1)S(1)}, bf16[2048,128]{1,0:T(8,128)(2,1)S(1)}, bf16[2,8,2,48,128]{4,3,2,1,0:T(8,128)(2,1)S(1)}, f32[2,8,2,48,128]{4,3,2,1,0:T(8,128)S(1)}) custom-call(s32[64]{0:T(128)S(1)} %copy-done.2, bf16[16,32,2048]{2,1,0:T(8,128)(2,1)S(1)} %all-to-all-done.both_ref, ...), custom_call_target="tpu_custom_call" | custom-call | tf_op jit(solution)/shard_map/expert/pallas_call | solution.py:215
  59.4 0.0 copy-start
  59.5 0.0 copy-start.1
  59.5 2.0 %collective-permute-start.3 = (bf16[2,8,2,48,128]{4,3,2,1,0:T(8,128)(2,1)S(1)}, bf16[2,8,2,48,128]{4,3,2,1,0:T(8,128)(2,1)S(1)}, u32[]{:S(2)}, u32[]{:S(2)}) collective-permute-start(bf16[2,8,2,48,128]{4,3,2,1,0:T(8,128)(2,1)S(1)} %get-tuple-element.41), channel_id=1, source_target_pairs={{0,8},{8,0},{1,9},{9,1},{2,10},{10,2},{3,11},{11,3},{4,12},{12,4},... | collective-permute-start | bytes 1179656 | tf_op jit(solution)/shard_map/ppermute | solution.py:336
  61.5 3.4 %collective-permute-start.2 = (bf16[128,128]{1,0:T(8,128)(2,1)S(1)}, bf16[128,128]{1,0:T(8,128)(2,1)S(1)}, u32[]{:S(2)}, u32[]{:S(2)}) collective-permute-start(bf16[128,128]{1,0:T(8,128)(2,1)S(1)} %get-tuple-element.37), channel_id=1, source_target_pairs={{0,16},{16,0},{1,17},{17,1},{2,18},{18,2},{3,19},{19,3},{4,20},{20... | collective-permute-start | bytes 98312 | tf_op jit(solution)/shard_map/ppermute | solution.py:336
  64.9 2.4 %collective-permute-done.2.got_ref = bf16[128,128]{1,0:T(8,128)(2,1)S(1)} collective-permute-done((bf16[128,128]{1,0:T(8,128)(2,1)S(1)}, bf16[128,128]{1,0:T(8,128)(2,1)S(1)}, u32[]{:S(2)}, u32[]{:S(2)}) %collective-permute-start.2) | collective-permute-done | bytes 32800 | tf_op jit(solution)/shard_map/ppermute | solution.py:336
  67.3 0.4 partial_rows.1
  67.7 0.0 collective-permute-done.3.got_ref
  67.7 0.1 add_halves.3
  67.8 1.9 %collective-permute-start.4 = (bf16[1,8,2,48,128]{4,3,2,1,0:T(8,128)(2,1)S(1)}, bf16[1,8,2,48,128]{4,3,2,1,0:T(8,128)(2,1)S(1)}, u32[]{:S(2)}, u32[]{:S(2)}) collective-permute-start(bf16[1,8,2,48,128]{4,3,2,1,0:T(8,128)(2,1)S(1)} %get-tuple-element.45), channel_id=1, source_target_pairs={{0,32},{32,0},{1,33},{33,1},{2,34},{34,2},{3,35},{35,3},{4,36},{36... | collective-permute-start | bytes 589832 | tf_op jit(solution)/shard_map/ppermute | solution.py:336
  69.7 2.8 %collective-permute-start.5 = (bf16[4,16,2048]{2,1,0:T(8,128)(2,1)S(1)}, bf16[4,16,2048]{2,1,0:T(8,128)(2,1)S(1)}, u32[]{:S(2)}, u32[]{:S(2)}) collective-permute-start(bf16[4,16,2048]{2,1,0:T(8,128)(2,1)S(1)} %get-tuple-element.46), channel_id=1, source_target_pairs={{0,1},{1,0},{2,3},{3,2},{4,5},{5,4},{6,7},{7,6},{8,9},{9,8},{10,11... | collective-permute-start | bytes 786440 | tf_op jit(solution)/shard_map/ppermute | solution.py:336
  72.5 3.2 %collective-permute-done.4 = bf16[1,8,2,48,128]{4,3,2,1,0:T(8,128)(2,1)S(1)} collective-permute-done((bf16[1,8,2,48,128]{4,3,2,1,0:T(8,128)(2,1)S(1)}, bf16[1,8,2,48,128]{4,3,2,1,0:T(8,128)(2,1)S(1)}, u32[]{:S(2)}, u32[]{:S(2)}) %collective-permute-start.4) | collective-permute-done | bytes 196640 | tf_op jit(solution)/shard_map/ppermute | solution.py:336
  75.7 0.7 add_convert_fusion
  76.4 2.6 %collective-permute-done.5.got_ref = bf16[4,16,2048]{2,1,0:T(8,128)(2,1)S(1)} collective-permute-done((bf16[4,16,2048]{2,1,0:T(8,128)(2,1)S(1)}, bf16[4,16,2048]{2,1,0:T(8,128)(2,1)S(1)}, u32[]{:S(2)}, u32[]{:S(2)}) %collective-permute-start.5) | collective-permute-done | bytes 262176 | tf_op jit(solution)/shard_map/ppermute | solution.py:336
  79.0 8.3 %all-to-all-start.1 = ((bf16[16,48,128]{2,1,0:T(8,128)(2,1)}), bf16[16,48,128]{2,1,0:T(8,128)(2,1)S(1)}, u32[]{:S(2)}, u32[]{:S(2)}) async-start(bf16[16,48,128]{2,1,0:T(8,128)(2,1)} %bitcast.6), calls=%async_computation.1 | async-start | bytes 393216 | tf_op jit(solution)/shard_map/all_to_all | solution.py:362
  87.5 3.4 %collective-permute-start.6 = (bf16[2,16,2048]{2,1,0:T(8,128)(2,1)S(1)}, bf16[2,16,2048]{2,1,0:T(8,128)(2,1)S(1)}, u32[]{:S(2)}, u32[]{:S(2)}) collective-permute-start(bf16[2,16,2048]{2,1,0:T(8,128)(2,1)S(1)} %get-tuple-element.49), channel_id=1, source_target_pairs={{0,2},{1,3},{2,0},{3,1},{4,6},{5,7},{6,4},{7,5},{8,10},{9,11},{10,... | collective-permute-start | bytes 393224 | tf_op jit(solution)/shard_map/ppermute | solution.py:336
  90.8 5.0 %collective-permute-done.6.got_ref = bf16[2,16,2048]{2,1,0:T(8,128)(2,1)S(1)} collective-permute-done((bf16[2,16,2048]{2,1,0:T(8,128)(2,1)S(1)}, bf16[2,16,2048]{2,1,0:T(8,128)(2,1)S(1)}, u32[]{:S(2)}, u32[]{:S(2)}) %collective-permute-start.6) | collective-permute-done | bytes 131104 | tf_op jit(solution)/shard_map/ppermute | solution.py:336
  95.9 4.6 %collective-permute-start.7 = (bf16[1,16,2048]{2,1,0:T(8,128)(2,1)S(1)}, bf16[1,16,2048]{2,1,0:T(8,128)(2,1)S(1)}, u32[]{:S(2)}, u32[]{:S(2)}) collective-permute-start(bf16[1,16,2048]{2,1,0:T(8,128)(2,1)S(1)} %get-tuple-element.51), channel_id=1, source_target_pairs={{0,4},{4,0},{1,5},{5,1},{2,6},{6,2},{3,7},{7,3},{8,12},{12,8},{9,1... | collective-permute-start | bytes 196616 | tf_op jit(solution)/shard_map/ppermute | solution.py:336
  100.4 3.1 %collective-permute-done.7.got_ref = bf16[1,16,2048]{2,1,0:T(8,128)(2,1)S(1)} collective-permute-done((bf16[1,16,2048]{2,1,0:T(8,128)(2,1)S(1)}, bf16[1,16,2048]{2,1,0:T(8,128)(2,1)S(1)}, u32[]{:S(2)}, u32[]{:S(2)}) %collective-permute-start.7) | collective-permute-done | bytes 65568 | tf_op jit(solution)/shard_map/ppermute | solution.py:336
  103.5 0.0 copy-done
  103.5 0.0 copy-done.1
  103.5 1.1 %mix.1 = bf16[128,2048]{1,0:T(8,128)(2,1)} custom-call(f32[1,16,2048]{2,1,0:T(8,128)S(1)} %get-tuple-element.50.own_ref, bf16[1,16,2048]{2,1,0:T(8,128)(2,1)S(1)} %collective-permute-done.7.got_ref, bf16[16,128]{1,0:T(8,128)(2,1)S(1)} %copy-done.1, f32[16,128]{1,0:T(8,128)S(1)} %copy-done), custom_call_target="tpu_custom_call" | custom-call | tf_op jit(solution)/shard_map/mix/pallas_call | solution.py:295
  104.6 0.0 all-to-all-done.1.blocks_ref
  104.7 0.7 finish.1
  (2 shorter events, 0.1 us)
Async XLA Ops:
  1.4 6.4 %collective-permute-start = (bf16[3,32,128]{2,1,0:T(8,128)(2,1)S(1)}, bf16[3,32,128]{2,1,0:T(8,128)(2,1)S(1)}, u32[]{:S(2)}, u32[]{:S(2)}) collective-permute-start(bf16[3,32,128]{2,1,0:T(8,128)(2,1)S(1)} %pad_maximum_fusion.own_ref), channel_id=1, source_target_pairs={{0,16},{16,0},{1,17},{17,1},{2,18},{18,2},{3,19},{19,3},{4,20},{20... | collective-permute-start | bytes 73736 | tf_op jit(solution)/shard_map/ppermute | solution.py:336
  7.8 49.3 %copy-start.2 = (s32[64]{0:T(128)S(1)}, s32[64]{0:T(128)}, u32[]{:S(2)}) copy-start(s32[64]{0:T(128)} %join_ref.1) | copy-start | bytes 772
  7.8 45.5 %all-to-all-start = ((bf16[16,32,2048]{2,1,0:T(8,128)(2,1)}), bf16[16,32,2048]{2,1,0:T(8,128)(2,1)S(1)}, u32[]{:S(2)}, u32[]{:S(2)}) async-start(bf16[16,32,2048]{2,1,0:T(8,128)(2,1)} %get-tuple-element.33), calls=%async_computation | async-start | bytes 4194304 | tf_op jit(solution)/shard_map/all_to_all | solution.py:347
  53.3 3.8 %collective-permute-start.1 = (bf16[16,128,128]{2,1,0:T(8,128)(2,1)S(1)}, bf16[16,128,128]{2,1,0:T(8,128)(2,1)S(1)}, u32[]{:S(2)}, u32[]{:S(2)}) collective-permute-start(bf16[16,128,128]{2,1,0:T(8,128)(2,1)S(1)} %bitcast.7), channel_id=1, source_target_pairs={{0,8},{8,0},{1,9},{9,1},{2,10},{10,2},{3,11},{11,3},{4,12},{12,4},... | collective-permute-start | bytes 1572872 | tf_op jit(solution)/shard_map/ppermute | solution.py:336
  59.4 44.1 %copy-start = (f32[16,128]{1,0:T(8,128)S(1)}, f32[16,128]{1,0:T(8,128)}, u32[]{:S(2)}) copy-start(f32[16,128]{1,0:T(8,128)} %get-tuple-element.53.slot_weight_ref) | copy-start | bytes 24580
  59.5 44.1 %copy-start.1 = (bf16[16,128]{1,0:T(8,128)(2,1)S(1)}, bf16[16,128]{1,0:T(8,128)(2,1)}, u32[]{:S(2)}) copy-start(bf16[16,128]{1,0:T(8,128)(2,1)} %get-tuple-element.52.chooser_ref) | copy-start | bytes 12292
  59.5 8.2 %collective-permute-start.3 = (bf16[2,8,2,48,128]{4,3,2,1,0:T(8,128)(2,1)S(1)}, bf16[2,8,2,48,128]{4,3,2,1,0:T(8,128)(2,1)S(1)}, u32[]{:S(2)}, u32[]{:S(2)}) collective-permute-start(bf16[2,8,2,48,128]{4,3,2,1,0:T(8,128)(2,1)S(1)} %get-tuple-element.41), channel_id=1, source_target_pairs={{0,8},{8,0},{1,9},{9,1},{2,10},{10,2},{3,11},{11,3},{4,12},{12,4},... | collective-permute-start | bytes 1179656 | tf_op jit(solution)/shard_map/ppermute | solution.py:336
  61.5 5.8 %collective-permute-start.2 = (bf16[128,128]{1,0:T(8,128)(2,1)S(1)}, bf16[128,128]{1,0:T(8,128)(2,1)S(1)}, u32[]{:S(2)}, u32[]{:S(2)}) collective-permute-start(bf16[128,128]{1,0:T(8,128)(2,1)S(1)} %get-tuple-element.37), channel_id=1, source_target_pairs={{0,16},{16,0},{1,17},{17,1},{2,18},{18,2},{3,19},{19,3},{4,20},{20... | collective-permute-start | bytes 98312 | tf_op jit(solution)/shard_map/ppermute | solution.py:336
  67.8 7.9 %collective-permute-start.4 = (bf16[1,8,2,48,128]{4,3,2,1,0:T(8,128)(2,1)S(1)}, bf16[1,8,2,48,128]{4,3,2,1,0:T(8,128)(2,1)S(1)}, u32[]{:S(2)}, u32[]{:S(2)}) collective-permute-start(bf16[1,8,2,48,128]{4,3,2,1,0:T(8,128)(2,1)S(1)} %get-tuple-element.45), channel_id=1, source_target_pairs={{0,32},{32,0},{1,33},{33,1},{2,34},{34,2},{3,35},{35,3},{4,36},{36... | collective-permute-start | bytes 589832 | tf_op jit(solution)/shard_map/ppermute | solution.py:336
  69.7 9.3 %collective-permute-start.5 = (bf16[4,16,2048]{2,1,0:T(8,128)(2,1)S(1)}, bf16[4,16,2048]{2,1,0:T(8,128)(2,1)S(1)}, u32[]{:S(2)}, u32[]{:S(2)}) collective-permute-start(bf16[4,16,2048]{2,1,0:T(8,128)(2,1)S(1)} %get-tuple-element.46), channel_id=1, source_target_pairs={{0,1},{1,0},{2,3},{3,2},{4,5},{5,4},{6,7},{7,6},{8,9},{9,8},{10,11... | collective-permute-start | bytes 786440 | tf_op jit(solution)/shard_map/ppermute | solution.py:336
  79.0 25.6 %all-to-all-start.1 = ((bf16[16,48,128]{2,1,0:T(8,128)(2,1)}), bf16[16,48,128]{2,1,0:T(8,128)(2,1)S(1)}, u32[]{:S(2)}, u32[]{:S(2)}) async-start(bf16[16,48,128]{2,1,0:T(8,128)(2,1)} %bitcast.6), calls=%async_computation.1 | async-start | bytes 393216 | tf_op jit(solution)/shard_map/all_to_all | solution.py:362
  87.5 8.4 %collective-permute-start.6 = (bf16[2,16,2048]{2,1,0:T(8,128)(2,1)S(1)}, bf16[2,16,2048]{2,1,0:T(8,128)(2,1)S(1)}, u32[]{:S(2)}, u32[]{:S(2)}) collective-permute-start(bf16[2,16,2048]{2,1,0:T(8,128)(2,1)S(1)} %get-tuple-element.49), channel_id=1, source_target_pairs={{0,2},{1,3},{2,0},{3,1},{4,6},{5,7},{6,4},{7,5},{8,10},{9,11},{10,... | collective-permute-start | bytes 393224 | tf_op jit(solution)/shard_map/ppermute | solution.py:336
  95.9 7.7 %collective-permute-start.7 = (bf16[1,16,2048]{2,1,0:T(8,128)(2,1)S(1)}, bf16[1,16,2048]{2,1,0:T(8,128)(2,1)S(1)}, u32[]{:S(2)}, u32[]{:S(2)}) collective-permute-start(bf16[1,16,2048]{2,1,0:T(8,128)(2,1)S(1)} %get-tuple-element.51), channel_id=1, source_target_pairs={{0,4},{4,0},{1,5},{5,1},{2,6},{6,2},{3,7},{7,3},{8,12},{12,8},{9,1... | collective-permute-start | bytes 196616 | tf_op jit(solution)/shard_map/ppermute | solution.py:336

commit v7 on v6

--- a/solution.py
+++ b/solution.py
@@ -29,6 +29,10 @@
 
 def params(mib):
     return pltpu.CompilerParams(vmem_limit_bytes=mib * 1024 * 1024)
+
+
+def cost(microseconds):
+    return pl.CostEstimate(flops=int(1.1e9 * microseconds), transcendentals=0, bytes_accessed=int(3.7e6 * microseconds))
 
 
 def route_kernel(
@@ -147,16 +151,14 @@
     )(own, got)
 
 
-def expert_kernel(
-    join_ref, both_ref, own_ref, got_ref, hidden_send_ref, hidden_keep_ref, down, send_ref, keep_ref,
-    gate_up, terms, hiddens,
+def forward_kernel(
+    both_ref, own_ref, got_ref, hidden_send_ref, hidden_keep_ref, acts_ref, down, gate_up, hiddens
 ):
     chips, rows, width = own_ref.shape
     rows = rows // 4
     half = width // 2
     peers, slots = both_ref.shape[0], both_ref.shape[1] // 2
-    depth = both_ref.shape[2]
-    z, y, c = lax.axis_index(Z), lax.axis_index("y"), lax.axis_index("c")
+    y, c = lax.axis_index("y"), lax.axis_index("c")
     for core, ref in ((c, own_ref), (1 - c, got_ref)):
         for chip in range(chips):
             for k in range(2):
@@ -164,26 +166,70 @@
                 gate_up[pl.ds(at, rows), :] = ref[chip, k * rows : (k + 1) * rows, :]
                 down[pl.ds(at, rows), :] = ref[chip, (2 + k) * rows : (3 + k) * rows, :]
     total = peers * slots
-    picked = both_ref[:, :slots, :].reshape(total, depth)
-    dpicked = both_ref[:, slots:, :].reshape(total, depth)
+    picked = both_ref[:, :slots, :].reshape(total, both_ref.shape[2])
     acts = jnp.dot(picked, gate_up[...], preferred_element_type=jnp.float32)
-    turned = pltpu.roll(acts, half, 1)
-    low = lanes(acts.shape) < half
-    gate, up = jnp.where(low, acts, turned), jnp.where(low, turned, acts)
-    sigma = jax.nn.sigmoid(gate)
-    hidden = gate * sigma * up
+    acts_ref[...] = acts
+    gate, up, _ = gate_and_up(acts)
+    hidden = gate * jax.nn.sigmoid(gate) * up
     mine = (lanes(acts.shape) >= half) == (y == 1)
     hiddens[...] = jnp.where(mine, hidden, 0.0)
     group_rows = total // 2
     hidden_send_ref[...] = hiddens[pl.ds((1 - y) * group_rows, group_rows), :].astype(jnp.bfloat16)
     hidden_keep_ref[...] = hiddens[pl.ds(y * group_rows, group_rows), :].astype(jnp.bfloat16)
+
+
+def gate_and_up(acts):
+    half = acts.shape[1] // 2
+    turned = pltpu.roll(acts, half, 1)
+    low = lanes(acts.shape) < half
+    return jnp.where(low, acts, turned), jnp.where(low, turned, acts), low
+
+
+def forward(both, own, got):
+    peers, doubled, depth = both.shape
+    rows = peers * doubled // 2
+    width = own.shape[2]
+    hidden = jax.ShapeDtypeStruct((rows // 2, width), jnp.bfloat16)
+    return pl.pallas_call(
+        forward_kernel,
+        out_shape=(
+            hidden,
+            hidden,
+            jax.ShapeDtypeStruct((rows, width), jnp.float32),
+            jax.ShapeDtypeStruct((depth, width), jnp.bfloat16),
+        ),
+        in_specs=whole(3),
+        out_specs=tuple(whole(4)),
+        scratch_shapes=[
+            pltpu.VMEM((depth, width), jnp.bfloat16),
+            pltpu.VMEM((rows, width), jnp.float32),
+        ],
+        compiler_params=params(12),
+        name="forward",
+    )(both, own, got)
+
+
+def backward_kernel(join_ref, both_ref, acts_ref, down, send_ref, keep_ref, terms):
+    peers, slots = both_ref.shape[0], both_ref.shape[1] // 2
+    depth = both_ref.shape[2]
+    total, width = acts_ref.shape
+    half = width // 2
+    chips = send_ref.shape[0] * send_ref.shape[1]
+    rows = send_ref.shape[3] // 3 * 2
+    z, y, c = lax.axis_index(Z), lax.axis_index("y"), lax.axis_index("c")
+    picked = both_ref[:, :slots, :].reshape(total, depth)
+    dpicked = both_ref[:, slots:, :].reshape(total, depth)
+    gate, up, low = gate_and_up(acts_ref[...])
+    sigma = jax.nn.sigmoid(gate)
+    hidden = gate * sigma * up
+    mine = (lanes(gate.shape) >= half) == (y == 1)
     dhidden = jnp.dot(dpicked, down[...], preferred_element_type=jnp.float32)
     dhidden = jnp.where(mine, dhidden, pltpu.roll(dhidden, half, 1))
     dgate = dhidden * up * sigma * (1.0 + gate * (1.0 - sigma))
     dup = dhidden * gate * sigma
     first = 1.0 - join_ref[(z * 2 + 0) * 2 + c].astype(jnp.float32)
     second = 1.0 - join_ref[(z * 2 + 1) * 2 + c].astype(jnp.float32)
-    group = lax.broadcasted_iota(jnp.int32, acts.shape, 0) // group_rows
+    group = lax.broadcasted_iota(jnp.int32, gate.shape, 0) // (total // 2)
     active = jnp.where(group == 0, first, second)
     dacts = (jnp.where(low, dgate, dup) * active).astype(jnp.bfloat16)
     counted = (hidden.astype(jnp.bfloat16).astype(jnp.float32) * active).astype(jnp.bfloat16)
@@ -206,31 +252,23 @@
                 ref[away, chip // 2, k, rows:, :] = packed.astype(ref.dtype)
 
 
-def expert(join, both, own, got):
-    peers, doubled, depth = both.shape
-    slots = doubled // 2
-    chips, rows, width = own.shape
-    chunk = (2, chips // 2, 2, rows // 8 * 3, width)
-    hidden = jax.ShapeDtypeStruct((peers * slots // 2, width), jnp.bfloat16)
-    return pl.pallas_call(
-        expert_kernel,
+def backward(join, both, acts, down, chips):
+    depth, width = down.shape
+    rows = depth // chips // 4
+    chunk = (2, chips // 2, 2, rows // 2 * 3, width)
+    return pl.pallas_call(
+        backward_kernel,
         out_shape=(
-            hidden,
-            hidden,
-            jax.ShapeDtypeStruct((depth, width), jnp.bfloat16),
             jax.ShapeDtypeStruct(chunk, jnp.bfloat16),
             jax.ShapeDtypeStruct(chunk, jnp.float32),
         ),
         in_specs=[pl.BlockSpec(memory_space=pltpu.SMEM), *whole(3)],
-        out_specs=tuple(whole(5)),
-        scratch_shapes=[
-            pltpu.VMEM((depth, width), jnp.bfloat16),
-            pltpu.VMEM((2, depth, width), jnp.float32),
-            pltpu.VMEM((peers * slots, width), jnp.float32),
-        ],
-        compiler_params=params(24),
-        name="expert",
-    )(join, both, own, got)
+        out_specs=tuple(whole(2)),
+        scratch_shapes=[pltpu.VMEM((2, depth, width), jnp.float32)],
+        compiler_params=params(16),
+        cost_estimate=cost(8),
+        name="backward",
+    )(join, both, acts, down)
 
 
 def partial_kernel(keep_ref, got_ref, down_ref, mine_ref, theirs_ref, partials):
@@ -258,6 +296,7 @@
         out_specs=tuple(whole(2)),
         scratch_shapes=[pltpu.VMEM((peers, slots, depth), jnp.float32)],
         compiler_params=params(8),
+        cost_estimate=cost(5),
         name="partial_rows",
     )(keep, got, down)
 
@@ -268,7 +307,7 @@
     theirs_ref[...] = (keep_ref[half:] + got_ref[half:].astype(jnp.float32)).astype(jnp.bfloat16)
 
 
-def add_halves(keep, got):
+def add_halves(keep, got, lasts):
     half = (keep.shape[0] // 2, *keep.shape[1:])
     return pl.pallas_call(
         add_kernel,
@@ -279,6 +318,7 @@
         in_specs=whole(2),
         out_specs=tuple(whole(2)),
         compiler_params=params(8),
+        cost_estimate=cost(lasts),
         name="add_halves",
     )(keep, got)
 
@@ -298,6 +338,7 @@
         in_specs=whole(4),
         out_specs=whole(1)[0],
         compiler_params=params(8),
+        cost_estimate=cost(1),
         name="mix",
     )(own, got, chooser, slot_weight)
 
@@ -348,20 +389,20 @@
     along = lax.all_gather(packed, Z, axis=0, tiled=False)
     along, rows_in = lax.optimization_barrier((along, rows_in))
     other = swapped(along, "c")
-    hidden_send, hidden, down, send, keep = expert(join_groups, rows_in, along, other)
+    hidden_send, hidden, acts, down = forward(rows_in, along, other)
     hidden_got = swapped(hidden_send, "y")
+    send, keep = backward(join_groups, rows_in, acts, down, lax.axis_size(Z))
     from_core = swapped(send, "c")
     partial, partial_send = partial_rows(hidden, hidden_got, down, lax.axis_size(("h", "x")))
-    from_core, partial_send = lax.optimization_barrier((from_core, partial_send))
     partial_got = swapped(partial_send, "x")
-    keep, to_pair = add_halves(keep, from_core)
+    from_core, _ = lax.optimization_barrier((from_core, partial_send))
+    keep, to_pair = add_halves(keep, from_core, 0.4)
     from_pair = swapped(to_pair, "zl")
     pair_sum = (keep + from_pair.astype(jnp.float32)).astype(jnp.bfloat16)
     pair_sum = pair_sum.reshape(-1, *pair_sum.shape[3:])
-    pair_sum, partial_got = lax.optimization_barrier((pair_sum, partial_got))
     pieces = lax.all_to_all(pair_sum, ("zh", "y"), 0, 0, tiled=True)
-    partial, partial_send = add_halves(partial, partial_got)
-    partial, partial_send = add_halves(partial, swapped(partial_send, "x", 2))
+    partial, partial_send = add_halves(partial, partial_got, 2)
+    partial, partial_send = add_halves(partial, swapped(partial_send, "x", 2), 1)
     mixed = mix(partial, swapped(partial_send, "h"), chooser, slot_weight)
     return (mixed, *finish(pieces))
 

time: 107 us -> 103 us (0.963)
  waiting for transfers between devices: 18.2 us -> 16 us
  starting transfers between devices: 40.5 us -> 39.1 us
    ppermute x8, waiting for transfers between devices: 18.2 us -> 15.2 us  [swapped(): return lax.ppermute(part, axis, [(i, i ^ distance) for i in range(size)])]
    all_to_all x1, starting transfers between devices: 8.35 us -> 6.83 us  [per_device(): pieces = lax.all_to_all(pair_sum, ('zh', 'y'), 0, 0, tiled=True)]
    pallas_call x1 -> x2, Pallas kernels: 2.34 us -> 2.53 us  [the longest x1 1.93 us: backward(): pl.pallas_call(backward_kernel, out_shape=(jax.ShapeDtypeStruct(chunk, jn...]
  transfers between devices with their start and end apart: 10 -> 10, of which waited for: 6 -> 6; matrix products, arithmetic and copies ran while one was open for 1% -> 1% of each run, Pallas kernels for 4% -> 6%
where the time goes in v7:
time: 103 us; the launch traced here: 102 us
  starting transfers between devices  39.1 us (38%)
  blocking collectives  36.8 us (36%)
  waiting for transfers between devices  16 us (16%)
  Pallas kernels  7.83 us (8%)
  other arithmetic  1.45 us (1%)
    all_gather x1, blocking collectives, per_device(): along = lax.all_gather(packed, Z, axis=0, tiled=False)  36.8 us
    ppermute x8, starting transfers between devices, swapped(): return lax.ppermute(part, axis, [(i, i ^ distance) for i in range(size)])  23.5 us
    ppermute x8, waiting for transfers between devices, swapped(): return lax.ppermute(part, axis, [(i, i ^ distance) for i in range(size)])  15.2 us
    all_to_all x1, starting transfers between devices, per_device(): rows_in = lax.all_to_all(copies, PLANE, 0, 0, tiled=True)  8.71 us
    all_to_all x1, starting transfers between devices, per_device(): pieces = lax.all_to_all(pair_sum, ('zh', 'y'), 0, 0, tiled=True)  6.83 us
    pallas_call x1, Pallas kernels, route(): pl.pallas_call(route_kernel, out_shape=(jax.ShapeDtypeStruct((peers, 2 *...  2.88 us
  transfers between devices with their start and end apart: 10, of which 6 were waited for; matrix products, arithmetic and copies ran while one was open for 1% of the time, Pallas kernels for 6%

profile of v7, /device:TPU:6, one launch (start us, length us, event | category | flops | bytes accessed | tf_op | source)
XLA Modules:
  0.0 102.0 jit_solution(16633427585441243066)
XLA Ops:
  0.6 0.7 pad_maximum_fusion.own_ref
  1.4 3.5 %collective-permute-start = (bf16[3,32,128]{2,1,0:T(8,128)(2,1)S(1)}, bf16[3,32,128]{2,1,0:T(8,128)(2,1)S(1)}, u32[]{:S(2)}, u32[]{:S(2)}) collective-permute-start(bf16[3,32,128]{2,1,0:T(8,128)(2,1)S(1)} %pad_maximum_fusion.own_ref), channel_id=1, source_target_pairs={{0,16},{16,0},{1,17},{17,1},{2,18},{18,2},{3,19},{19,3},{4,20},{20... | collective-permute-start | bytes 73736 | tf_op jit(solution)/shard_map/ppermute | solution.py:377
  4.8 2.9 %route.1 = (bf16[16,32,2048]{2,1,0:T(8,128)(2,1)}, bf16[16,128]{1,0:T(8,128)(2,1)}, f32[16,128]{1,0:T(8,128)}) custom-call(s32[8,128]{1,0:T(8,128)} %bitcast.12, f32[8,128]{1,0:T(8,128)} %bitcast.13, bf16[128,2048]{1,0:T(8,128)(2,1)} %tokens_ref.1, bf16[128,2048]{1,0:T(8,128)(2,1)} %cot_ref.1), custom_call_target="tpu_custom_call" | custom-call | tf_op jit(solution)/shard_map/route/pallas_call | solution.py:98
  7.7 0.0 collective-permute-done.got_ref
  7.7 0.1 pack_shards.1
  7.8 8.7 %all-to-all-start = ((bf16[16,32,2048]{2,1,0:T(8,128)(2,1)}), bf16[16,32,2048]{2,1,0:T(8,128)(2,1)S(1)}, u32[]{:S(2)}, u32[]{:S(2)}) async-start(bf16[16,32,2048]{2,1,0:T(8,128)(2,1)} %get-tuple-element.31), calls=%async_computation | async-start | bytes 4194304 | tf_op jit(solution)/shard_map/all_to_all | solution.py:388
  16.5 0.0 copy-start.2
  16.6 36.8 %all-gather = bf16[2048,128]{1,0:T(8,128)(2,1)S(1)} all-gather(bf16[128,128]{1,0:T(8,128)(2,1)S(1)} %pack_shards.1), channel_id=2, replica_groups=mesh['zh'=8,'zl'=2,'y'=2,'c'=2,'h'=2,'x'=4] {'zh','zl'}, dimensions={0}, use_global_device_ids=true | all-gather | bytes 557056 | tf_op jit(solution)/shard_map/all_gather | solution.py:389
  53.3 0.0 all-to-all-done.both_ref
  53.3 1.9 %collective-permute-start.1 = (bf16[16,128,128]{2,1,0:T(8,128)(2,1)S(1)}, bf16[16,128,128]{2,1,0:T(8,128)(2,1)S(1)}, u32[]{:S(2)}, u32[]{:S(2)}) collective-permute-start(bf16[16,128,128]{2,1,0:T(8,128)(2,1)S(1)} %bitcast.7), channel_id=1, source_target_pairs={{0,8},{8,0},{1,9},{9,1},{2,10},{10,2},{3,11},{11,3},{4,12},{12,4},... | collective-permute-start | bytes 1572872 | tf_op jit(solution)/shard_map/ppermute | solution.py:377
  55.2 1.9 %collective-permute-done.1.got_ref = bf16[16,128,128]{2,1,0:T(8,128)(2,1)S(1)} collective-permute-done((bf16[16,128,128]{2,1,0:T(8,128)(2,1)S(1)}, bf16[16,128,128]{2,1,0:T(8,128)(2,1)S(1)}, u32[]{:S(2)}, u32[]{:S(2)}) %collective-permute-start.1) | collective-permute-done | bytes 524320 | tf_op jit(solution)/shard_map/ppermute | solution.py:377
  57.1 0.6 forward.1
  57.7 3.4 %collective-permute-start.2 = (bf16[128,128]{1,0:T(8,128)(2,1)S(1)}, bf16[128,128]{1,0:T(8,128)(2,1)S(1)}, u32[]{:S(2)}, u32[]{:S(2)}) collective-permute-start(bf16[128,128]{1,0:T(8,128)(2,1)S(1)} %get-tuple-element.35), channel_id=1, source_target_pairs={{0,16},{16,0},{1,17},{17,1},{2,18},{18,2},{3,19},{19,3},{4,20},{20... | collective-permute-start | bytes 98312 | tf_op jit(solution)/shard_map/ppermute | solution.py:377
  61.1 0.0 copy-done.2
  61.1 1.9 %backward.1 = (bf16[2,8,2,48,128]{4,3,2,1,0:T(8,128)(2,1)S(1)}, f32[2,8,2,48,128]{4,3,2,1,0:T(8,128)S(1)}) custom-call(s32[64]{0:T(128)S(1)} %copy-done.2, bf16[16,32,2048]{2,1,0:T(8,128)(2,1)S(1)} %all-to-all-done.both_ref, f32[256,128]{1,0:T(8,128)S(1)} %get-tuple-element.45.acts_ref, bf16[2048,128]{1,0:T(8,128)(2,1)S(1)} %get-tuple-element.36.down_ref.down), custom_call_target="tpu_custom_call" | custom-call | flops 8800000000 | bytes 29600000 | tf_op jit(solution)/shard_map/backward/pallas_call | solution.py:259
  63.0 1.9 %collective-permute-start.6 = (bf16[2,8,2,48,128]{4,3,2,1,0:T(8,128)(2,1)S(1)}, bf16[2,8,2,48,128]{4,3,2,1,0:T(8,128)(2,1)S(1)}, u32[]{:S(2)}, u32[]{:S(2)}) collective-permute-start(bf16[2,8,2,48,128]{4,3,2,1,0:T(8,128)(2,1)S(1)} %get-tuple-element.47), channel_id=1, source_target_pairs={{0,8},{8,0},{1,9},{9,1},{2,10},{10,2},{3,11},{11,3},{4,12},{12,4},... | collective-permute-start | bytes 1179656 | tf_op jit(solution)/shard_map/ppermute | solution.py:377
  65.0 0.0 collective-permute-done.2.got_ref
  65.0 0.4 partial_rows.1
  65.3 1.3 %collective-permute-done.6.got_ref = bf16[2,8,2,48,128]{4,3,2,1,0:T(8,128)(2,1)S(1)} collective-permute-done((bf16[2,8,2,48,128]{4,3,2,1,0:T(8,128)(2,1)S(1)}, bf16[2,8,2,48,128]{4,3,2,1,0:T(8,128)(2,1)S(1)}, u32[]{:S(2)}, u32[]{:S(2)}) %collective-permute-start.6) | collective-permute-done | bytes 393248 | tf_op jit(solution)/shard_map/ppermute | solution.py:377
  66.7 0.1 add_halves.5
  66.7 1.9 %collective-permute-start.7 = (bf16[1,8,2,48,128]{4,3,2,1,0:T(8,128)(2,1)S(1)}, bf16[1,8,2,48,128]{4,3,2,1,0:T(8,128)(2,1)S(1)}, u32[]{:S(2)}, u32[]{:S(2)}) collective-permute-start(bf16[1,8,2,48,128]{4,3,2,1,0:T(8,128)(2,1)S(1)} %get-tuple-element.50), channel_id=1, source_target_pairs={{0,32},{32,0},{1,33},{33,1},{2,34},{34,2},{3,35},{35,3},{4,36},{36... | collective-permute-start | bytes 589832 | tf_op jit(solution)/shard_map/ppermute | solution.py:377
  68.6 2.8 %collective-permute-start.3 = (bf16[4,16,2048]{2,1,0:T(8,128)(2,1)S(1)}, bf16[4,16,2048]{2,1,0:T(8,128)(2,1)S(1)}, u32[]{:S(2)}, u32[]{:S(2)}) collective-permute-start(bf16[4,16,2048]{2,1,0:T(8,128)(2,1)S(1)} %get-tuple-element.38), channel_id=1, source_target_pairs={{0,1},{1,0},{2,3},{3,2},{4,5},{5,4},{6,7},{7,6},{8,9},{9,8},{10,11... | collective-permute-start | bytes 786440 | tf_op jit(solution)/shard_map/ppermute | solution.py:377
  71.4 4.1 %collective-permute-done.7 = bf16[1,8,2,48,128]{4,3,2,1,0:T(8,128)(2,1)S(1)} collective-permute-done((bf16[1,8,2,48,128]{4,3,2,1,0:T(8,128)(2,1)S(1)}, bf16[1,8,2,48,128]{4,3,2,1,0:T(8,128)(2,1)S(1)}, u32[]{:S(2)}, u32[]{:S(2)}) %collective-permute-start.7) | collective-permute-done | bytes 196640 | tf_op jit(solution)/shard_map/ppermute | solution.py:377
  75.6 0.7 add_convert_fusion
  76.3 6.8 %all-to-all-start.1 = ((bf16[16,48,128]{2,1,0:T(8,128)(2,1)}), bf16[16,48,128]{2,1,0:T(8,128)(2,1)S(1)}, u32[]{:S(2)}, u32[]{:S(2)}) async-start(bf16[16,48,128]{2,1,0:T(8,128)(2,1)} %bitcast.6), calls=%async_computation.1 | async-start | bytes 393216 | tf_op jit(solution)/shard_map/all_to_all | solution.py:403
  83.1 0.0 collective-permute-done.3.got_ref
  83.2 0.0 copy-start
  83.2 0.0 copy-start.1
  83.2 3.3 %collective-permute-start.4 = (bf16[2,16,2048]{2,1,0:T(8,128)(2,1)S(1)}, bf16[2,16,2048]{2,1,0:T(8,128)(2,1)S(1)}, u32[]{:S(2)}, u32[]{:S(2)}) collective-permute-start(bf16[2,16,2048]{2,1,0:T(8,128)(2,1)S(1)} %get-tuple-element.40), channel_id=1, source_target_pairs={{0,2},{1,3},{2,0},{3,1},{4,6},{5,7},{6,4},{7,5},{8,10},{9,11},{10,... | collective-permute-start | bytes 393224 | tf_op jit(solution)/shard_map/ppermute | solution.py:377
  86.5 5.0 %collective-permute-done.4.got_ref = bf16[2,16,2048]{2,1,0:T(8,128)(2,1)S(1)} collective-permute-done((bf16[2,16,2048]{2,1,0:T(8,128)(2,1)S(1)}, bf16[2,16,2048]{2,1,0:T(8,128)(2,1)S(1)}, u32[]{:S(2)}, u32[]{:S(2)}) %collective-permute-start.4) | collective-permute-done | bytes 131104 | tf_op jit(solution)/shard_map/ppermute | solution.py:377
  91.6 4.8 %collective-permute-start.5 = (bf16[1,16,2048]{2,1,0:T(8,128)(2,1)S(1)}, bf16[1,16,2048]{2,1,0:T(8,128)(2,1)S(1)}, u32[]{:S(2)}, u32[]{:S(2)}) collective-permute-start(bf16[1,16,2048]{2,1,0:T(8,128)(2,1)S(1)} %get-tuple-element.42), channel_id=1, source_target_pairs={{0,4},{4,0},{1,5},{5,1},{2,6},{6,2},{3,7},{7,3},{8,12},{12,8},{9,1... | collective-permute-start | bytes 196616 | tf_op jit(solution)/shard_map/ppermute | solution.py:377
  96.4 2.9 %collective-permute-done.5.got_ref = bf16[1,16,2048]{2,1,0:T(8,128)(2,1)S(1)} collective-permute-done((bf16[1,16,2048]{2,1,0:T(8,128)(2,1)S(1)}, bf16[1,16,2048]{2,1,0:T(8,128)(2,1)S(1)}, u32[]{:S(2)}, u32[]{:S(2)}) %collective-permute-start.5) | collective-permute-done | bytes 65568 | tf_op jit(solution)/shard_map/ppermute | solution.py:377
  99.3 0.0 copy-done
  99.3 0.0 copy-done.1
  99.3 1.1 %mix.1 = bf16[128,2048]{1,0:T(8,128)(2,1)} custom-call(f32[1,16,2048]{2,1,0:T(8,128)S(1)} %get-tuple-element.41.own_ref, bf16[1,16,2048]{2,1,0:T(8,128)(2,1)S(1)} %collective-permute-done.5.got_ref, bf16[16,128]{1,0:T(8,128)(2,1)S(1)} %copy-done.1, f32[16,128]{1,0:T(8,128)S(1)} %copy-done), custom_call_target="tpu_custom_call" | custom-call | flops 1100000000 | bytes 3700000 | tf_op jit(solution)/shard_map/mix/pallas_call | solution.py:335
  100.5 0.8 all-to-all-done.1.blocks_ref
  101.3 0.7 finish.1
  (2 shorter events, 0.1 us)
Async XLA Ops:
  1.4 6.4 %collective-permute-start = (bf16[3,32,128]{2,1,0:T(8,128)(2,1)S(1)}, bf16[3,32,128]{2,1,0:T(8,128)(2,1)S(1)}, u32[]{:S(2)}, u32[]{:S(2)}) collective-permute-start(bf16[3,32,128]{2,1,0:T(8,128)(2,1)S(1)} %pad_maximum_fusion.own_ref), channel_id=1, source_target_pairs={{0,16},{16,0},{1,17},{17,1},{2,18},{18,2},{3,19},{19,3},{4,20},{20... | collective-permute-start | bytes 73736 | tf_op jit(solution)/shard_map/ppermute | solution.py:377
  7.8 45.5 %all-to-all-start = ((bf16[16,32,2048]{2,1,0:T(8,128)(2,1)}), bf16[16,32,2048]{2,1,0:T(8,128)(2,1)S(1)}, u32[]{:S(2)}, u32[]{:S(2)}) async-start(bf16[16,32,2048]{2,1,0:T(8,128)(2,1)} %get-tuple-element.31), calls=%async_computation | async-start | bytes 4194304 | tf_op jit(solution)/shard_map/all_to_all | solution.py:388
  16.5 44.5 %copy-start.2 = (s32[64]{0:T(128)S(1)}, s32[64]{0:T(128)}, u32[]{:S(2)}) copy-start(s32[64]{0:T(128)} %join_ref.1) | copy-start | bytes 772
  53.3 3.8 %collective-permute-start.1 = (bf16[16,128,128]{2,1,0:T(8,128)(2,1)S(1)}, bf16[16,128,128]{2,1,0:T(8,128)(2,1)S(1)}, u32[]{:S(2)}, u32[]{:S(2)}) collective-permute-start(bf16[16,128,128]{2,1,0:T(8,128)(2,1)S(1)} %bitcast.7), channel_id=1, source_target_pairs={{0,8},{8,0},{1,9},{9,1},{2,10},{10,2},{3,11},{11,3},{4,12},{12,4},... | collective-permute-start | bytes 1572872 | tf_op jit(solution)/shard_map/ppermute | solution.py:377
  57.7 7.3 %collective-permute-start.2 = (bf16[128,128]{1,0:T(8,128)(2,1)S(1)}, bf16[128,128]{1,0:T(8,128)(2,1)S(1)}, u32[]{:S(2)}, u32[]{:S(2)}) collective-permute-start(bf16[128,128]{1,0:T(8,128)(2,1)S(1)} %get-tuple-element.35), channel_id=1, source_target_pairs={{0,16},{16,0},{1,17},{17,1},{2,18},{18,2},{3,19},{19,3},{4,20},{20... | collective-permute-start | bytes 98312 | tf_op jit(solution)/shard_map/ppermute | solution.py:377
  63.0 3.6 %collective-permute-start.6 = (bf16[2,8,2,48,128]{4,3,2,1,0:T(8,128)(2,1)S(1)}, bf16[2,8,2,48,128]{4,3,2,1,0:T(8,128)(2,1)S(1)}, u32[]{:S(2)}, u32[]{:S(2)}) collective-permute-start(bf16[2,8,2,48,128]{4,3,2,1,0:T(8,128)(2,1)S(1)} %get-tuple-element.47), channel_id=1, source_target_pairs={{0,8},{8,0},{1,9},{9,1},{2,10},{10,2},{3,11},{11,3},{4,12},{12,4},... | collective-permute-start | bytes 1179656 | tf_op jit(solution)/shard_map/ppermute | solution.py:377
  66.7 8.8 %collective-permute-start.7 = (bf16[1,8,2,48,128]{4,3,2,1,0:T(8,128)(2,1)S(1)}, bf16[1,8,2,48,128]{4,3,2,1,0:T(8,128)(2,1)S(1)}, u32[]{:S(2)}, u32[]{:S(2)}) collective-permute-start(bf16[1,8,2,48,128]{4,3,2,1,0:T(8,128)(2,1)S(1)} %get-tuple-element.50), channel_id=1, source_target_pairs={{0,32},{32,0},{1,33},{33,1},{2,34},{34,2},{3,35},{35,3},{4,36},{36... | collective-permute-start | bytes 589832 | tf_op jit(solution)/shard_map/ppermute | solution.py:377
  68.6 14.5 %collective-permute-start.3 = (bf16[4,16,2048]{2,1,0:T(8,128)(2,1)S(1)}, bf16[4,16,2048]{2,1,0:T(8,128)(2,1)S(1)}, u32[]{:S(2)}, u32[]{:S(2)}) collective-permute-start(bf16[4,16,2048]{2,1,0:T(8,128)(2,1)S(1)} %get-tuple-element.38), channel_id=1, source_target_pairs={{0,1},{1,0},{2,3},{3,2},{4,5},{5,4},{6,7},{7,6},{8,9},{9,8},{10,11... | collective-permute-start | bytes 786440 | tf_op jit(solution)/shard_map/ppermute | solution.py:377
  76.3 25.0 %all-to-all-start.1 = ((bf16[16,48,128]{2,1,0:T(8,128)(2,1)}), bf16[16,48,128]{2,1,0:T(8,128)(2,1)S(1)}, u32[]{:S(2)}, u32[]{:S(2)}) async-start(bf16[16,48,128]{2,1,0:T(8,128)(2,1)} %bitcast.6), calls=%async_computation.1 | async-start | bytes 393216 | tf_op jit(solution)/shard_map/all_to_all | solution.py:403
  83.2 16.1 %copy-start = (f32[16,128]{1,0:T(8,128)S(1)}, f32[16,128]{1,0:T(8,128)}, u32[]{:S(2)}) copy-start(f32[16,128]{1,0:T(8,128)} %get-tuple-element.44.slot_weight_ref) | copy-start | bytes 24580
  83.2 16.1 %copy-start.1 = (bf16[16,128]{1,0:T(8,128)(2,1)S(1)}, bf16[16,128]{1,0:T(8,128)(2,1)}, u32[]{:S(2)}) copy-start(bf16[16,128]{1,0:T(8,128)(2,1)} %get-tuple-element.43.chooser_ref) | copy-start | bytes 12292
  83.2 8.4 %collective-permute-start.4 = (bf16[2,16,2048]{2,1,0:T(8,128)(2,1)S(1)}, bf16[2,16,2048]{2,1,0:T(8,128)(2,1)S(1)}, u32[]{:S(2)}, u32[]{:S(2)}) collective-permute-start(bf16[2,16,2048]{2,1,0:T(8,128)(2,1)S(1)} %get-tuple-element.40), channel_id=1, source_target_pairs={{0,2},{1,3},{2,0},{3,1},{4,6},{5,7},{6,4},{7,5},{8,10},{9,11},{10,... | collective-permute-start | bytes 393224 | tf_op jit(solution)/shard_map/ppermute | solution.py:377
  91.6 7.7 %collective-permute-start.5 = (bf16[1,16,2048]{2,1,0:T(8,128)(2,1)S(1)}, bf16[1,16,2048]{2,1,0:T(8,128)(2,1)S(1)}, u32[]{:S(2)}, u32[]{:S(2)}) collective-permute-start(bf16[1,16,2048]{2,1,0:T(8,128)(2,1)S(1)} %get-tuple-element.42), channel_id=1, source_target_pairs={{0,4},{4,0},{1,5},{5,1},{2,6},{6,2},{3,7},{7,3},{8,12},{12,8},{9,1... | collective-permute-start | bytes 196616 | tf_op jit(solution)/shard_map/ppermute | solution.py:377

commit v8 on v7

--- a/solution.py
+++ b/solution.py
@@ -277,11 +277,11 @@
     )
     partials[...] = partial.reshape(partials.shape)
     h, x = lax.axis_index("h"), lax.axis_index("x")
-    for low, ref in enumerate((mine_ref, theirs_ref)):
-        for high in range(2):
+    for high, ref in enumerate((mine_ref, theirs_ref)):
+        for low in range(2):
             for row in range(2):
                 peer = jnp.bitwise_xor(h, row) * 4 + jnp.bitwise_xor(x, 2 * high + low)
-                ref[2 * high + row] = partials[peer].astype(ref.dtype)
+                ref[2 * low + row] = partials[peer].astype(ref.dtype)
 
 
 def partial_rows(keep, got, down, peers):
@@ -394,7 +394,7 @@
     send, keep = backward(join_groups, rows_in, acts, down, lax.axis_size(Z))
     from_core = swapped(send, "c")
     partial, partial_send = partial_rows(hidden, hidden_got, down, lax.axis_size(("h", "x")))
-    partial_got = swapped(partial_send, "x")
+    partial_got = swapped(partial_send, "x", 2)
     from_core, _ = lax.optimization_barrier((from_core, partial_send))
     keep, to_pair = add_halves(keep, from_core, 0.4)
     from_pair = swapped(to_pair, "zl")
@@ -402,7 +402,7 @@
     pair_sum = pair_sum.reshape(-1, *pair_sum.shape[3:])
     pieces = lax.all_to_all(pair_sum, ("zh", "y"), 0, 0, tiled=True)
     partial, partial_send = add_halves(partial, partial_got, 2)
-    partial, partial_send = add_halves(partial, swapped(partial_send, "x", 2), 1)
+    partial, partial_send = add_halves(partial, swapped(partial_send, "x"), 1)
     mixed = mix(partial, swapped(partial_send, "h"), chooser, slot_weight)
     return (mixed, *finish(pieces))
 

time: 103 us -> 103 us (level)
    ppermute x8, waiting for transfers between devices: 15.2 us -> 13.9 us  [swapped(): return lax.ppermute(part, axis, [(i, i ^ distance) for i in range(size)])]
    all_to_all x1, waiting for transfers between devices: 0.8 us -> 2.08 us  [per_device(): pieces = lax.all_to_all(pair_sum, ('zh', 'y'), 0, 0, tiled=True)]
where the time goes in v8:
time: 103 us; the launch traced here: 102 us
  starting transfers between devices  39.1 us (38%)
  blocking collectives  36.8 us (36%)
  waiting for transfers between devices  16 us (16%)
  Pallas kernels  7.84 us (8%)
  other arithmetic  1.45 us (1%)
    all_gather x1, blocking collectives, per_device(): along = lax.all_gather(packed, Z, axis=0, tiled=False)  36.8 us
    ppermute x8, starting transfers between devices, swapped(): return lax.ppermute(part, axis, [(i, i ^ distance) for i in range(size)])  23.5 us
    ppermute x8, waiting for transfers between devices, swapped(): return lax.ppermute(part, axis, [(i, i ^ distance) for i in range(size)])  13.9 us
    all_to_all x1, starting transfers between devices, per_device(): rows_in = lax.all_to_all(copies, PLANE, 0, 0, tiled=True)  8.71 us
    all_to_all x1, starting transfers between devices, per_device(): pieces = lax.all_to_all(pair_sum, ('zh', 'y'), 0, 0, tiled=True)  6.83 us
    pallas_call x1, Pallas kernels, route(): pl.pallas_call(route_kernel, out_shape=(jax.ShapeDtypeStruct((peers, 2 *...  2.88 us
    all_to_all x1, waiting for transfers between devices, per_device(): pieces = lax.all_to_all(pair_sum, ('zh', 'y'), 0, 0, tiled=True)  2.08 us
  transfers between devices with their start and end apart: 10, of which 6 were waited for; matrix products, arithmetic and copies ran while one was open for 1% of the time, Pallas kernels for 6%

profile of v8, /device:TPU:6, one launch (start us, length us, event | category | flops | bytes accessed | tf_op | source)
XLA Modules:
  0.0 102.0 jit_solution(1649426178036139156)
XLA Ops:
  0.6 0.7 pad_maximum_fusion.own_ref
  1.4 3.5 %collective-permute-start = (bf16[3,32,128]{2,1,0:T(8,128)(2,1)S(1)}, bf16[3,32,128]{2,1,0:T(8,128)(2,1)S(1)}, u32[]{:S(2)}, u32[]{:S(2)}) collective-permute-start(bf16[3,32,128]{2,1,0:T(8,128)(2,1)S(1)} %pad_maximum_fusion.own_ref), channel_id=1, source_target_pairs={{0,16},{16,0},{1,17},{17,1},{2,18},{18,2},{3,19},{19,3},{4,20},{20... | collective-permute-start | bytes 73736 | tf_op jit(solution)/shard_map/ppermute | solution.py:377
  4.8 2.9 %route.1 = (bf16[16,32,2048]{2,1,0:T(8,128)(2,1)}, bf16[16,128]{1,0:T(8,128)(2,1)}, f32[16,128]{1,0:T(8,128)}) custom-call(s32[8,128]{1,0:T(8,128)} %bitcast.12, f32[8,128]{1,0:T(8,128)} %bitcast.13, bf16[128,2048]{1,0:T(8,128)(2,1)} %tokens_ref.1, bf16[128,2048]{1,0:T(8,128)(2,1)} %cot_ref.1), custom_call_target="tpu_custom_call" | custom-call | tf_op jit(solution)/shard_map/route/pallas_call | solution.py:98
  7.7 0.0 collective-permute-done.got_ref
  7.7 0.1 pack_shards.1
  7.8 8.7 %all-to-all-start = ((bf16[16,32,2048]{2,1,0:T(8,128)(2,1)}), bf16[16,32,2048]{2,1,0:T(8,128)(2,1)S(1)}, u32[]{:S(2)}, u32[]{:S(2)}) async-start(bf16[16,32,2048]{2,1,0:T(8,128)(2,1)} %get-tuple-element.31), calls=%async_computation | async-start | bytes 4194304 | tf_op jit(solution)/shard_map/all_to_all | solution.py:388
  16.5 0.0 copy-start.2
  16.6 36.8 %all-gather = bf16[2048,128]{1,0:T(8,128)(2,1)S(1)} all-gather(bf16[128,128]{1,0:T(8,128)(2,1)S(1)} %pack_shards.1), channel_id=2, replica_groups=mesh['zh'=8,'zl'=2,'y'=2,'c'=2,'h'=2,'x'=4] {'zh','zl'}, dimensions={0}, use_global_device_ids=true | all-gather | bytes 557056 | tf_op jit(solution)/shard_map/all_gather | solution.py:389
  53.3 0.0 all-to-all-done.both_ref
  53.3 1.9 %collective-permute-start.1 = (bf16[16,128,128]{2,1,0:T(8,128)(2,1)S(1)}, bf16[16,128,128]{2,1,0:T(8,128)(2,1)S(1)}, u32[]{:S(2)}, u32[]{:S(2)}) collective-permute-start(bf16[16,128,128]{2,1,0:T(8,128)(2,1)S(1)} %bitcast.7), channel_id=1, source_target_pairs={{0,8},{8,0},{1,9},{9,1},{2,10},{10,2},{3,11},{11,3},{4,12},{12,4},... | collective-permute-start | bytes 1572872 | tf_op jit(solution)/shard_map/ppermute | solution.py:377
  55.2 1.9 %collective-permute-done.1.got_ref = bf16[16,128,128]{2,1,0:T(8,128)(2,1)S(1)} collective-permute-done((bf16[16,128,128]{2,1,0:T(8,128)(2,1)S(1)}, bf16[16,128,128]{2,1,0:T(8,128)(2,1)S(1)}, u32[]{:S(2)}, u32[]{:S(2)}) %collective-permute-start.1) | collective-permute-done | bytes 524320 | tf_op jit(solution)/shard_map/ppermute | solution.py:377
  57.1 0.6 forward.1
  57.7 3.4 %collective-permute-start.2 = (bf16[128,128]{1,0:T(8,128)(2,1)S(1)}, bf16[128,128]{1,0:T(8,128)(2,1)S(1)}, u32[]{:S(2)}, u32[]{:S(2)}) collective-permute-start(bf16[128,128]{1,0:T(8,128)(2,1)S(1)} %get-tuple-element.35), channel_id=1, source_target_pairs={{0,16},{16,0},{1,17},{17,1},{2,18},{18,2},{3,19},{19,3},{4,20},{20... | collective-permute-start | bytes 98312 | tf_op jit(solution)/shard_map/ppermute | solution.py:377
  61.1 0.0 copy-done.2
  61.1 1.9 %backward.1 = (bf16[2,8,2,48,128]{4,3,2,1,0:T(8,128)(2,1)S(1)}, f32[2,8,2,48,128]{4,3,2,1,0:T(8,128)S(1)}) custom-call(s32[64]{0:T(128)S(1)} %copy-done.2, bf16[16,32,2048]{2,1,0:T(8,128)(2,1)S(1)} %all-to-all-done.both_ref, f32[256,128]{1,0:T(8,128)S(1)} %get-tuple-element.45.acts_ref, bf16[2048,128]{1,0:T(8,128)(2,1)S(1)} %get-tuple-element.36.down_ref.down), custom_call_target="tpu_custom_call" | custom-call | flops 8800000000 | bytes 29600000 | tf_op jit(solution)/shard_map/backward/pallas_call | solution.py:259
  63.0 1.9 %collective-permute-start.6 = (bf16[2,8,2,48,128]{4,3,2,1,0:T(8,128)(2,1)S(1)}, bf16[2,8,2,48,128]{4,3,2,1,0:T(8,128)(2,1)S(1)}, u32[]{:S(2)}, u32[]{:S(2)}) collective-permute-start(bf16[2,8,2,48,128]{4,3,2,1,0:T(8,128)(2,1)S(1)} %get-tuple-element.47), channel_id=1, source_target_pairs={{0,8},{8,0},{1,9},{9,1},{2,10},{10,2},{3,11},{11,3},{4,12},{12,4},... | collective-permute-start | bytes 1179656 | tf_op jit(solution)/shard_map/ppermute | solution.py:377
  65.0 0.0 collective-permute-done.2.got_ref
  65.0 0.4 partial_rows.1
  65.3 1.3 %collective-permute-done.6.got_ref = bf16[2,8,2,48,128]{4,3,2,1,0:T(8,128)(2,1)S(1)} collective-permute-done((bf16[2,8,2,48,128]{4,3,2,1,0:T(8,128)(2,1)S(1)}, bf16[2,8,2,48,128]{4,3,2,1,0:T(8,128)(2,1)S(1)}, u32[]{:S(2)}, u32[]{:S(2)}) %collective-permute-start.6) | collective-permute-done | bytes 393248 | tf_op jit(solution)/shard_map/ppermute | solution.py:377
  66.7 0.1 add_halves.5
  66.7 1.9 %collective-permute-start.7 = (bf16[1,8,2,48,128]{4,3,2,1,0:T(8,128)(2,1)S(1)}, bf16[1,8,2,48,128]{4,3,2,1,0:T(8,128)(2,1)S(1)}, u32[]{:S(2)}, u32[]{:S(2)}) collective-permute-start(bf16[1,8,2,48,128]{4,3,2,1,0:T(8,128)(2,1)S(1)} %get-tuple-element.50), channel_id=1, source_target_pairs={{0,32},{32,0},{1,33},{33,1},{2,34},{34,2},{3,35},{35,3},{4,36},{36... | collective-permute-start | bytes 589832 | tf_op jit(solution)/shard_map/ppermute | solution.py:377
  68.6 3.4 %collective-permute-start.3 = (bf16[4,16,2048]{2,1,0:T(8,128)(2,1)S(1)}, bf16[4,16,2048]{2,1,0:T(8,128)(2,1)S(1)}, u32[]{:S(2)}, u32[]{:S(2)}) collective-permute-start(bf16[4,16,2048]{2,1,0:T(8,128)(2,1)S(1)} %get-tuple-element.38), channel_id=1, source_target_pairs={{0,2},{1,3},{2,0},{3,1},{4,6},{5,7},{6,4},{7,5},{8,10},{9,11},{10,... | collective-permute-start | bytes 786440 | tf_op jit(solution)/shard_map/ppermute | solution.py:377
  72.0 3.5 %collective-permute-done.7 = bf16[1,8,2,48,128]{4,3,2,1,0:T(8,128)(2,1)S(1)} collective-permute-done((bf16[1,8,2,48,128]{4,3,2,1,0:T(8,128)(2,1)S(1)}, bf16[1,8,2,48,128]{4,3,2,1,0:T(8,128)(2,1)S(1)}, u32[]{:S(2)}, u32[]{:S(2)}) %collective-permute-start.7) | collective-permute-done | bytes 196640 | tf_op jit(solution)/shard_map/ppermute | solution.py:377
  75.6 0.7 add_convert_fusion
  76.3 6.8 %all-to-all-start.1 = ((bf16[16,48,128]{2,1,0:T(8,128)(2,1)}), bf16[16,48,128]{2,1,0:T(8,128)(2,1)S(1)}, u32[]{:S(2)}, u32[]{:S(2)}) async-start(bf16[16,48,128]{2,1,0:T(8,128)(2,1)} %bitcast.6), calls=%async_computation.1 | async-start | bytes 393216 | tf_op jit(solution)/shard_map/all_to_all | solution.py:403
  83.1 0.0 collective-permute-done.3.got_ref
  83.2 0.0 copy-start
  83.2 0.0 copy-start.1
  83.2 2.8 %collective-permute-start.4 = (bf16[2,16,2048]{2,1,0:T(8,128)(2,1)S(1)}, bf16[2,16,2048]{2,1,0:T(8,128)(2,1)S(1)}, u32[]{:S(2)}, u32[]{:S(2)}) collective-permute-start(bf16[2,16,2048]{2,1,0:T(8,128)(2,1)S(1)} %get-tuple-element.40), channel_id=1, source_target_pairs={{0,1},{1,0},{2,3},{3,2},{4,5},{5,4},{6,7},{7,6},{8,9},{9,8},{10,11... | collective-permute-start | bytes 393224 | tf_op jit(solution)/shard_map/ppermute | solution.py:377
  86.0 4.1 %collective-permute-done.4.got_ref = bf16[2,16,2048]{2,1,0:T(8,128)(2,1)S(1)} collective-permute-done((bf16[2,16,2048]{2,1,0:T(8,128)(2,1)S(1)}, bf16[2,16,2048]{2,1,0:T(8,128)(2,1)S(1)}, u32[]{:S(2)}, u32[]{:S(2)}) %collective-permute-start.4) | collective-permute-done | bytes 131104 | tf_op jit(solution)/shard_map/ppermute | solution.py:377
  90.1 4.8 %collective-permute-start.5 = (bf16[1,16,2048]{2,1,0:T(8,128)(2,1)S(1)}, bf16[1,16,2048]{2,1,0:T(8,128)(2,1)S(1)}, u32[]{:S(2)}, u32[]{:S(2)}) collective-permute-start(bf16[1,16,2048]{2,1,0:T(8,128)(2,1)S(1)} %get-tuple-element.42), channel_id=1, source_target_pairs={{0,4},{4,0},{1,5},{5,1},{2,6},{6,2},{3,7},{7,3},{8,12},{12,8},{9,1... | collective-permute-start | bytes 196616 | tf_op jit(solution)/shard_map/ppermute | solution.py:377
  94.9 3.1 %collective-permute-done.5.got_ref = bf16[1,16,2048]{2,1,0:T(8,128)(2,1)S(1)} collective-permute-done((bf16[1,16,2048]{2,1,0:T(8,128)(2,1)S(1)}, bf16[1,16,2048]{2,1,0:T(8,128)(2,1)S(1)}, u32[]{:S(2)}, u32[]{:S(2)}) %collective-permute-start.5) | collective-permute-done | bytes 65568 | tf_op jit(solution)/shard_map/ppermute | solution.py:377
  98.0 0.0 copy-done
  98.0 0.0 copy-done.1
  98.0 1.1 %mix.1 = bf16[128,2048]{1,0:T(8,128)(2,1)} custom-call(f32[1,16,2048]{2,1,0:T(8,128)S(1)} %get-tuple-element.41.own_ref, bf16[1,16,2048]{2,1,0:T(8,128)(2,1)S(1)} %collective-permute-done.5.got_ref, bf16[16,128]{1,0:T(8,128)(2,1)S(1)} %copy-done.1, f32[16,128]{1,0:T(8,128)S(1)} %copy-done), custom_call_target="tpu_custom_call" | custom-call | flops 1100000000 | bytes 3700000 | tf_op jit(solution)/shard_map/mix/pallas_call | solution.py:335
  99.2 2.1 %all-to-all-done.1.blocks_ref = bf16[16,48,128]{2,1,0:T(8,128)(2,1)S(1)} async-done(((bf16[16,48,128]{2,1,0:T(8,128)(2,1)}), bf16[16,48,128]{2,1,0:T(8,128)(2,1)S(1)}, u32[]{:S(2)}, u32[]{:S(2)}) %all-to-all-start.1) | async-done | bytes 196640 | tf_op jit(solution)/shard_map/all_to_all | solution.py:403
  101.3 0.7 finish.1
  (2 shorter events, 0.1 us)
Async XLA Ops:
  1.4 6.4 %collective-permute-start = (bf16[3,32,128]{2,1,0:T(8,128)(2,1)S(1)}, bf16[3,32,128]{2,1,0:T(8,128)(2,1)S(1)}, u32[]{:S(2)}, u32[]{:S(2)}) collective-permute-start(bf16[3,32,128]{2,1,0:T(8,128)(2,1)S(1)} %pad_maximum_fusion.own_ref), channel_id=1, source_target_pairs={{0,16},{16,0},{1,17},{17,1},{2,18},{18,2},{3,19},{19,3},{4,20},{20... | collective-permute-start | bytes 73736 | tf_op jit(solution)/shard_map/ppermute | solution.py:377
  7.8 45.5 %all-to-all-start = ((bf16[16,32,2048]{2,1,0:T(8,128)(2,1)}), bf16[16,32,2048]{2,1,0:T(8,128)(2,1)S(1)}, u32[]{:S(2)}, u32[]{:S(2)}) async-start(bf16[16,32,2048]{2,1,0:T(8,128)(2,1)} %get-tuple-element.31), calls=%async_computation | async-start | bytes 4194304 | tf_op jit(solution)/shard_map/all_to_all | solution.py:388
  16.5 44.5 %copy-start.2 = (s32[64]{0:T(128)S(1)}, s32[64]{0:T(128)}, u32[]{:S(2)}) copy-start(s32[64]{0:T(128)} %join_ref.1) | copy-start | bytes 772
  53.3 3.8 %collective-permute-start.1 = (bf16[16,128,128]{2,1,0:T(8,128)(2,1)S(1)}, bf16[16,128,128]{2,1,0:T(8,128)(2,1)S(1)}, u32[]{:S(2)}, u32[]{:S(2)}) collective-permute-start(bf16[16,128,128]{2,1,0:T(8,128)(2,1)S(1)} %bitcast.7), channel_id=1, source_target_pairs={{0,8},{8,0},{1,9},{9,1},{2,10},{10,2},{3,11},{11,3},{4,12},{12,4},... | collective-permute-start | bytes 1572872 | tf_op jit(solution)/shard_map/ppermute | solution.py:377
  57.7 7.3 %collective-permute-start.2 = (bf16[128,128]{1,0:T(8,128)(2,1)S(1)}, bf16[128,128]{1,0:T(8,128)(2,1)S(1)}, u32[]{:S(2)}, u32[]{:S(2)}) collective-permute-start(bf16[128,128]{1,0:T(8,128)(2,1)S(1)} %get-tuple-element.35), channel_id=1, source_target_pairs={{0,16},{16,0},{1,17},{17,1},{2,18},{18,2},{3,19},{19,3},{4,20},{20... | collective-permute-start | bytes 98312 | tf_op jit(solution)/shard_map/ppermute | solution.py:377
  63.0 3.6 %collective-permute-start.6 = (bf16[2,8,2,48,128]{4,3,2,1,0:T(8,128)(2,1)S(1)}, bf16[2,8,2,48,128]{4,3,2,1,0:T(8,128)(2,1)S(1)}, u32[]{:S(2)}, u32[]{:S(2)}) collective-permute-start(bf16[2,8,2,48,128]{4,3,2,1,0:T(8,128)(2,1)S(1)} %get-tuple-element.47), channel_id=1, source_target_pairs={{0,8},{8,0},{1,9},{9,1},{2,10},{10,2},{3,11},{11,3},{4,12},{12,4},... | collective-permute-start | bytes 1179656 | tf_op jit(solution)/shard_map/ppermute | solution.py:377
  66.7 8.8 %collective-permute-start.7 = (bf16[1,8,2,48,128]{4,3,2,1,0:T(8,128)(2,1)S(1)}, bf16[1,8,2,48,128]{4,3,2,1,0:T(8,128)(2,1)S(1)}, u32[]{:S(2)}, u32[]{:S(2)}) collective-permute-start(bf16[1,8,2,48,128]{4,3,2,1,0:T(8,128)(2,1)S(1)} %get-tuple-element.50), channel_id=1, source_target_pairs={{0,32},{32,0},{1,33},{33,1},{2,34},{34,2},{3,35},{35,3},{4,36},{36... | collective-permute-start | bytes 589832 | tf_op jit(solution)/shard_map/ppermute | solution.py:377
  68.6 14.5 %collective-permute-start.3 = (bf16[4,16,2048]{2,1,0:T(8,128)(2,1)S(1)}, bf16[4,16,2048]{2,1,0:T(8,128)(2,1)S(1)}, u32[]{:S(2)}, u32[]{:S(2)}) collective-permute-start(bf16[4,16,2048]{2,1,0:T(8,128)(2,1)S(1)} %get-tuple-element.38), channel_id=1, source_target_pairs={{0,2},{1,3},{2,0},{3,1},{4,6},{5,7},{6,4},{7,5},{8,10},{9,11},{10,... | collective-permute-start | bytes 786440 | tf_op jit(solution)/shard_map/ppermute | solution.py:377
  76.3 25.0 %all-to-all-start.1 = ((bf16[16,48,128]{2,1,0:T(8,128)(2,1)}), bf16[16,48,128]{2,1,0:T(8,128)(2,1)S(1)}, u32[]{:S(2)}, u32[]{:S(2)}) async-start(bf16[16,48,128]{2,1,0:T(8,128)(2,1)} %bitcast.6), calls=%async_computation.1 | async-start | bytes 393216 | tf_op jit(solution)/shard_map/all_to_all | solution.py:403
  83.2 14.9 %copy-start = (f32[16,128]{1,0:T(8,128)S(1)}, f32[16,128]{1,0:T(8,128)}, u32[]{:S(2)}) copy-start(f32[16,128]{1,0:T(8,128)} %get-tuple-element.44.slot_weight_ref) | copy-start | bytes 24580
  83.2 14.8 %copy-start.1 = (bf16[16,128]{1,0:T(8,128)(2,1)S(1)}, bf16[16,128]{1,0:T(8,128)(2,1)}, u32[]{:S(2)}) copy-start(bf16[16,128]{1,0:T(8,128)(2,1)} %get-tuple-element.43.chooser_ref) | copy-start | bytes 12292
  83.2 6.9 %collective-permute-start.4 = (bf16[2,16,2048]{2,1,0:T(8,128)(2,1)S(1)}, bf16[2,16,2048]{2,1,0:T(8,128)(2,1)S(1)}, u32[]{:S(2)}, u32[]{:S(2)}) collective-permute-start(bf16[2,16,2048]{2,1,0:T(8,128)(2,1)S(1)} %get-tuple-element.40), channel_id=1, source_target_pairs={{0,1},{1,0},{2,3},{3,2},{4,5},{5,4},{6,7},{7,6},{8,9},{9,8},{10,11... | collective-permute-start | bytes 393224 | tf_op jit(solution)/shard_map/ppermute | solution.py:377
  90.1 7.9 %collective-permute-start.5 = (bf16[1,16,2048]{2,1,0:T(8,128)(2,1)S(1)}, bf16[1,16,2048]{2,1,0:T(8,128)(2,1)S(1)}, u32[]{:S(2)}, u32[]{:S(2)}) collective-permute-start(bf16[1,16,2048]{2,1,0:T(8,128)(2,1)S(1)} %get-tuple-element.42), channel_id=1, source_target_pairs={{0,4},{4,0},{1,5},{5,1},{2,6},{6,2},{3,7},{7,3},{8,12},{12,8},{9,1... | collective-permute-start | bytes 196616 | tf_op jit(solution)/shard_map/ppermute | solution.py:377

commit v9 on v8

--- a/solution.py
+++ b/solution.py
@@ -6,8 +6,8 @@
 from jax.sharding import Mesh
 from jax.sharding import PartitionSpec as P
 
-AXES = ("zh", "zl", "y", "c", "h", "x")
-Z = ("zh", "zl")
+AXES = ("zh", "zm", "zl", "y", "c", "h", "x")
+Z = ("zh", "zm", "zl")
 PLANE = ("y", "h", "x")
 HBM = pl.BlockSpec(memory_space=pltpu.HBM)
 ROW_DIMS = (((0,), (0,)), ((), ()))
@@ -240,22 +240,23 @@
     for chip in range(chips):
         for k in range(2):
             base = (chip * 2 + k) * 2 * rows
-            away = jnp.bitwise_xor(chip % 2, lax.rem(z, 2))
+            away = jnp.bitwise_xor(chip % 2, lax.rem(z, 2)) * 2
+            away += jnp.bitwise_xor(chip // 2 % 2, lax.rem(z // 2, 2))
             for which, ref in ((c, keep_ref), (1 - c, send_ref)):
                 at = pl.multiple_of(base + which * rows, rows)
-                ref[away, chip // 2, k, :rows, :] = terms[0, pl.ds(at, rows), :].astype(ref.dtype)
+                ref[away, chip // 4, k, :rows, :] = terms[0, pl.ds(at, rows), :].astype(ref.dtype)
                 packed = jnp.where(
                     low,
                     terms[1, pl.ds(at, half_rows), :],
                     terms[1, pl.ds(at + half_rows, half_rows), :],
                 )
-                ref[away, chip // 2, k, rows:, :] = packed.astype(ref.dtype)
+                ref[away, chip // 4, k, rows:, :] = packed.astype(ref.dtype)
 
 
 def backward(join, both, acts, down, chips):
     depth, width = down.shape
     rows = depth // chips // 4
-    chunk = (2, chips // 2, 2, rows // 2 * 3, width)
+    chunk = (4, chips // 4, 2, rows // 2 * 3, width)
     return pl.pallas_call(
         backward_kernel,
         out_shape=(
@@ -266,7 +267,7 @@
         out_specs=tuple(whole(2)),
         scratch_shapes=[pltpu.VMEM((2, depth, width), jnp.float32)],
         compiler_params=params(16),
-        cost_estimate=cost(8),
+        cost_estimate=cost(0.5),
         name="backward",
     )(join, both, acts, down)
 
@@ -296,7 +297,7 @@
         out_specs=tuple(whole(2)),
         scratch_shapes=[pltpu.VMEM((peers, slots, depth), jnp.float32)],
         compiler_params=params(8),
-        cost_estimate=cost(5),
+        cost_estimate=cost(0.5),
         name="partial_rows",
     )(keep, got, down)
 
@@ -307,7 +308,7 @@
     theirs_ref[...] = (keep_ref[half:] + got_ref[half:].astype(jnp.float32)).astype(jnp.bfloat16)
 
 
-def add_halves(keep, got, lasts):
+def add_halves(keep, got):
     half = (keep.shape[0] // 2, *keep.shape[1:])
     return pl.pallas_call(
         add_kernel,
@@ -318,7 +319,7 @@
         in_specs=whole(2),
         out_specs=tuple(whole(2)),
         compiler_params=params(8),
-        cost_estimate=cost(lasts),
+        cost_estimate=cost(0.5),
         name="add_halves",
     )(keep, got)
 
@@ -338,7 +339,7 @@
         in_specs=whole(4),
         out_specs=whole(1)[0],
         compiler_params=params(8),
-        cost_estimate=cost(1),
+        cost_estimate=cost(0.5),
         name="mix",
     )(own, got, chooser, slot_weight)
 
@@ -395,22 +396,24 @@
     from_core = swapped(send, "c")
     partial, partial_send = partial_rows(hidden, hidden_got, down, lax.axis_size(("h", "x")))
     partial_got = swapped(partial_send, "x", 2)
-    from_core, _ = lax.optimization_barrier((from_core, partial_send))
-    keep, to_pair = add_halves(keep, from_core, 0.4)
+    keep, to_pair = add_halves(keep, from_core)
     from_pair = swapped(to_pair, "zl")
-    pair_sum = (keep + from_pair.astype(jnp.float32)).astype(jnp.bfloat16)
+    from_pair, _ = lax.optimization_barrier((from_pair, partial_send))
+    keep, to_far = add_halves(keep, from_pair)
+    from_far = swapped(to_far, "zm")
+    pair_sum = (keep + from_far.astype(jnp.float32)).astype(jnp.bfloat16)
     pair_sum = pair_sum.reshape(-1, *pair_sum.shape[3:])
     pieces = lax.all_to_all(pair_sum, ("zh", "y"), 0, 0, tiled=True)
-    partial, partial_send = add_halves(partial, partial_got, 2)
-    partial, partial_send = add_halves(partial, swapped(partial_send, "x"), 1)
+    partial, partial_send = add_halves(partial, partial_got)
+    partial, partial_send = add_halves(partial, swapped(partial_send, "x"))
     mixed = mix(partial, swapped(partial_send, "h"), chooser, slot_weight)
     return (mixed, *finish(pieces))
 
 
 def solution(mesh):
     experts = mesh.shape["expert"]
-    split = Mesh(mesh.devices.reshape(-1, 2, 2, 2, 2, experts // 2), AXES)
-    dp = ("zh", "zl", "y", "c")
+    split = Mesh(mesh.devices.reshape(-1, 2, 2, 2, 2, 2, experts // 2), AXES)
+    dp = (*Z, "y", "c")
     tok, weight = P(AXES, None), P(dp, ("h", "x"))
     return jax.shard_map(
         per_device,

time: 103 us -> 107 us (1.039)
  starting transfers between devices: 39.1 us -> 42 us
  waiting for transfers between devices: 16 us -> 17.2 us
    ppermute x8 -> x9, waiting for transfers between devices: 13.9 us -> 17.2 us  [swapped(): return lax.ppermute(part, axis, [(i, i ^ distance) for i in range(size)])]
    all_to_all x1, waiting for transfers between devices: 2.08 us -> 0.01 us  [per_device(): pieces = lax.all_to_all(pair_sum, ('zh', 'y'), 0, 0, tiled=True)]
    ppermute x8 -> x9, starting transfers between devices: 23.5 us -> 25.5 us  [swapped(): return lax.ppermute(part, axis, [(i, i ^ distance) for i in range(size)])]
  transfers between devices with their start and end apart: 10 -> 11, of which waited for: 6 -> 7; matrix products, arithmetic and copies ran while one was open for 1% -> 1% of each run, Pallas kernels for 6% -> 4%
where the time goes in v9:
time: 107 us; the launch traced here: 106 us
  starting transfers between devices  42 us (39%)
  blocking collectives  36.8 us (34%)
  waiting for transfers between devices  17.2 us (16%)
  Pallas kernels  7.86 us (7%)
  other arithmetic  1.4 us (1%)
    all_gather x1, blocking collectives, per_device(): along = lax.all_gather(packed, Z, axis=0, tiled=False)  36.8 us
    ppermute x9, starting transfers between devices, swapped(): return lax.ppermute(part, axis, [(i, i ^ distance) for i in range(size)])  25.5 us
    ppermute x9, waiting for transfers between devices, swapped(): return lax.ppermute(part, axis, [(i, i ^ distance) for i in range(size)])  17.2 us
    all_to_all x1, starting transfers between devices, per_device(): rows_in = lax.all_to_all(copies, PLANE, 0, 0, tiled=True)  8.71 us
    all_to_all x1, starting transfers between devices, per_device(): pieces = lax.all_to_all(pair_sum, ('zh', 'y'), 0, 0, tiled=True)  7.76 us
    pallas_call x1, Pallas kernels, route(): pl.pallas_call(route_kernel, out_shape=(jax.ShapeDtypeStruct((peers, 2 *...  2.89 us
  transfers between devices with their start and end apart: 11, of which 7 were waited for; matrix products, arithmetic and copies ran while one was open for 1% of the time, Pallas kernels for 4%

profile of v9, /device:TPU:6, one launch (start us, length us, event | category | flops | bytes accessed | tf_op | source)
XLA Modules:
  0.0 106.0 jit_solution(1520512882104489166)
XLA Ops:
  0.6 0.7 pad_maximum_fusion.own_ref
  1.4 3.5 %collective-permute-start = (bf16[3,32,128]{2,1,0:T(8,128)(2,1)S(1)}, bf16[3,32,128]{2,1,0:T(8,128)(2,1)S(1)}, u32[]{:S(2)}, u32[]{:S(2)}) collective-permute-start(bf16[3,32,128]{2,1,0:T(8,128)(2,1)S(1)} %pad_maximum_fusion.own_ref), channel_id=1, source_target_pairs={{0,16},{16,0},{1,17},{17,1},{2,18},{18,2},{3,19},{19,3},{4,20},{20... | collective-permute-start | bytes 73736 | tf_op jit(solution)/shard_map/ppermute | solution.py:378
  4.8 2.9 %route.1 = (bf16[16,32,2048]{2,1,0:T(8,128)(2,1)}, bf16[16,128]{1,0:T(8,128)(2,1)}, f32[16,128]{1,0:T(8,128)}) custom-call(s32[8,128]{1,0:T(8,128)} %bitcast.12, f32[8,128]{1,0:T(8,128)} %bitcast.13, bf16[128,2048]{1,0:T(8,128)(2,1)} %tokens_ref.1, bf16[128,2048]{1,0:T(8,128)(2,1)} %cot_ref.1), custom_call_target="tpu_custom_call" | custom-call | tf_op jit(solution)/shard_map/route/pallas_call | solution.py:98
  7.7 0.0 collective-permute-done.got_ref
  7.8 0.1 pack_shards.1
  7.8 8.7 %all-to-all-start = ((bf16[16,32,2048]{2,1,0:T(8,128)(2,1)}), bf16[16,32,2048]{2,1,0:T(8,128)(2,1)S(1)}, u32[]{:S(2)}, u32[]{:S(2)}) async-start(bf16[16,32,2048]{2,1,0:T(8,128)(2,1)} %get-tuple-element.33), calls=%async_computation | async-start | bytes 4194304 | tf_op jit(solution)/shard_map/all_to_all | solution.py:389
  16.5 0.0 copy-start
  16.6 36.8 %all-gather = bf16[2048,128]{1,0:T(8,128)(2,1)S(1)} all-gather(bf16[128,128]{1,0:T(8,128)(2,1)S(1)} %pack_shards.1), channel_id=2, replica_groups=mesh['zh'=4,'zm'=2,'zl'=2,'y'=2,'c'=2,'h'=2,'x'=4] {'zh','zm','zl'}, dimensions={0}, use_global_device_ids=true | all-gather | bytes 557056 | tf_op jit(solution)/shard_map/all_gather | solution.py:390
  53.3 0.0 all-to-all-done.both_ref
  53.3 1.9 %collective-permute-start.1 = (bf16[16,128,128]{2,1,0:T(8,128)(2,1)S(1)}, bf16[16,128,128]{2,1,0:T(8,128)(2,1)S(1)}, u32[]{:S(2)}, u32[]{:S(2)}) collective-permute-start(bf16[16,128,128]{2,1,0:T(8,128)(2,1)S(1)} %bitcast.7), channel_id=1, source_target_pairs={{0,8},{8,0},{1,9},{9,1},{2,10},{10,2},{3,11},{11,3},{4,12},{12,4},... | collective-permute-start | bytes 1572872 | tf_op jit(solution)/shard_map/ppermute | solution.py:378
  55.2 1.9 %collective-permute-done.1.got_ref = bf16[16,128,128]{2,1,0:T(8,128)(2,1)S(1)} collective-permute-done((bf16[16,128,128]{2,1,0:T(8,128)(2,1)S(1)}, bf16[16,128,128]{2,1,0:T(8,128)(2,1)S(1)}, u32[]{:S(2)}, u32[]{:S(2)}) %collective-permute-start.1) | collective-permute-done | bytes 524320 | tf_op jit(solution)/shard_map/ppermute | solution.py:378
  57.1 0.6 forward.1
  57.7 0.0 copy-done
  57.7 1.9 %backward.1 = (bf16[4,4,2,48,128]{4,3,2,1,0:T(8,128)(2,1)S(1)}, f32[4,4,2,48,128]{4,3,2,1,0:T(8,128)S(1)}) custom-call(s32[64]{0:T(128)S(1)} %copy-done, bf16[16,32,2048]{2,1,0:T(8,128)(2,1)S(1)} %all-to-all-done.both_ref, f32[256,128]{1,0:T(8,128)S(1)} %get-tuple-element.47.acts_ref, bf16[2048,128]{1,0:T(8,128)(2,1)S(1)} %get-tuple-element.38.down_ref.down), custom_call_target="tpu_custom_call" | custom-call | flops 550000000 | bytes 1850000 | tf_op jit(solution)/shard_map/backward/pallas_call | solution.py:260
  59.6 2.0 %collective-permute-start.6 = (bf16[4,4,2,48,128]{4,3,2,1,0:T(8,128)(2,1)S(1)}, bf16[4,4,2,48,128]{4,3,2,1,0:T(8,128)(2,1)S(1)}, u32[]{:S(2)}, u32[]{:S(2)}) collective-permute-start(bf16[4,4,2,48,128]{4,3,2,1,0:T(8,128)(2,1)S(1)} %get-tuple-element.49), channel_id=1, source_target_pairs={{0,8},{8,0},{1,9},{9,1},{2,10},{10,2},{3,11},{11,3},{4,12},{12,4},... | collective-permute-start | bytes 1179656 | tf_op jit(solution)/shard_map/ppermute | solution.py:378
  61.7 1.6 %collective-permute-done.6.got_ref = bf16[4,4,2,48,128]{4,3,2,1,0:T(8,128)(2,1)S(1)} collective-permute-done((bf16[4,4,2,48,128]{4,3,2,1,0:T(8,128)(2,1)S(1)}, bf16[4,4,2,48,128]{4,3,2,1,0:T(8,128)(2,1)S(1)}, u32[]{:S(2)}, u32[]{:S(2)}) %collective-permute-start.6) | collective-permute-done | bytes 393248 | tf_op jit(solution)/shard_map/ppermute | solution.py:378
  63.3 0.1 add_halves.6
  63.3 1.9 %collective-permute-start.7 = (bf16[2,4,2,48,128]{4,3,2,1,0:T(8,128)(2,1)S(1)}, bf16[2,4,2,48,128]{4,3,2,1,0:T(8,128)(2,1)S(1)}, u32[]{:S(2)}, u32[]{:S(2)}) collective-permute-start(bf16[2,4,2,48,128]{4,3,2,1,0:T(8,128)(2,1)S(1)} %get-tuple-element.51), channel_id=1, source_target_pairs={{0,32},{32,0},{1,33},{33,1},{2,34},{34,2},{3,35},{35,3},{4,36},{36... | collective-permute-start | bytes 589832 | tf_op jit(solution)/shard_map/ppermute | solution.py:378
  65.3 3.4 %collective-permute-start.2 = (bf16[128,128]{1,0:T(8,128)(2,1)S(1)}, bf16[128,128]{1,0:T(8,128)(2,1)S(1)}, u32[]{:S(2)}, u32[]{:S(2)}) collective-permute-start(bf16[128,128]{1,0:T(8,128)(2,1)S(1)} %get-tuple-element.37), channel_id=1, source_target_pairs={{0,16},{16,0},{1,17},{17,1},{2,18},{18,2},{3,19},{19,3},{4,20},{20... | collective-permute-start | bytes 98312 | tf_op jit(solution)/shard_map/ppermute | solution.py:378
  68.6 2.4 %collective-permute-done.2.got_ref = bf16[128,128]{1,0:T(8,128)(2,1)S(1)} collective-permute-done((bf16[128,128]{1,0:T(8,128)(2,1)S(1)}, bf16[128,128]{1,0:T(8,128)(2,1)S(1)}, u32[]{:S(2)}, u32[]{:S(2)}) %collective-permute-start.2) | collective-permute-done | bytes 32800 | tf_op jit(solution)/shard_map/ppermute | solution.py:378
  71.1 0.4 partial_rows.1
  71.4 0.7 collective-permute-done.7.got_ref
  72.2 2.2 %collective-permute-start.8 = (bf16[1,4,2,48,128]{4,3,2,1,0:T(8,128)(2,1)S(1)}, bf16[1,4,2,48,128]{4,3,2,1,0:T(8,128)(2,1)S(1)}, u32[]{:S(2)}, u32[]{:S(2)}) collective-permute-start(bf16[1,4,2,48,128]{4,3,2,1,0:T(8,128)(2,1)S(1)} %get-tuple-element.54), channel_id=1, source_target_pairs={{0,64},{64,0},{1,65},{65,1},{2,66},{66,2},{3,67},{67,3},{4,68},{68... | collective-permute-start | bytes 294920 | tf_op jit(solution)/shard_map/ppermute | solution.py:378
  74.4 3.4 %collective-permute-start.3 = (bf16[4,16,2048]{2,1,0:T(8,128)(2,1)S(1)}, bf16[4,16,2048]{2,1,0:T(8,128)(2,1)S(1)}, u32[]{:S(2)}, u32[]{:S(2)}) collective-permute-start(bf16[4,16,2048]{2,1,0:T(8,128)(2,1)S(1)} %get-tuple-element.40), channel_id=1, source_target_pairs={{0,2},{1,3},{2,0},{3,1},{4,6},{5,7},{6,4},{7,5},{8,10},{9,11},{10,... | collective-permute-start | bytes 786440 | tf_op jit(solution)/shard_map/ppermute | solution.py:378
  77.8 3.4 %collective-permute-done.8 = bf16[1,4,2,48,128]{4,3,2,1,0:T(8,128)(2,1)S(1)} collective-permute-done((bf16[1,4,2,48,128]{4,3,2,1,0:T(8,128)(2,1)S(1)}, bf16[1,4,2,48,128]{4,3,2,1,0:T(8,128)(2,1)S(1)}, u32[]{:S(2)}, u32[]{:S(2)}) %collective-permute-start.8) | collective-permute-done | bytes 98336 | tf_op jit(solution)/shard_map/ppermute | solution.py:378
  81.1 0.7 add_convert_fusion
  81.8 0.0 copy-start.1
  81.8 0.0 copy-start.2
  81.8 7.8 %all-to-all-start.1 = ((bf16[8,48,128]{2,1,0:T(8,128)(2,1)}), bf16[8,48,128]{2,1,0:T(8,128)(2,1)S(1)}, u32[]{:S(2)}, u32[]{:S(2)}) async-start(bf16[8,48,128]{2,1,0:T(8,128)(2,1)} %bitcast.6), calls=%async_computation.1 | async-start | bytes 196608 | tf_op jit(solution)/shard_map/all_to_all | solution.py:406
  89.5 0.0 collective-permute-done.3.got_ref
  89.6 0.1 add_halves.4
  89.6 2.7 %collective-permute-start.4 = (bf16[2,16,2048]{2,1,0:T(8,128)(2,1)S(1)}, bf16[2,16,2048]{2,1,0:T(8,128)(2,1)S(1)}, u32[]{:S(2)}, u32[]{:S(2)}) collective-permute-start(bf16[2,16,2048]{2,1,0:T(8,128)(2,1)S(1)} %get-tuple-element.42), channel_id=1, source_target_pairs={{0,1},{1,0},{2,3},{3,2},{4,5},{5,4},{6,7},{7,6},{8,9},{9,8},{10,11... | collective-permute-start | bytes 393224 | tf_op jit(solution)/shard_map/ppermute | solution.py:378
  92.3 4.2 %collective-permute-done.4.got_ref = bf16[2,16,2048]{2,1,0:T(8,128)(2,1)S(1)} collective-permute-done((bf16[2,16,2048]{2,1,0:T(8,128)(2,1)S(1)}, bf16[2,16,2048]{2,1,0:T(8,128)(2,1)S(1)}, u32[]{:S(2)}, u32[]{:S(2)}) %collective-permute-start.4) | collective-permute-done | bytes 131104 | tf_op jit(solution)/shard_map/ppermute | solution.py:378
  96.5 4.6 %collective-permute-start.5 = (bf16[1,16,2048]{2,1,0:T(8,128)(2,1)S(1)}, bf16[1,16,2048]{2,1,0:T(8,128)(2,1)S(1)}, u32[]{:S(2)}, u32[]{:S(2)}) collective-permute-start(bf16[1,16,2048]{2,1,0:T(8,128)(2,1)S(1)} %get-tuple-element.44), channel_id=1, source_target_pairs={{0,4},{4,0},{1,5},{5,1},{2,6},{6,2},{3,7},{7,3},{8,12},{12,8},{9,1... | collective-permute-start | bytes 196616 | tf_op jit(solution)/shard_map/ppermute | solution.py:378
  101.1 3.1 %collective-permute-done.5.got_ref = bf16[1,16,2048]{2,1,0:T(8,128)(2,1)S(1)} collective-permute-done((bf16[1,16,2048]{2,1,0:T(8,128)(2,1)S(1)}, bf16[1,16,2048]{2,1,0:T(8,128)(2,1)S(1)}, u32[]{:S(2)}, u32[]{:S(2)}) %collective-permute-start.5) | collective-permute-done | bytes 65568 | tf_op jit(solution)/shard_map/ppermute | solution.py:378
  104.2 0.0 copy-done.1
  104.2 0.0 copy-done.2
  104.2 1.1 %mix.1 = bf16[128,2048]{1,0:T(8,128)(2,1)} custom-call(f32[1,16,2048]{2,1,0:T(8,128)S(1)} %get-tuple-element.43.own_ref, bf16[1,16,2048]{2,1,0:T(8,128)(2,1)S(1)} %collective-permute-done.5.got_ref, bf16[16,128]{1,0:T(8,128)(2,1)S(1)} %copy-done.2, f32[16,128]{1,0:T(8,128)S(1)} %copy-done.1), custom_call_target="tpu_custom_call" | custom-call | flops 550000000 | bytes 1850000 | tf_op jit(solution)/shard_map/mix/pallas_call | solution.py:336
  105.3 0.0 all-to-all-done.1.blocks_ref
  105.3 0.7 finish.1
  (2 shorter events, 0.1 us)
Async XLA Ops:
  1.4 6.4 %collective-permute-start = (bf16[3,32,128]{2,1,0:T(8,128)(2,1)S(1)}, bf16[3,32,128]{2,1,0:T(8,128)(2,1)S(1)}, u32[]{:S(2)}, u32[]{:S(2)}) collective-permute-start(bf16[3,32,128]{2,1,0:T(8,128)(2,1)S(1)} %pad_maximum_fusion.own_ref), channel_id=1, source_target_pairs={{0,16},{16,0},{1,17},{17,1},{2,18},{18,2},{3,19},{19,3},{4,20},{20... | collective-permute-start | bytes 73736 | tf_op jit(solution)/shard_map/ppermute | solution.py:378
  7.8 45.5 %all-to-all-start = ((bf16[16,32,2048]{2,1,0:T(8,128)(2,1)}), bf16[16,32,2048]{2,1,0:T(8,128)(2,1)S(1)}, u32[]{:S(2)}, u32[]{:S(2)}) async-start(bf16[16,32,2048]{2,1,0:T(8,128)(2,1)} %get-tuple-element.33), calls=%async_computation | async-start | bytes 4194304 | tf_op jit(solution)/shard_map/all_to_all | solution.py:389
  16.5 41.2 %copy-start = (s32[64]{0:T(128)S(1)}, s32[64]{0:T(128)}, u32[]{:S(2)}) copy-start(s32[64]{0:T(128)} %join_ref.1) | copy-start | bytes 772
  53.3 3.8 %collective-permute-start.1 = (bf16[16,128,128]{2,1,0:T(8,128)(2,1)S(1)}, bf16[16,128,128]{2,1,0:T(8,128)(2,1)S(1)}, u32[]{:S(2)}, u32[]{:S(2)}) collective-permute-start(bf16[16,128,128]{2,1,0:T(8,128)(2,1)S(1)} %bitcast.7), channel_id=1, source_target_pairs={{0,8},{8,0},{1,9},{9,1},{2,10},{10,2},{3,11},{11,3},{4,12},{12,4},... | collective-permute-start | bytes 1572872 | tf_op jit(solution)/shard_map/ppermute | solution.py:378
  59.6 3.6 %collective-permute-start.6 = (bf16[4,4,2,48,128]{4,3,2,1,0:T(8,128)(2,1)S(1)}, bf16[4,4,2,48,128]{4,3,2,1,0:T(8,128)(2,1)S(1)}, u32[]{:S(2)}, u32[]{:S(2)}) collective-permute-start(bf16[4,4,2,48,128]{4,3,2,1,0:T(8,128)(2,1)S(1)} %get-tuple-element.49), channel_id=1, source_target_pairs={{0,8},{8,0},{1,9},{9,1},{2,10},{10,2},{3,11},{11,3},{4,12},{12,4},... | collective-permute-start | bytes 1179656 | tf_op jit(solution)/shard_map/ppermute | solution.py:378
  63.3 8.8 %collective-permute-start.7 = (bf16[2,4,2,48,128]{4,3,2,1,0:T(8,128)(2,1)S(1)}, bf16[2,4,2,48,128]{4,3,2,1,0:T(8,128)(2,1)S(1)}, u32[]{:S(2)}, u32[]{:S(2)}) collective-permute-start(bf16[2,4,2,48,128]{4,3,2,1,0:T(8,128)(2,1)S(1)} %get-tuple-element.51), channel_id=1, source_target_pairs={{0,32},{32,0},{1,33},{33,1},{2,34},{34,2},{3,35},{35,3},{4,36},{36... | collective-permute-start | bytes 589832 | tf_op jit(solution)/shard_map/ppermute | solution.py:378
  65.3 5.8 %collective-permute-start.2 = (bf16[128,128]{1,0:T(8,128)(2,1)S(1)}, bf16[128,128]{1,0:T(8,128)(2,1)S(1)}, u32[]{:S(2)}, u32[]{:S(2)}) collective-permute-start(bf16[128,128]{1,0:T(8,128)(2,1)S(1)} %get-tuple-element.37), channel_id=1, source_target_pairs={{0,16},{16,0},{1,17},{17,1},{2,18},{18,2},{3,19},{19,3},{4,20},{20... | collective-permute-start | bytes 98312 | tf_op jit(solution)/shard_map/ppermute | solution.py:378
  72.2 8.9 %collective-permute-start.8 = (bf16[1,4,2,48,128]{4,3,2,1,0:T(8,128)(2,1)S(1)}, bf16[1,4,2,48,128]{4,3,2,1,0:T(8,128)(2,1)S(1)}, u32[]{:S(2)}, u32[]{:S(2)}) collective-permute-start(bf16[1,4,2,48,128]{4,3,2,1,0:T(8,128)(2,1)S(1)} %get-tuple-element.54), channel_id=1, source_target_pairs={{0,64},{64,0},{1,65},{65,1},{2,66},{66,2},{3,67},{67,3},{4,68},{68... | collective-permute-start | bytes 294920 | tf_op jit(solution)/shard_map/ppermute | solution.py:378
  74.4 15.2 %collective-permute-start.3 = (bf16[4,16,2048]{2,1,0:T(8,128)(2,1)S(1)}, bf16[4,16,2048]{2,1,0:T(8,128)(2,1)S(1)}, u32[]{:S(2)}, u32[]{:S(2)}) collective-permute-start(bf16[4,16,2048]{2,1,0:T(8,128)(2,1)S(1)} %get-tuple-element.40), channel_id=1, source_target_pairs={{0,2},{1,3},{2,0},{3,1},{4,6},{5,7},{6,4},{7,5},{8,10},{9,11},{10,... | collective-permute-start | bytes 786440 | tf_op jit(solution)/shard_map/ppermute | solution.py:378
  81.8 22.4 %copy-start.1 = (f32[16,128]{1,0:T(8,128)S(1)}, f32[16,128]{1,0:T(8,128)}, u32[]{:S(2)}) copy-start(f32[16,128]{1,0:T(8,128)} %get-tuple-element.46.slot_weight_ref) | copy-start | bytes 24580
  81.8 22.4 %copy-start.2 = (bf16[16,128]{1,0:T(8,128)(2,1)S(1)}, bf16[16,128]{1,0:T(8,128)(2,1)}, u32[]{:S(2)}) copy-start(bf16[16,128]{1,0:T(8,128)(2,1)} %get-tuple-element.45.chooser_ref) | copy-start | bytes 12292
  81.8 23.5 %all-to-all-start.1 = ((bf16[8,48,128]{2,1,0:T(8,128)(2,1)}), bf16[8,48,128]{2,1,0:T(8,128)(2,1)S(1)}, u32[]{:S(2)}, u32[]{:S(2)}) async-start(bf16[8,48,128]{2,1,0:T(8,128)(2,1)} %bitcast.6), calls=%async_computation.1 | async-start | bytes 196608 | tf_op jit(solution)/shard_map/all_to_all | solution.py:406
  89.6 6.9 %collective-permute-start.4 = (bf16[2,16,2048]{2,1,0:T(8,128)(2,1)S(1)}, bf16[2,16,2048]{2,1,0:T(8,128)(2,1)S(1)}, u32[]{:S(2)}, u32[]{:S(2)}) collective-permute-start(bf16[2,16,2048]{2,1,0:T(8,128)(2,1)S(1)} %get-tuple-element.42), channel_id=1, source_target_pairs={{0,1},{1,0},{2,3},{3,2},{4,5},{5,4},{6,7},{7,6},{8,9},{9,8},{10,11... | collective-permute-start | bytes 393224 | tf_op jit(solution)/shard_map/ppermute | solution.py:378
  96.5 7.7 %collective-permute-start.5 = (bf16[1,16,2048]{2,1,0:T(8,128)(2,1)S(1)}, bf16[1,16,2048]{2,1,0:T(8,128)(2,1)S(1)}, u32[]{:S(2)}, u32[]{:S(2)}) collective-permute-start(bf16[1,16,2048]{2,1,0:T(8,128)(2,1)S(1)} %get-tuple-element.44), channel_id=1, source_target_pairs={{0,4},{4,0},{1,5},{5,1},{2,6},{6,2},{3,7},{7,3},{8,12},{12,8},{9,1... | collective-permute-start | bytes 196616 | tf_op jit(solution)/shard_map/ppermute | solution.py:378

commit v10 on v8

--- a/solution.py
+++ b/solution.py
@@ -126,24 +126,25 @@
     low = lanes((rows, width)) < width // 2
     top = lax.axis_index("y") == 0
 
-    def half_of(left, right):
-        left, right = left.astype(jnp.float32), right.astype(jnp.float32)
-        if_top = jnp.where(low, left, halves_swapped(right))
-        return jnp.where(top, if_top, jnp.where(low, halves_swapped(left), right)).astype(jnp.bfloat16)
-
-    mine = half_of(own_ref[0], own_ref[1])
-    got = half_of(got_ref[0], got_ref[1])
-    packed_ref[:rows, :] = jnp.where(top, mine, got)
-    packed_ref[rows : 2 * rows, :] = jnp.where(top, got, mine)
-    packed_ref[2 * rows : 3 * rows, :] = jnp.where(top, own_ref[2], got_ref[2])
-    packed_ref[3 * rows :, :] = jnp.where(top, got_ref[2], own_ref[2])
+    def halves_of(ref):
+        left, right = ref[0].astype(jnp.float32), ref[1].astype(jnp.float32)
+        firsts = jnp.where(low, left, halves_swapped(right)).astype(jnp.bfloat16)
+        seconds = jnp.where(low, halves_swapped(left), right).astype(jnp.bfloat16)
+        return jnp.where(top, firsts, seconds), jnp.where(top, seconds, firsts)
+
+    for k, (own, got) in enumerate(
+        (*zip(halves_of(own_ref), halves_of(got_ref), strict=True), (own_ref[2], got_ref[2]))
+    ):
+        at = 2 * k * rows
+        packed_ref[at : at + rows, :] = jnp.where(top, own, got)
+        packed_ref[at + rows : at + 2 * rows, :] = jnp.where(top, got, own)
 
 
 def pack_shards(own, got):
     _, rows, width = own.shape
     return pl.pallas_call(
         pack_kernel,
-        out_shape=jax.ShapeDtypeStruct((4 * rows, width), own.dtype),
+        out_shape=jax.ShapeDtypeStruct((6 * rows, width), own.dtype),
         in_specs=whole(2),
         out_specs=whole(1)[0],
         compiler_params=params(2),
@@ -152,30 +153,43 @@
 
 
 def forward_kernel(
-    both_ref, own_ref, got_ref, hidden_send_ref, hidden_keep_ref, acts_ref, down, gate_up, hiddens
+    both_ref, own_ref, got_ref, mine_ref, theirs_ref, acts_ref, down, gate_up, others, hiddens, partials
 ):
     chips, rows, width = own_ref.shape
-    rows = rows // 4
+    rows = rows // 6
     half = width // 2
     peers, slots = both_ref.shape[0], both_ref.shape[1] // 2
+    depth = both_ref.shape[2]
     y, c = lax.axis_index("y"), lax.axis_index("c")
     for core, ref in ((c, own_ref), (1 - c, got_ref)):
         for chip in range(chips):
             for k in range(2):
                 at = pl.multiple_of((chip * 2 + k) * 2 * rows + core * rows, rows)
-                gate_up[pl.ds(at, rows), :] = ref[chip, k * rows : (k + 1) * rows, :]
-                down[pl.ds(at, rows), :] = ref[chip, (2 + k) * rows : (3 + k) * rows, :]
+                for part, target in enumerate((gate_up, others, down)):
+                    first = (2 * part + k) * rows
+                    target[pl.ds(at, rows), :] = ref[chip, first : first + rows, :]
     total = peers * slots
-    picked = both_ref[:, :slots, :].reshape(total, both_ref.shape[2])
+    picked = both_ref[:, :slots, :].reshape(total, depth)
     acts = jnp.dot(picked, gate_up[...], preferred_element_type=jnp.float32)
     acts_ref[...] = acts
     gate, up, _ = gate_and_up(acts)
+    hiddens[...] = gate * jax.nn.sigmoid(gate) * up
+    group_rows = total // 2
+    group = both_ref[pl.ds(y * (peers // 2), peers // 2), :slots, :].reshape(group_rows, depth)
+    gate, up, _ = gate_and_up(jnp.dot(group, others[...], preferred_element_type=jnp.float32))
     hidden = gate * jax.nn.sigmoid(gate) * up
-    mine = (lanes(acts.shape) >= half) == (y == 1)
-    hiddens[...] = jnp.where(mine, hidden, 0.0)
-    group_rows = total // 2
-    hidden_send_ref[...] = hiddens[pl.ds((1 - y) * group_rows, group_rows), :].astype(jnp.bfloat16)
-    hidden_keep_ref[...] = hiddens[pl.ds(y * group_rows, group_rows), :].astype(jnp.bfloat16)
+    mine = (lanes(hidden.shape) >= half) == (y == 1)
+    hidden = jnp.where(mine, hiddens[pl.ds(y * group_rows, group_rows), :], hidden)
+    partial = lax.dot_general(
+        hidden.astype(jnp.bfloat16), down[...], LANE_DIMS, preferred_element_type=jnp.float32
+    )
+    partials[...] = partial.reshape(partials.shape)
+    h, x = lax.axis_index("h"), lax.axis_index("x")
+    for high, ref in enumerate((mine_ref, theirs_ref)):
+        for low in range(2):
+            for row in range(2):
+                peer = jnp.bitwise_xor(h, row) * 4 + jnp.bitwise_xor(x, 2 * high + low)
+                ref[2 * low + row] = partials[peer].astype(ref.dtype)
 
 
 def gate_and_up(acts):
@@ -187,14 +201,14 @@
 
 def forward(both, own, got):
     peers, doubled, depth = both.shape
-    rows = peers * doubled // 2
+    slots = doubled // 2
+    rows = peers * slots
     width = own.shape[2]
-    hidden = jax.ShapeDtypeStruct((rows // 2, width), jnp.bfloat16)
     return pl.pallas_call(
         forward_kernel,
         out_shape=(
-            hidden,
-            hidden,
+            jax.ShapeDtypeStruct((peers // 4, slots, depth), jnp.float32),
+            jax.ShapeDtypeStruct((peers // 4, slots, depth), jnp.bfloat16),
             jax.ShapeDtypeStruct((rows, width), jnp.float32),
             jax.ShapeDtypeStruct((depth, width), jnp.bfloat16),
         ),
@@ -202,9 +216,11 @@
         out_specs=tuple(whole(4)),
         scratch_shapes=[
             pltpu.VMEM((depth, width), jnp.bfloat16),
+            pltpu.VMEM((depth, width), jnp.bfloat16),
             pltpu.VMEM((rows, width), jnp.float32),
+            pltpu.VMEM((peers // 2, slots, depth), jnp.float32),
         ],
-        compiler_params=params(12),
+        compiler_params=params(16),
         name="forward",
     )(both, own, got)
 
@@ -271,36 +287,6 @@
     )(join, both, acts, down)
 
 
-def partial_kernel(keep_ref, got_ref, down_ref, mine_ref, theirs_ref, partials):
-    partial = lax.dot_general(
-        keep_ref[...] + got_ref[...], down_ref[...], LANE_DIMS, preferred_element_type=jnp.float32
-    )
-    partials[...] = partial.reshape(partials.shape)
-    h, x = lax.axis_index("h"), lax.axis_index("x")
-    for high, ref in enumerate((mine_ref, theirs_ref)):
-        for low in range(2):
-            for row in range(2):
-                peer = jnp.bitwise_xor(h, row) * 4 + jnp.bitwise_xor(x, 2 * high + low)
-                ref[2 * low + row] = partials[peer].astype(ref.dtype)
-
-
-def partial_rows(keep, got, down, peers):
-    slots, depth = keep.shape[0] // peers, down.shape[0]
-    return pl.pallas_call(
-        partial_kernel,
-        out_shape=(
-            jax.ShapeDtypeStruct((peers // 2, slots, depth), jnp.float32),
-            jax.ShapeDtypeStruct((peers // 2, slots, depth), jnp.bfloat16),
-        ),
-        in_specs=whole(3),
-        out_specs=tuple(whole(2)),
-        scratch_shapes=[pltpu.VMEM((peers, slots, depth), jnp.float32)],
-        compiler_params=params(8),
-        cost_estimate=cost(5),
-        name="partial_rows",
-    )(keep, got, down)
-
-
 def add_kernel(keep_ref, got_ref, mine_ref, theirs_ref):
     half = mine_ref.shape[0]
     mine_ref[...] = keep_ref[:half] + got_ref[:half].astype(jnp.float32)
@@ -389,14 +375,10 @@
     along = lax.all_gather(packed, Z, axis=0, tiled=False)
     along, rows_in = lax.optimization_barrier((along, rows_in))
     other = swapped(along, "c")
-    hidden_send, hidden, acts, down = forward(rows_in, along, other)
-    hidden_got = swapped(hidden_send, "y")
+    partial, partial_send, acts, down = forward(rows_in, along, other)
+    partial_got = swapped(partial_send, "x", 2)
     send, keep = backward(join_groups, rows_in, acts, down, lax.axis_size(Z))
-    from_core = swapped(send, "c")
-    partial, partial_send = partial_rows(hidden, hidden_got, down, lax.axis_size(("h", "x")))
-    partial_got = swapped(partial_send, "x", 2)
-    from_core, _ = lax.optimization_barrier((from_core, partial_send))
-    keep, to_pair = add_halves(keep, from_core, 0.4)
+    keep, to_pair = add_halves(keep, swapped(send, "c"), 0.4)
     from_pair = swapped(to_pair, "zl")
     pair_sum = (keep + from_pair.astype(jnp.float32)).astype(jnp.bfloat16)
     pair_sum = pair_sum.reshape(-1, *pair_sum.shape[3:])

time: 103 us -> 103 us (level)
  starting transfers between devices: 39.1 us -> 36.3 us
  blocking collectives: 36.8 us -> 38.5 us
    ppermute x8 -> x7, starting transfers between devices: 23.5 us -> 19.9 us  [swapped(): return lax.ppermute(part, axis, [(i, i ^ distance) for i in range(size)])]
    all_gather x1, blocking collectives: 36.8 us -> 38.5 us  [per_device(): along = lax.all_gather(packed, Z, axis=0, tiled=False)]
    ppermute x8 -> x7, waiting for transfers between devices: 13.9 us -> 14.9 us  [swapped(): return lax.ppermute(part, axis, [(i, i ^ distance) for i in range(size)])]
  transfers between devices with their start and end apart: 10 -> 9, of which waited for: 6 -> 6; matrix products, arithmetic and copies ran while one was open for 1% -> 1% of each run, Pallas kernels for 6% -> 4%
where the time goes in v10:
time: 103 us
  blocking collectives  38.5 us (37%)
  starting transfers between devices  36.3 us (35%)
  waiting for transfers between devices  17 us (17%)
  Pallas kernels  8.62 us (8%)
  other arithmetic  1.44 us (1%)
    all_gather x1, blocking collectives, per_device(): along = lax.all_gather(packed, Z, axis=0, tiled=False)  38.5 us
    ppermute x7, starting transfers between devices, swapped(): return lax.ppermute(part, axis, [(i, i ^ distance) for i in range(size)])  19.9 us
    ppermute x7, waiting for transfers between devices, swapped(): return lax.ppermute(part, axis, [(i, i ^ distance) for i in range(size)])  14.9 us
    all_to_all x1, starting transfers between devices, per_device(): rows_in = lax.all_to_all(copies, PLANE, 0, 0, tiled=True)  8.72 us
    all_to_all x1, starting transfers between devices, per_device(): pieces = lax.all_to_all(pair_sum, ('zh', 'y'), 0, 0, tiled=True)  7.62 us
    pallas_call x1, Pallas kernels, route(): pl.pallas_call(route_kernel, out_shape=(jax.ShapeDtypeStruct((peers, 2 *...  2.87 us
    all_to_all x1, waiting for transfers between devices, per_device(): pieces = lax.all_to_all(pair_sum, ('zh', 'y'), 0, 0, tiled=True)  2.14 us
  transfers between devices with their start and end apart: 9, of which 6 were waited for; matrix products, arithmetic and copies ran while one was open for 1% of the time, Pallas kernels for 4%

profile of v10, /device:TPU:6, one launch (start us, length us, event | category | flops | bytes accessed | tf_op | source)
XLA Modules:
  0.0 102.6 jit_solution(6735690761079489401)
XLA Ops:
  0.6 0.7 pad_maximum_fusion.own_ref
  1.4 3.5 %collective-permute-start = (bf16[3,32,128]{2,1,0:T(8,128)(2,1)S(1)}, bf16[3,32,128]{2,1,0:T(8,128)(2,1)S(1)}, u32[]{:S(2)}, u32[]{:S(2)}) collective-permute-start(bf16[3,32,128]{2,1,0:T(8,128)(2,1)S(1)} %pad_maximum_fusion.own_ref), channel_id=1, source_target_pairs={{0,16},{16,0},{1,17},{17,1},{2,18},{18,2},{3,19},{19,3},{4,20},{20... | collective-permute-start | bytes 73736 | tf_op jit(solution)/shard_map/ppermute | solution.py:363
  4.8 2.9 %route.1 = (bf16[16,32,2048]{2,1,0:T(8,128)(2,1)}, bf16[16,128]{1,0:T(8,128)(2,1)}, f32[16,128]{1,0:T(8,128)}) custom-call(s32[8,128]{1,0:T(8,128)} %bitcast.12, f32[8,128]{1,0:T(8,128)} %bitcast.13, bf16[128,2048]{1,0:T(8,128)(2,1)} %tokens_ref.1, bf16[128,2048]{1,0:T(8,128)(2,1)} %cot_ref.1), custom_call_target="tpu_custom_call" | custom-call | tf_op jit(solution)/shard_map/route/pallas_call | solution.py:98
  7.7 0.0 collective-permute-done.got_ref
  7.7 0.1 pack_shards.1
  7.8 8.7 %all-to-all-start = ((bf16[16,32,2048]{2,1,0:T(8,128)(2,1)}), bf16[16,32,2048]{2,1,0:T(8,128)(2,1)S(1)}, u32[]{:S(2)}, u32[]{:S(2)}) async-start(bf16[16,32,2048]{2,1,0:T(8,128)(2,1)} %get-tuple-element.28), calls=%async_computation | async-start | bytes 4194304 | tf_op jit(solution)/shard_map/all_to_all | solution.py:374
  16.5 0.0 copy-start.2
  16.6 38.5 %all-gather = bf16[3072,128]{1,0:T(8,128)(2,1)S(1)} all-gather(bf16[192,128]{1,0:T(8,128)(2,1)S(1)} %pack_shards.1), channel_id=2, replica_groups=mesh['zh'=8,'zl'=2,'y'=2,'c'=2,'h'=2,'x'=4] {'zh','zl'}, dimensions={0}, use_global_device_ids=true | all-gather | bytes 835584 | tf_op jit(solution)/shard_map/all_gather | solution.py:375
  55.0 0.0 all-to-all-done.both_ref
  55.0 1.9 %collective-permute-start.1 = (bf16[16,192,128]{2,1,0:T(8,128)(2,1)S(1)}, bf16[16,192,128]{2,1,0:T(8,128)(2,1)S(1)}, u32[]{:S(2)}, u32[]{:S(2)}) collective-permute-start(bf16[16,192,128]{2,1,0:T(8,128)(2,1)S(1)} %bitcast.7), channel_id=1, source_target_pairs={{0,8},{8,0},{1,9},{9,1},{2,10},{10,2},{3,11},{11,3},{4,12},{12,4},... | collective-permute-start | bytes 2359304 | tf_op jit(solution)/shard_map/ppermute | solution.py:363
  57.0 2.3 %collective-permute-done.1.got_ref = bf16[16,192,128]{2,1,0:T(8,128)(2,1)S(1)} collective-permute-done((bf16[16,192,128]{2,1,0:T(8,128)(2,1)S(1)}, bf16[16,192,128]{2,1,0:T(8,128)(2,1)S(1)}, u32[]{:S(2)}, u32[]{:S(2)}) %collective-permute-start.1) | collective-permute-done | bytes 786464 | tf_op jit(solution)/shard_map/ppermute | solution.py:363
  59.2 1.8 %forward.1 = (f32[4,16,2048]{2,1,0:T(8,128)S(1)}, bf16[4,16,2048]{2,1,0:T(8,128)(2,1)}, f32[256,128]{1,0:T(8,128)S(1)}, bf16[2048,128]{1,0:T(8,128)(2,1)S(1)}) custom-call(bf16[16,32,2048]{2,1,0:T(8,128)(2,1)S(1)} %all-to-all-done.both_ref, bf16[16,192,128]{2,1,0:T(8,128)(2,1)S(1)} %bitcast.8, bf16[16,192,128]{2,1,0:T(8,128)(2,1)S(1)} %collective-permute-done.1.got_ref), custom_call_target="tpu_custom_call" | custom-call | tf_op jit(solution)/shard_map/forward/pallas_call | solution.py:207
  61.0 0.0 copy-done.2
  61.0 1.9 %backward.1 = (bf16[2,8,2,48,128]{4,3,2,1,0:T(8,128)(2,1)S(1)}, f32[2,8,2,48,128]{4,3,2,1,0:T(8,128)S(1)}) custom-call(s32[64]{0:T(128)S(1)} %copy-done.2, bf16[16,32,2048]{2,1,0:T(8,128)(2,1)S(1)} %all-to-all-done.both_ref, f32[256,128]{1,0:T(8,128)S(1)} %get-tuple-element.39.acts_ref, bf16[2048,128]{1,0:T(8,128)(2,1)S(1)} %get-tuple-element.40.down), custom_call_target="tpu_custom_call" | custom-call | flops 8800000000 | bytes 29600000 | tf_op jit(solution)/shard_map/backward/pallas_call | solution.py:275
  62.9 2.0 %collective-permute-start.5 = (bf16[2,8,2,48,128]{4,3,2,1,0:T(8,128)(2,1)S(1)}, bf16[2,8,2,48,128]{4,3,2,1,0:T(8,128)(2,1)S(1)}, u32[]{:S(2)}, u32[]{:S(2)}) collective-permute-start(bf16[2,8,2,48,128]{4,3,2,1,0:T(8,128)(2,1)S(1)} %get-tuple-element.42), channel_id=1, source_target_pairs={{0,8},{8,0},{1,9},{9,1},{2,10},{10,2},{3,11},{11,3},{4,12},{12,4},... | collective-permute-start | bytes 1179656 | tf_op jit(solution)/shard_map/ppermute | solution.py:363
  65.0 1.6 %collective-permute-done.5.got_ref = bf16[2,8,2,48,128]{4,3,2,1,0:T(8,128)(2,1)S(1)} collective-permute-done((bf16[2,8,2,48,128]{4,3,2,1,0:T(8,128)(2,1)S(1)}, bf16[2,8,2,48,128]{4,3,2,1,0:T(8,128)(2,1)S(1)}, u32[]{:S(2)}, u32[]{:S(2)}) %collective-permute-start.5) | collective-permute-done | bytes 393248 | tf_op jit(solution)/shard_map/ppermute | solution.py:363
  66.5 0.1 add_halves.5
  66.6 1.9 %collective-permute-start.6 = (bf16[1,8,2,48,128]{4,3,2,1,0:T(8,128)(2,1)S(1)}, bf16[1,8,2,48,128]{4,3,2,1,0:T(8,128)(2,1)S(1)}, u32[]{:S(2)}, u32[]{:S(2)}) collective-permute-start(bf16[1,8,2,48,128]{4,3,2,1,0:T(8,128)(2,1)S(1)} %get-tuple-element.44), channel_id=1, source_target_pairs={{0,32},{32,0},{1,33},{33,1},{2,34},{34,2},{3,35},{35,3},{4,36},{36... | collective-permute-start | bytes 589832 | tf_op jit(solution)/shard_map/ppermute | solution.py:363
  68.5 3.4 %collective-permute-start.2 = (bf16[4,16,2048]{2,1,0:T(8,128)(2,1)}, bf16[4,16,2048]{2,1,0:T(8,128)(2,1)S(1)}, u32[]{:S(2)}, u32[]{:S(2)}) collective-permute-start(bf16[4,16,2048]{2,1,0:T(8,128)(2,1)} %get-tuple-element.32), channel_id=1, source_target_pairs={{0,2},{1,3},{2,0},{3,1},{4,6},{5,7},{6,4},{7,5},{8,10},{9,11},{10,... | collective-permute-start | bytes 786440 | tf_op jit(solution)/shard_map/ppermute | solution.py:363
  71.9 3.5 %collective-permute-done.6 = bf16[1,8,2,48,128]{4,3,2,1,0:T(8,128)(2,1)S(1)} collective-permute-done((bf16[1,8,2,48,128]{4,3,2,1,0:T(8,128)(2,1)S(1)}, bf16[1,8,2,48,128]{4,3,2,1,0:T(8,128)(2,1)S(1)}, u32[]{:S(2)}, u32[]{:S(2)}) %collective-permute-start.6) | collective-permute-done | bytes 196640 | tf_op jit(solution)/shard_map/ppermute | solution.py:363
  75.5 0.7 add_convert_fusion
  76.2 7.6 %all-to-all-start.1 = ((bf16[16,48,128]{2,1,0:T(8,128)(2,1)}), bf16[16,48,128]{2,1,0:T(8,128)(2,1)S(1)}, u32[]{:S(2)}, u32[]{:S(2)}) async-start(bf16[16,48,128]{2,1,0:T(8,128)(2,1)} %bitcast.6), calls=%async_computation.1 | async-start | bytes 393216 | tf_op jit(solution)/shard_map/all_to_all | solution.py:385
  83.8 0.0 collective-permute-done.2.got_ref
  83.9 0.0 copy-start
  83.9 0.0 copy-start.1
  83.9 2.6 %collective-permute-start.3 = (bf16[2,16,2048]{2,1,0:T(8,128)(2,1)S(1)}, bf16[2,16,2048]{2,1,0:T(8,128)(2,1)S(1)}, u32[]{:S(2)}, u32[]{:S(2)}) collective-permute-start(bf16[2,16,2048]{2,1,0:T(8,128)(2,1)S(1)} %get-tuple-element.34), channel_id=1, source_target_pairs={{0,1},{1,0},{2,3},{3,2},{4,5},{5,4},{6,7},{7,6},{8,9},{9,8},{10,11... | collective-permute-start | bytes 393224 | tf_op jit(solution)/shard_map/ppermute | solution.py:363
  86.5 4.2 %collective-permute-done.3.got_ref = bf16[2,16,2048]{2,1,0:T(8,128)(2,1)S(1)} collective-permute-done((bf16[2,16,2048]{2,1,0:T(8,128)(2,1)S(1)}, bf16[2,16,2048]{2,1,0:T(8,128)(2,1)S(1)}, u32[]{:S(2)}, u32[]{:S(2)}) %collective-permute-start.3) | collective-permute-done | bytes 131104 | tf_op jit(solution)/shard_map/ppermute | solution.py:363
  90.8 4.6 %collective-permute-start.4 = (bf16[1,16,2048]{2,1,0:T(8,128)(2,1)S(1)}, bf16[1,16,2048]{2,1,0:T(8,128)(2,1)S(1)}, u32[]{:S(2)}, u32[]{:S(2)}) collective-permute-start(bf16[1,16,2048]{2,1,0:T(8,128)(2,1)S(1)} %get-tuple-element.36), channel_id=1, source_target_pairs={{0,4},{4,0},{1,5},{5,1},{2,6},{6,2},{3,7},{7,3},{8,12},{12,8},{9,1... | collective-permute-start | bytes 196616 | tf_op jit(solution)/shard_map/ppermute | solution.py:363
  95.4 3.3 %collective-permute-done.4.got_ref = bf16[1,16,2048]{2,1,0:T(8,128)(2,1)S(1)} collective-permute-done((bf16[1,16,2048]{2,1,0:T(8,128)(2,1)S(1)}, bf16[1,16,2048]{2,1,0:T(8,128)(2,1)S(1)}, u32[]{:S(2)}, u32[]{:S(2)}) %collective-permute-start.4) | collective-permute-done | bytes 65568 | tf_op jit(solution)/shard_map/ppermute | solution.py:363
  98.6 0.0 copy-done
  98.6 0.0 copy-done.1
  98.6 1.1 %mix.1 = bf16[128,2048]{1,0:T(8,128)(2,1)} custom-call(f32[1,16,2048]{2,1,0:T(8,128)S(1)} %get-tuple-element.35.own_ref, bf16[1,16,2048]{2,1,0:T(8,128)(2,1)S(1)} %collective-permute-done.4.got_ref, bf16[16,128]{1,0:T(8,128)(2,1)S(1)} %copy-done.1, f32[16,128]{1,0:T(8,128)S(1)} %copy-done), custom_call_target="tpu_custom_call" | custom-call | flops 1100000000 | bytes 3700000 | tf_op jit(solution)/shard_map/mix/pallas_call | solution.py:321
  99.8 2.1 %all-to-all-done.1.blocks_ref = bf16[16,48,128]{2,1,0:T(8,128)(2,1)S(1)} async-done(((bf16[16,48,128]{2,1,0:T(8,128)(2,1)}), bf16[16,48,128]{2,1,0:T(8,128)(2,1)S(1)}, u32[]{:S(2)}, u32[]{:S(2)}) %all-to-all-start.1) | async-done | bytes 196640 | tf_op jit(solution)/shard_map/all_to_all | solution.py:385
  101.9 0.7 finish.1
  (2 shorter events, 0.1 us)
Async XLA Ops:
  1.4 6.4 %collective-permute-start = (bf16[3,32,128]{2,1,0:T(8,128)(2,1)S(1)}, bf16[3,32,128]{2,1,0:T(8,128)(2,1)S(1)}, u32[]{:S(2)}, u32[]{:S(2)}) collective-permute-start(bf16[3,32,128]{2,1,0:T(8,128)(2,1)S(1)} %pad_maximum_fusion.own_ref), channel_id=1, source_target_pairs={{0,16},{16,0},{1,17},{17,1},{2,18},{18,2},{3,19},{19,3},{4,20},{20... | collective-permute-start | bytes 73736 | tf_op jit(solution)/shard_map/ppermute | solution.py:363
  7.8 47.2 %all-to-all-start = ((bf16[16,32,2048]{2,1,0:T(8,128)(2,1)}), bf16[16,32,2048]{2,1,0:T(8,128)(2,1)S(1)}, u32[]{:S(2)}, u32[]{:S(2)}) async-start(bf16[16,32,2048]{2,1,0:T(8,128)(2,1)} %get-tuple-element.28), calls=%async_computation | async-start | bytes 4194304 | tf_op jit(solution)/shard_map/all_to_all | solution.py:374
  16.5 44.4 %copy-start.2 = (s32[64]{0:T(128)S(1)}, s32[64]{0:T(128)}, u32[]{:S(2)}) copy-start(s32[64]{0:T(128)} %join_ref.1) | copy-start | bytes 772
  55.0 4.2 %collective-permute-start.1 = (bf16[16,192,128]{2,1,0:T(8,128)(2,1)S(1)}, bf16[16,192,128]{2,1,0:T(8,128)(2,1)S(1)}, u32[]{:S(2)}, u32[]{:S(2)}) collective-permute-start(bf16[16,192,128]{2,1,0:T(8,128)(2,1)S(1)} %bitcast.7), channel_id=1, source_target_pairs={{0,8},{8,0},{1,9},{9,1},{2,10},{10,2},{3,11},{11,3},{4,12},{12,4},... | collective-permute-start | bytes 2359304 | tf_op jit(solution)/shard_map/ppermute | solution.py:363
  62.9 3.6 %collective-permute-start.5 = (bf16[2,8,2,48,128]{4,3,2,1,0:T(8,128)(2,1)S(1)}, bf16[2,8,2,48,128]{4,3,2,1,0:T(8,128)(2,1)S(1)}, u32[]{:S(2)}, u32[]{:S(2)}) collective-permute-start(bf16[2,8,2,48,128]{4,3,2,1,0:T(8,128)(2,1)S(1)} %get-tuple-element.42), channel_id=1, source_target_pairs={{0,8},{8,0},{1,9},{9,1},{2,10},{10,2},{3,11},{11,3},{4,12},{12,4},... | collective-permute-start | bytes 1179656 | tf_op jit(solution)/shard_map/ppermute | solution.py:363
  66.6 8.8 %collective-permute-start.6 = (bf16[1,8,2,48,128]{4,3,2,1,0:T(8,128)(2,1)S(1)}, bf16[1,8,2,48,128]{4,3,2,1,0:T(8,128)(2,1)S(1)}, u32[]{:S(2)}, u32[]{:S(2)}) collective-permute-start(bf16[1,8,2,48,128]{4,3,2,1,0:T(8,128)(2,1)S(1)} %get-tuple-element.44), channel_id=1, source_target_pairs={{0,32},{32,0},{1,33},{33,1},{2,34},{34,2},{3,35},{35,3},{4,36},{36... | collective-permute-start | bytes 589832 | tf_op jit(solution)/shard_map/ppermute | solution.py:363
  68.5 15.2 %collective-permute-start.2 = (bf16[4,16,2048]{2,1,0:T(8,128)(2,1)}, bf16[4,16,2048]{2,1,0:T(8,128)(2,1)S(1)}, u32[]{:S(2)}, u32[]{:S(2)}) collective-permute-start(bf16[4,16,2048]{2,1,0:T(8,128)(2,1)} %get-tuple-element.32), channel_id=1, source_target_pairs={{0,2},{1,3},{2,0},{3,1},{4,6},{5,7},{6,4},{7,5},{8,10},{9,11},{10,... | collective-permute-start | bytes 786440 | tf_op jit(solution)/shard_map/ppermute | solution.py:363
  76.2 25.7 %all-to-all-start.1 = ((bf16[16,48,128]{2,1,0:T(8,128)(2,1)}), bf16[16,48,128]{2,1,0:T(8,128)(2,1)S(1)}, u32[]{:S(2)}, u32[]{:S(2)}) async-start(bf16[16,48,128]{2,1,0:T(8,128)(2,1)} %bitcast.6), calls=%async_computation.1 | async-start | bytes 393216 | tf_op jit(solution)/shard_map/all_to_all | solution.py:385
  83.9 14.8 %copy-start = (f32[16,128]{1,0:T(8,128)S(1)}, f32[16,128]{1,0:T(8,128)}, u32[]{:S(2)}) copy-start(f32[16,128]{1,0:T(8,128)} %get-tuple-element.38.slot_weight_ref) | copy-start | bytes 24580
  83.9 14.8 %copy-start.1 = (bf16[16,128]{1,0:T(8,128)(2,1)S(1)}, bf16[16,128]{1,0:T(8,128)(2,1)}, u32[]{:S(2)}) copy-start(bf16[16,128]{1,0:T(8,128)(2,1)} %get-tuple-element.37.chooser_ref) | copy-start | bytes 12292
  83.9 6.9 %collective-permute-start.3 = (bf16[2,16,2048]{2,1,0:T(8,128)(2,1)S(1)}, bf16[2,16,2048]{2,1,0:T(8,128)(2,1)S(1)}, u32[]{:S(2)}, u32[]{:S(2)}) collective-permute-start(bf16[2,16,2048]{2,1,0:T(8,128)(2,1)S(1)} %get-tuple-element.34), channel_id=1, source_target_pairs={{0,1},{1,0},{2,3},{3,2},{4,5},{5,4},{6,7},{7,6},{8,9},{9,8},{10,11... | collective-permute-start | bytes 393224 | tf_op jit(solution)/shard_map/ppermute | solution.py:363
  90.8 7.8 %collective-permute-start.4 = (bf16[1,16,2048]{2,1,0:T(8,128)(2,1)S(1)}, bf16[1,16,2048]{2,1,0:T(8,128)(2,1)S(1)}, u32[]{:S(2)}, u32[]{:S(2)}) collective-permute-start(bf16[1,16,2048]{2,1,0:T(8,128)(2,1)S(1)} %get-tuple-element.36), channel_id=1, source_target_pairs={{0,4},{4,0},{1,5},{5,1},{2,6},{6,2},{3,7},{7,3},{8,12},{12,8},{9,1... | collective-permute-start | bytes 196616 | tf_op jit(solution)/shard_map/ppermute | solution.py:363

commit v11 on v10

--- a/solution.py
+++ b/solution.py
@@ -152,44 +152,70 @@
     )(own, got)
 
 
-def forward_kernel(
-    both_ref, own_ref, got_ref, mine_ref, theirs_ref, acts_ref, down, gate_up, others, hiddens, partials
-):
-    chips, rows, width = own_ref.shape
+def lay_out(own_ref, got_ref, part, target):
+    chips, rows, _ = own_ref.shape
     rows = rows // 6
-    half = width // 2
-    peers, slots = both_ref.shape[0], both_ref.shape[1] // 2
-    depth = both_ref.shape[2]
-    y, c = lax.axis_index("y"), lax.axis_index("c")
+    c = lax.axis_index("c")
     for core, ref in ((c, own_ref), (1 - c, got_ref)):
         for chip in range(chips):
             for k in range(2):
                 at = pl.multiple_of((chip * 2 + k) * 2 * rows + core * rows, rows)
-                for part, target in enumerate((gate_up, others, down)):
-                    first = (2 * part + k) * rows
-                    target[pl.ds(at, rows), :] = ref[chip, first : first + rows, :]
-    total = peers * slots
-    picked = both_ref[:, :slots, :].reshape(total, depth)
-    acts = jnp.dot(picked, gate_up[...], preferred_element_type=jnp.float32)
-    acts_ref[...] = acts
-    gate, up, _ = gate_and_up(acts)
-    hiddens[...] = gate * jax.nn.sigmoid(gate) * up
-    group_rows = total // 2
-    group = both_ref[pl.ds(y * (peers // 2), peers // 2), :slots, :].reshape(group_rows, depth)
-    gate, up, _ = gate_and_up(jnp.dot(group, others[...], preferred_element_type=jnp.float32))
-    hidden = gate * jax.nn.sigmoid(gate) * up
-    mine = (lanes(hidden.shape) >= half) == (y == 1)
-    hidden = jnp.where(mine, hiddens[pl.ds(y * group_rows, group_rows), :], hidden)
+                first = (2 * part + k) * rows
+                target[pl.ds(at, rows), :] = ref[chip, first : first + rows, :]
+
+
+def forward_kernel(both_ref, own_ref, got_ref, acts_ref, down, gate_up):
+    peers, slots = both_ref.shape[0], both_ref.shape[1] // 2
+    lay_out(own_ref, got_ref, 0, gate_up)
+    lay_out(own_ref, got_ref, 2, down)
+    picked = both_ref[:, :slots, :].reshape(peers * slots, both_ref.shape[2])
+    acts_ref[...] = jnp.dot(picked, gate_up[...], preferred_element_type=jnp.float32)
+
+
+def partial_kernel(
+    both_ref, own_ref, got_ref, acts_ref, down_ref, mine_ref, theirs_ref, others, partials
+):
+    group_rows, width = acts_ref.shape[0] // 2, acts_ref.shape[1]
+    peers, slots = both_ref.shape[0] // 2, both_ref.shape[1] // 2
+    y, h, x = lax.axis_index("y"), lax.axis_index("h"), lax.axis_index("x")
+    lay_out(own_ref, got_ref, 1, others)
+    group = both_ref[pl.ds(y * peers, peers), :slots, :].reshape(group_rows, both_ref.shape[2])
+    theirs = jnp.dot(group, others[...], preferred_element_type=jnp.float32)
+    mine = acts_ref[pl.ds(pl.multiple_of(y * group_rows, group_rows), group_rows), :]
+    (gate, up, low), (their_gate, their_up, _) = gate_and_up(mine), gate_and_up(theirs)
+    here = jnp.logical_not(low) == (y == 1)
+    gate, up = jnp.where(here, gate, their_gate), jnp.where(here, up, their_up)
+    hidden = (gate * jax.nn.sigmoid(gate) * up).astype(jnp.bfloat16)
     partial = lax.dot_general(
-        hidden.astype(jnp.bfloat16), down[...], LANE_DIMS, preferred_element_type=jnp.float32
+        hidden, down_ref[...], LANE_DIMS, preferred_element_type=jnp.float32
     )
     partials[...] = partial.reshape(partials.shape)
-    h, x = lax.axis_index("h"), lax.axis_index("x")
     for high, ref in enumerate((mine_ref, theirs_ref)):
-        for low in range(2):
+        for low_bit in range(2):
             for row in range(2):
-                peer = jnp.bitwise_xor(h, row) * 4 + jnp.bitwise_xor(x, 2 * high + low)
-                ref[2 * low + row] = partials[peer].astype(ref.dtype)
+                peer = jnp.bitwise_xor(h, row) * 4 + jnp.bitwise_xor(x, 2 * high + low_bit)
+                ref[2 * low_bit + row] = partials[peer].astype(ref.dtype)
+
+
+def partial_rows(both, own, got, acts, down):
+    peers, doubled, depth = both.shape
+    peers, slots = peers // 2, doubled // 2
+    return pl.pallas_call(
+        partial_kernel,
+        out_shape=(
+            jax.ShapeDtypeStruct((peers // 2, slots, depth), jnp.float32),
+            jax.ShapeDtypeStruct((peers // 2, slots, depth), jnp.bfloat16),
+        ),
+        in_specs=whole(5),
+        out_specs=tuple(whole(2)),
+        scratch_shapes=[
+            pltpu.VMEM(down.shape, jnp.bfloat16),
+            pltpu.VMEM((peers, slots, depth), jnp.float32),
+        ],
+        compiler_params=params(12),
+        cost_estimate=cost(4),
+        name="partial_rows",
+    )(both, own, got, acts, down)
 
 
 def gate_and_up(acts):
@@ -201,26 +227,17 @@
 
 def forward(both, own, got):
     peers, doubled, depth = both.shape
-    slots = doubled // 2
-    rows = peers * slots
     width = own.shape[2]
     return pl.pallas_call(
         forward_kernel,
         out_shape=(
-            jax.ShapeDtypeStruct((peers // 4, slots, depth), jnp.float32),
-            jax.ShapeDtypeStruct((peers // 4, slots, depth), jnp.bfloat16),
-            jax.ShapeDtypeStruct((rows, width), jnp.float32),
+            jax.ShapeDtypeStruct((peers * doubled // 2, width), jnp.float32),
             jax.ShapeDtypeStruct((depth, width), jnp.bfloat16),
         ),
         in_specs=whole(3),
-        out_specs=tuple(whole(4)),
-        scratch_shapes=[
-            pltpu.VMEM((depth, width), jnp.bfloat16),
-            pltpu.VMEM((depth, width), jnp.bfloat16),
-            pltpu.VMEM((rows, width), jnp.float32),
-            pltpu.VMEM((peers // 2, slots, depth), jnp.float32),
-        ],
-        compiler_params=params(16),
+        out_specs=tuple(whole(2)),
+        scratch_shapes=[pltpu.VMEM((depth, width), jnp.bfloat16)],
+        compiler_params=params(12),
         name="forward",
     )(both, own, got)
 
@@ -375,10 +392,14 @@
     along = lax.all_gather(packed, Z, axis=0, tiled=False)
     along, rows_in = lax.optimization_barrier((along, rows_in))
     other = swapped(along, "c")
-    partial, partial_send, acts, down = forward(rows_in, along, other)
+    acts, down = forward(rows_in, along, other)
+    send, keep = backward(join_groups, rows_in, acts, down, lax.axis_size(Z))
+    acts, keep = lax.optimization_barrier((acts, keep))
+    partial, partial_send = partial_rows(rows_in, along, other, acts, down)
     partial_got = swapped(partial_send, "x", 2)
-    send, keep = backward(join_groups, rows_in, acts, down, lax.axis_size(Z))
-    keep, to_pair = add_halves(keep, swapped(send, "c"), 0.4)
+    from_core = swapped(send, "c")
+    from_core, _ = lax.optimization_barrier((from_core, partial_send))
+    keep, to_pair = add_halves(keep, from_core, 0.4)
     from_pair = swapped(to_pair, "zl")
     pair_sum = (keep + from_pair.astype(jnp.float32)).astype(jnp.bfloat16)
     pair_sum = pair_sum.reshape(-1, *pair_sum.shape[3:])

time: 103 us -> 102 us (level)
  waiting for transfers between devices: 17 us -> 15.2 us
  local copies, waits for them, and re-layouts: 0.02 us -> 1.06 us
    unnamed x6 -> x10, local copies, waits for them, and re-layouts: 0.02 us -> 1.06 us
  transfers between devices with their start and end apart: 9 -> 9, of which waited for: 6 -> 6; matrix products, arithmetic and copies ran while one was open for 1% -> 1% of each run, Pallas kernels for 4% -> 5%
where the time goes in v11:
time: 102 us; the launch traced here: 101 us
  blocking collectives  38.5 us (38%)
  starting transfers between devices  36.2 us (35%)
  waiting for transfers between devices  15.2 us (15%)
  Pallas kernels  8.13 us (8%)
  other arithmetic  1.44 us (1%)
  local copies, waits for them, and re-layouts  1.06 us (1%)
    all_gather x1, blocking collectives, per_device(): along = lax.all_gather(packed, Z, axis=0, tiled=False)  38.5 us
    ppermute x7, starting transfers between devices, swapped(): return lax.ppermute(part, axis, [(i, i ^ distance) for i in range(size)])  19.9 us
    ppermute x7, waiting for transfers between devices, swapped(): return lax.ppermute(part, axis, [(i, i ^ distance) for i in range(size)])  14 us
    all_to_all x1, starting transfers between devices, per_device(): rows_in = lax.all_to_all(copies, PLANE, 0, 0, tiled=True)  8.72 us
    all_to_all x1, starting transfers between devices, per_device(): pieces = lax.all_to_all(pair_sum, ('zh', 'y'), 0, 0, tiled=True)  7.63 us
    pallas_call x1, Pallas kernels, route(): pl.pallas_call(route_kernel, out_shape=(jax.ShapeDtypeStruct((peers, 2 *...  2.87 us
  transfers between devices with their start and end apart: 9, of which 6 were waited for; matrix products, arithmetic and copies ran while one was open for 1% of the time, Pallas kernels for 5%

profile of v11, /device:TPU:6, one launch (start us, length us, event | category | flops | bytes accessed | tf_op | source)
XLA Modules:
  0.0 101.4 jit_solution(17787586454187484968)
XLA Ops:
  0.6 0.7 pad_maximum_fusion.own_ref
  1.4 3.5 %collective-permute-start = (bf16[3,32,128]{2,1,0:T(8,128)(2,1)S(1)}, bf16[3,32,128]{2,1,0:T(8,128)(2,1)S(1)}, u32[]{:S(2)}, u32[]{:S(2)}) collective-permute-start(bf16[3,32,128]{2,1,0:T(8,128)(2,1)S(1)} %pad_maximum_fusion.own_ref), channel_id=1, source_target_pairs={{0,16},{16,0},{1,17},{17,1},{2,18},{18,2},{3,19},{19,3},{4,20},{20... | collective-permute-start | bytes 73736 | tf_op jit(solution)/shard_map/ppermute | solution.py:380
  4.8 2.9 %route.1 = (bf16[16,32,2048]{2,1,0:T(8,128)(2,1)}, bf16[16,128]{1,0:T(8,128)(2,1)}, f32[16,128]{1,0:T(8,128)}) custom-call(s32[8,128]{1,0:T(8,128)} %bitcast.13, f32[8,128]{1,0:T(8,128)} %bitcast.14, bf16[128,2048]{1,0:T(8,128)(2,1)} %tokens_ref.1, bf16[128,2048]{1,0:T(8,128)(2,1)} %cot_ref.1), custom_call_target="tpu_custom_call" | custom-call | tf_op jit(solution)/shard_map/route/pallas_call | solution.py:98
  7.7 0.0 collective-permute-done.got_ref
  7.7 0.1 pack_shards.1
  7.8 8.7 %all-to-all-start = ((bf16[16,32,2048]{2,1,0:T(8,128)(2,1)}), bf16[16,32,2048]{2,1,0:T(8,128)(2,1)S(1)}, u32[]{:S(2)}, u32[]{:S(2)}) async-start(bf16[16,32,2048]{2,1,0:T(8,128)(2,1)} %get-tuple-element.31), calls=%async_computation | async-start | bytes 4194304 | tf_op jit(solution)/shard_map/all_to_all | solution.py:391
  16.5 0.0 copy-start.2
  16.6 38.5 %all-gather = bf16[3072,128]{1,0:T(8,128)(2,1)S(1)} all-gather(bf16[192,128]{1,0:T(8,128)(2,1)S(1)} %pack_shards.1), channel_id=2, replica_groups=mesh['zh'=8,'zl'=2,'y'=2,'c'=2,'h'=2,'x'=4] {'zh','zl'}, dimensions={0}, use_global_device_ids=true | all-gather | bytes 835584 | tf_op jit(solution)/shard_map/all_gather | solution.py:392
  55.1 0.0 all-to-all-done.both_ref
  55.1 1.9 %collective-permute-start.1 = (bf16[16,192,128]{2,1,0:T(8,128)(2,1)S(1)}, bf16[16,192,128]{2,1,0:T(8,128)(2,1)S(1)}, u32[]{:S(2)}, u32[]{:S(2)}) collective-permute-start(bf16[16,192,128]{2,1,0:T(8,128)(2,1)S(1)} %bitcast.7), channel_id=1, source_target_pairs={{0,8},{8,0},{1,9},{9,1},{2,10},{10,2},{3,11},{11,3},{4,12},{12,4},... | collective-permute-start | bytes 2359304 | tf_op jit(solution)/shard_map/ppermute | solution.py:380
  57.0 2.3 %collective-permute-done.1.got_ref = bf16[16,192,128]{2,1,0:T(8,128)(2,1)S(1)} collective-permute-done((bf16[16,192,128]{2,1,0:T(8,128)(2,1)S(1)}, bf16[16,192,128]{2,1,0:T(8,128)(2,1)S(1)}, u32[]{:S(2)}, u32[]{:S(2)}) %collective-permute-start.1) | collective-permute-done | bytes 786464 | tf_op jit(solution)/shard_map/ppermute | solution.py:380
  59.2 0.5 forward.1
  59.7 0.0 copy-done.2
  59.7 1.9 %backward.1 = (bf16[2,8,2,48,128]{4,3,2,1,0:T(8,128)(2,1)S(1)}, f32[2,8,2,48,128]{4,3,2,1,0:T(8,128)S(1)}) custom-call(s32[64]{0:T(128)S(1)} %copy-done.2, bf16[16,32,2048]{2,1,0:T(8,128)(2,1)S(1)} %all-to-all-done.both_ref, f32[256,128]{1,0:T(8,128)S(1)} %get-tuple-element.37.acts_ref, bf16[2048,128]{1,0:T(8,128)(2,1)S(1)} %get-tuple-element.35.down.down_ref), custom_call_target="tpu_custom_call" | custom-call | flops 8800000000 | bytes 29600000 | tf_op jit(solution)/shard_map/backward/pallas_call | solution.py:292
  61.7 2.0 %collective-permute-start.5 = (bf16[2,8,2,48,128]{4,3,2,1,0:T(8,128)(2,1)S(1)}, bf16[2,8,2,48,128]{4,3,2,1,0:T(8,128)(2,1)S(1)}, u32[]{:S(2)}, u32[]{:S(2)}) collective-permute-start(bf16[2,8,2,48,128]{4,3,2,1,0:T(8,128)(2,1)S(1)} %get-tuple-element.47), channel_id=1, source_target_pairs={{0,8},{8,0},{1,9},{9,1},{2,10},{10,2},{3,11},{11,3},{4,12},{12,4},... | collective-permute-start | bytes 1179656 | tf_op jit(solution)/shard_map/ppermute | solution.py:380
  63.7 0.8 partial_rows.1
  64.5 0.0 copy-start.3
  64.5 0.8 collective-permute-done.5.got_ref
  65.3 0.1 add_halves.5
  65.4 1.9 %collective-permute-start.6 = (bf16[1,8,2,48,128]{4,3,2,1,0:T(8,128)(2,1)S(1)}, bf16[1,8,2,48,128]{4,3,2,1,0:T(8,128)(2,1)S(1)}, u32[]{:S(2)}, u32[]{:S(2)}) collective-permute-start(bf16[1,8,2,48,128]{4,3,2,1,0:T(8,128)(2,1)S(1)} %get-tuple-element.50), channel_id=1, source_target_pairs={{0,32},{32,0},{1,33},{33,1},{2,34},{34,2},{3,35},{35,3},{4,36},{36... | collective-permute-start | bytes 589832 | tf_op jit(solution)/shard_map/ppermute | solution.py:380
  67.3 3.4 %collective-permute-start.2 = (bf16[4,16,2048]{2,1,0:T(8,128)(2,1)S(1)}, bf16[4,16,2048]{2,1,0:T(8,128)(2,1)S(1)}, u32[]{:S(2)}, u32[]{:S(2)}) collective-permute-start(bf16[4,16,2048]{2,1,0:T(8,128)(2,1)S(1)} %get-tuple-element.39), channel_id=1, source_target_pairs={{0,2},{1,3},{2,0},{3,1},{4,6},{5,7},{6,4},{7,5},{8,10},{9,11},{10,... | collective-permute-start | bytes 786440 | tf_op jit(solution)/shard_map/ppermute | solution.py:380
  70.7 3.5 %collective-permute-done.6 = bf16[1,8,2,48,128]{4,3,2,1,0:T(8,128)(2,1)S(1)} collective-permute-done((bf16[1,8,2,48,128]{4,3,2,1,0:T(8,128)(2,1)S(1)}, bf16[1,8,2,48,128]{4,3,2,1,0:T(8,128)(2,1)S(1)}, u32[]{:S(2)}, u32[]{:S(2)}) %collective-permute-start.6) | collective-permute-done | bytes 196640 | tf_op jit(solution)/shard_map/ppermute | solution.py:380
  74.2 0.7 add_convert_fusion
  74.9 0.0 copy-done.3
  74.9 7.6 %all-to-all-start.1 = ((bf16[16,48,128]{2,1,0:T(8,128)(2,1)}), bf16[16,48,128]{2,1,0:T(8,128)(2,1)S(1)}, u32[]{:S(2)}, u32[]{:S(2)}) async-start(bf16[16,48,128]{2,1,0:T(8,128)(2,1)} %bitcast.6), calls=%async_computation.1 | async-start | bytes 393216 | tf_op jit(solution)/shard_map/all_to_all | solution.py:406
  82.6 0.0 collective-permute-done.2.got_ref
  82.6 0.0 copy-start.4
  82.6 1.0 %copy-done.4 = f32[4,16,2048]{2,1,0:T(8,128)S(1)} copy-done((f32[4,16,2048]{2,1,0:T(8,128)S(1)}, f32[4,16,2048]{2,1,0:T(8,128)}, u32[]{:S(2)}) %copy-start.4) | copy-done | bytes 524312
  83.6 0.1 add_halves.3
  83.7 0.0 copy-start
  83.7 0.0 copy-start.1
  83.7 2.6 %collective-permute-start.3 = (bf16[2,16,2048]{2,1,0:T(8,128)(2,1)S(1)}, bf16[2,16,2048]{2,1,0:T(8,128)(2,1)S(1)}, u32[]{:S(2)}, u32[]{:S(2)}) collective-permute-start(bf16[2,16,2048]{2,1,0:T(8,128)(2,1)S(1)} %get-tuple-element.41), channel_id=1, source_target_pairs={{0,1},{1,0},{2,3},{3,2},{4,5},{5,4},{6,7},{7,6},{8,9},{9,8},{10,11... | collective-permute-start | bytes 393224 | tf_op jit(solution)/shard_map/ppermute | solution.py:380
  86.3 4.2 %collective-permute-done.3.got_ref = bf16[2,16,2048]{2,1,0:T(8,128)(2,1)S(1)} collective-permute-done((bf16[2,16,2048]{2,1,0:T(8,128)(2,1)S(1)}, bf16[2,16,2048]{2,1,0:T(8,128)(2,1)S(1)}, u32[]{:S(2)}, u32[]{:S(2)}) %collective-permute-start.3) | collective-permute-done | bytes 131104 | tf_op jit(solution)/shard_map/ppermute | solution.py:380
  90.6 4.6 %collective-permute-start.4 = (bf16[1,16,2048]{2,1,0:T(8,128)(2,1)S(1)}, bf16[1,16,2048]{2,1,0:T(8,128)(2,1)S(1)}, u32[]{:S(2)}, u32[]{:S(2)}) collective-permute-start(bf16[1,16,2048]{2,1,0:T(8,128)(2,1)S(1)} %get-tuple-element.43), channel_id=1, source_target_pairs={{0,4},{4,0},{1,5},{5,1},{2,6},{6,2},{3,7},{7,3},{8,12},{12,8},{9,1... | collective-permute-start | bytes 196616 | tf_op jit(solution)/shard_map/ppermute | solution.py:380
  95.2 3.2 %collective-permute-done.4.got_ref = bf16[1,16,2048]{2,1,0:T(8,128)(2,1)S(1)} collective-permute-done((bf16[1,16,2048]{2,1,0:T(8,128)(2,1)S(1)}, bf16[1,16,2048]{2,1,0:T(8,128)(2,1)S(1)}, u32[]{:S(2)}, u32[]{:S(2)}) %collective-permute-start.4) | collective-permute-done | bytes 65568 | tf_op jit(solution)/shard_map/ppermute | solution.py:380
  98.4 0.0 copy-done
  98.4 0.0 copy-done.1
  98.4 1.1 %mix.1 = bf16[128,2048]{1,0:T(8,128)(2,1)} custom-call(f32[1,16,2048]{2,1,0:T(8,128)S(1)} %get-tuple-element.42.own_ref, bf16[1,16,2048]{2,1,0:T(8,128)(2,1)S(1)} %collective-permute-done.4.got_ref, bf16[16,128]{1,0:T(8,128)(2,1)S(1)} %copy-done.1, f32[16,128]{1,0:T(8,128)S(1)} %copy-done), custom_call_target="tpu_custom_call" | custom-call | flops 1100000000 | bytes 3700000 | tf_op jit(solution)/shard_map/mix/pallas_call | solution.py:338
  99.5 1.1 %all-to-all-done.1.blocks_ref = bf16[16,48,128]{2,1,0:T(8,128)(2,1)S(1)} async-done(((bf16[16,48,128]{2,1,0:T(8,128)(2,1)}), bf16[16,48,128]{2,1,0:T(8,128)(2,1)S(1)}, u32[]{:S(2)}, u32[]{:S(2)}) %all-to-all-start.1) | async-done | bytes 196640 | tf_op jit(solution)/shard_map/all_to_all | solution.py:406
  100.7 0.7 finish.1
  (1 shorter events, 0.0 us)
Async XLA Ops:
  1.4 6.4 %collective-permute-start = (bf16[3,32,128]{2,1,0:T(8,128)(2,1)S(1)}, bf16[3,32,128]{2,1,0:T(8,128)(2,1)S(1)}, u32[]{:S(2)}, u32[]{:S(2)}) collective-permute-start(bf16[3,32,128]{2,1,0:T(8,128)(2,1)S(1)} %pad_maximum_fusion.own_ref), channel_id=1, source_target_pairs={{0,16},{16,0},{1,17},{17,1},{2,18},{18,2},{3,19},{19,3},{4,20},{20... | collective-permute-start | bytes 73736 | tf_op jit(solution)/shard_map/ppermute | solution.py:380
  7.8 47.2 %all-to-all-start = ((bf16[16,32,2048]{2,1,0:T(8,128)(2,1)}), bf16[16,32,2048]{2,1,0:T(8,128)(2,1)S(1)}, u32[]{:S(2)}, u32[]{:S(2)}) async-start(bf16[16,32,2048]{2,1,0:T(8,128)(2,1)} %get-tuple-element.31), calls=%async_computation | async-start | bytes 4194304 | tf_op jit(solution)/shard_map/all_to_all | solution.py:391
  16.5 43.2 %copy-start.2 = (s32[64]{0:T(128)S(1)}, s32[64]{0:T(128)}, u32[]{:S(2)}) copy-start(s32[64]{0:T(128)} %join_ref.1) | copy-start | bytes 772
  55.1 4.2 %collective-permute-start.1 = (bf16[16,192,128]{2,1,0:T(8,128)(2,1)S(1)}, bf16[16,192,128]{2,1,0:T(8,128)(2,1)S(1)}, u32[]{:S(2)}, u32[]{:S(2)}) collective-permute-start(bf16[16,192,128]{2,1,0:T(8,128)(2,1)S(1)} %bitcast.7), channel_id=1, source_target_pairs={{0,8},{8,0},{1,9},{9,1},{2,10},{10,2},{3,11},{11,3},{4,12},{12,4},... | collective-permute-start | bytes 2359304 | tf_op jit(solution)/shard_map/ppermute | solution.py:380
  61.7 3.6 %collective-permute-start.5 = (bf16[2,8,2,48,128]{4,3,2,1,0:T(8,128)(2,1)S(1)}, bf16[2,8,2,48,128]{4,3,2,1,0:T(8,128)(2,1)S(1)}, u32[]{:S(2)}, u32[]{:S(2)}) collective-permute-start(bf16[2,8,2,48,128]{4,3,2,1,0:T(8,128)(2,1)S(1)} %get-tuple-element.47), channel_id=1, source_target_pairs={{0,8},{8,0},{1,9},{9,1},{2,10},{10,2},{3,11},{11,3},{4,12},{12,4},... | collective-permute-start | bytes 1179656 | tf_op jit(solution)/shard_map/ppermute | solution.py:380
  64.5 10.4 %copy-start.3 = (f32[4,16,2048]{2,1,0:T(8,128)}, f32[4,16,2048]{2,1,0:T(8,128)S(1)}, u32[]{:S(2)}) copy-start(f32[4,16,2048]{2,1,0:T(8,128)S(1)} %get-tuple-element.38.keep_ref) | copy-start | bytes 1572868
  65.4 8.8 %collective-permute-start.6 = (bf16[1,8,2,48,128]{4,3,2,1,0:T(8,128)(2,1)S(1)}, bf16[1,8,2,48,128]{4,3,2,1,0:T(8,128)(2,1)S(1)}, u32[]{:S(2)}, u32[]{:S(2)}) collective-permute-start(bf16[1,8,2,48,128]{4,3,2,1,0:T(8,128)(2,1)S(1)} %get-tuple-element.50), channel_id=1, source_target_pairs={{0,32},{32,0},{1,33},{33,1},{2,34},{34,2},{3,35},{35,3},{4,36},{36... | collective-permute-start | bytes 589832 | tf_op jit(solution)/shard_map/ppermute | solution.py:380
  67.3 15.3 %collective-permute-start.2 = (bf16[4,16,2048]{2,1,0:T(8,128)(2,1)S(1)}, bf16[4,16,2048]{2,1,0:T(8,128)(2,1)S(1)}, u32[]{:S(2)}, u32[]{:S(2)}) collective-permute-start(bf16[4,16,2048]{2,1,0:T(8,128)(2,1)S(1)} %get-tuple-element.39), channel_id=1, source_target_pairs={{0,2},{1,3},{2,0},{3,1},{4,6},{5,7},{6,4},{7,5},{8,10},{9,11},{10,... | collective-permute-start | bytes 786440 | tf_op jit(solution)/shard_map/ppermute | solution.py:380
  74.9 25.7 %all-to-all-start.1 = ((bf16[16,48,128]{2,1,0:T(8,128)(2,1)}), bf16[16,48,128]{2,1,0:T(8,128)(2,1)S(1)}, u32[]{:S(2)}, u32[]{:S(2)}) async-start(bf16[16,48,128]{2,1,0:T(8,128)(2,1)} %bitcast.6), calls=%async_computation.1 | async-start | bytes 393216 | tf_op jit(solution)/shard_map/all_to_all | solution.py:406
  82.6 1.0 %copy-start.4 = (f32[4,16,2048]{2,1,0:T(8,128)S(1)}, f32[4,16,2048]{2,1,0:T(8,128)}, u32[]{:S(2)}) copy-start(f32[4,16,2048]{2,1,0:T(8,128)} %copy-done.3) | copy-start | bytes 1572868
  83.7 14.7 %copy-start = (f32[16,128]{1,0:T(8,128)S(1)}, f32[16,128]{1,0:T(8,128)}, u32[]{:S(2)}) copy-start(f32[16,128]{1,0:T(8,128)} %get-tuple-element.45.slot_weight_ref) | copy-start | bytes 24580
  83.7 14.7 %copy-start.1 = (bf16[16,128]{1,0:T(8,128)(2,1)S(1)}, bf16[16,128]{1,0:T(8,128)(2,1)}, u32[]{:S(2)}) copy-start(bf16[16,128]{1,0:T(8,128)(2,1)} %get-tuple-element.44.chooser_ref) | copy-start | bytes 12292
  83.7 6.9 %collective-permute-start.3 = (bf16[2,16,2048]{2,1,0:T(8,128)(2,1)S(1)}, bf16[2,16,2048]{2,1,0:T(8,128)(2,1)S(1)}, u32[]{:S(2)}, u32[]{:S(2)}) collective-permute-start(bf16[2,16,2048]{2,1,0:T(8,128)(2,1)S(1)} %get-tuple-element.41), channel_id=1, source_target_pairs={{0,1},{1,0},{2,3},{3,2},{4,5},{5,4},{6,7},{7,6},{8,9},{9,8},{10,11... | collective-permute-start | bytes 393224 | tf_op jit(solution)/shard_map/ppermute | solution.py:380
  90.6 7.8 %collective-permute-start.4 = (bf16[1,16,2048]{2,1,0:T(8,128)(2,1)S(1)}, bf16[1,16,2048]{2,1,0:T(8,128)(2,1)S(1)}, u32[]{:S(2)}, u32[]{:S(2)}) collective-permute-start(bf16[1,16,2048]{2,1,0:T(8,128)(2,1)S(1)} %get-tuple-element.43), channel_id=1, source_target_pairs={{0,4},{4,0},{1,5},{5,1},{2,6},{6,2},{3,7},{7,3},{8,12},{12,8},{9,1... | collective-permute-start | bytes 196616 | tf_op jit(solution)/shard_map/ppermute | solution.py:380

commit v12 on v11

--- a/solution.py
+++ b/solution.py
@@ -203,7 +203,7 @@
     return pl.pallas_call(
         partial_kernel,
         out_shape=(
-            jax.ShapeDtypeStruct((peers // 2, slots, depth), jnp.float32),
+            jax.ShapeDtypeStruct((peers // 2, slots, depth), jnp.bfloat16),
             jax.ShapeDtypeStruct((peers // 2, slots, depth), jnp.bfloat16),
         ),
         in_specs=whole(5),

time: 102 us -> 102 us (level)
  local copies, waits for them, and re-layouts: 1.06 us -> 0.02 us
    unnamed x10 -> x6, local copies, waits for them, and re-layouts: 1.06 us -> 0.02 us
where the time goes in v12:
time: 102 us; the launch traced here: 101 us
  blocking collectives  38.5 us (38%)
  starting transfers between devices  36.3 us (36%)
  waiting for transfers between devices  16.2 us (16%)
  Pallas kernels  8.12 us (8%)
  other arithmetic  1.45 us (1%)
    all_gather x1, blocking collectives, per_device(): along = lax.all_gather(packed, Z, axis=0, tiled=False)  38.5 us
    ppermute x7, starting transfers between devices, swapped(): return lax.ppermute(part, axis, [(i, i ^ distance) for i in range(size)])  19.9 us
    ppermute x7, waiting for transfers between devices, swapped(): return lax.ppermute(part, axis, [(i, i ^ distance) for i in range(size)])  14.1 us
    all_to_all x1, starting transfers between devices, per_device(): rows_in = lax.all_to_all(copies, PLANE, 0, 0, tiled=True)  8.71 us
    all_to_all x1, starting transfers between devices, per_device(): pieces = lax.all_to_all(pair_sum, ('zh', 'y'), 0, 0, tiled=True)  7.62 us
    pallas_call x1, Pallas kernels, route(): pl.pallas_call(route_kernel, out_shape=(jax.ShapeDtypeStruct((peers, 2 *...  2.88 us
    all_to_all x1, waiting for transfers between devices, per_device(): pieces = lax.all_to_all(pair_sum, ('zh', 'y'), 0, 0, tiled=True)  2.11 us
  transfers between devices with their start and end apart: 9, of which 6 were waited for; matrix products, arithmetic and copies ran while one was open for 1% of the time, Pallas kernels for 5%

profile of v12, /device:TPU:6, one launch (start us, length us, event | category | flops | bytes accessed | tf_op | source)
XLA Modules:
  0.0 101.3 jit_solution(13518439360218576519)
XLA Ops:
  0.6 0.7 pad_maximum_fusion.own_ref
  1.4 3.5 %collective-permute-start = (bf16[3,32,128]{2,1,0:T(8,128)(2,1)S(1)}, bf16[3,32,128]{2,1,0:T(8,128)(2,1)S(1)}, u32[]{:S(2)}, u32[]{:S(2)}) collective-permute-start(bf16[3,32,128]{2,1,0:T(8,128)(2,1)S(1)} %pad_maximum_fusion.own_ref), channel_id=1, source_target_pairs={{0,16},{16,0},{1,17},{17,1},{2,18},{18,2},{3,19},{19,3},{4,20},{20... | collective-permute-start | bytes 73736 | tf_op jit(solution)/shard_map/ppermute | solution.py:380
  4.8 2.9 %route.1 = (bf16[16,32,2048]{2,1,0:T(8,128)(2,1)}, bf16[16,128]{1,0:T(8,128)(2,1)}, f32[16,128]{1,0:T(8,128)}) custom-call(s32[8,128]{1,0:T(8,128)} %bitcast.13, f32[8,128]{1,0:T(8,128)} %bitcast.14, bf16[128,2048]{1,0:T(8,128)(2,1)} %tokens_ref.1, bf16[128,2048]{1,0:T(8,128)(2,1)} %cot_ref.1), custom_call_target="tpu_custom_call" | custom-call | tf_op jit(solution)/shard_map/route/pallas_call | solution.py:98
  7.7 0.0 collective-permute-done.got_ref
  7.7 0.1 pack_shards.1
  7.8 8.7 %all-to-all-start = ((bf16[16,32,2048]{2,1,0:T(8,128)(2,1)}), bf16[16,32,2048]{2,1,0:T(8,128)(2,1)S(1)}, u32[]{:S(2)}, u32[]{:S(2)}) async-start(bf16[16,32,2048]{2,1,0:T(8,128)(2,1)} %get-tuple-element.31), calls=%async_computation | async-start | bytes 4194304 | tf_op jit(solution)/shard_map/all_to_all | solution.py:391
  16.5 0.0 copy-start.2
  16.6 38.5 %all-gather = bf16[3072,128]{1,0:T(8,128)(2,1)S(1)} all-gather(bf16[192,128]{1,0:T(8,128)(2,1)S(1)} %pack_shards.1), channel_id=2, replica_groups=mesh['zh'=8,'zl'=2,'y'=2,'c'=2,'h'=2,'x'=4] {'zh','zl'}, dimensions={0}, use_global_device_ids=true | all-gather | bytes 835584 | tf_op jit(solution)/shard_map/all_gather | solution.py:392
  55.1 0.0 all-to-all-done.both_ref
  55.1 1.9 %collective-permute-start.1 = (bf16[16,192,128]{2,1,0:T(8,128)(2,1)S(1)}, bf16[16,192,128]{2,1,0:T(8,128)(2,1)S(1)}, u32[]{:S(2)}, u32[]{:S(2)}) collective-permute-start(bf16[16,192,128]{2,1,0:T(8,128)(2,1)S(1)} %bitcast.7), channel_id=1, source_target_pairs={{0,8},{8,0},{1,9},{9,1},{2,10},{10,2},{3,11},{11,3},{4,12},{12,4},... | collective-permute-start | bytes 2359304 | tf_op jit(solution)/shard_map/ppermute | solution.py:380
  57.0 2.3 %collective-permute-done.1.got_ref = bf16[16,192,128]{2,1,0:T(8,128)(2,1)S(1)} collective-permute-done((bf16[16,192,128]{2,1,0:T(8,128)(2,1)S(1)}, bf16[16,192,128]{2,1,0:T(8,128)(2,1)S(1)}, u32[]{:S(2)}, u32[]{:S(2)}) %collective-permute-start.1) | collective-permute-done | bytes 786464 | tf_op jit(solution)/shard_map/ppermute | solution.py:380
  59.2 0.5 forward.1
  59.7 0.0 copy-done.2
  59.7 1.9 %backward.1 = (bf16[2,8,2,48,128]{4,3,2,1,0:T(8,128)(2,1)S(1)}, f32[2,8,2,48,128]{4,3,2,1,0:T(8,128)S(1)}) custom-call(s32[64]{0:T(128)S(1)} %copy-done.2, bf16[16,32,2048]{2,1,0:T(8,128)(2,1)S(1)} %all-to-all-done.both_ref, f32[256,128]{1,0:T(8,128)S(1)} %get-tuple-element.37.acts_ref, bf16[2048,128]{1,0:T(8,128)(2,1)S(1)} %get-tuple-element.35.down.down_ref), custom_call_target="tpu_custom_call" | custom-call | flops 8800000000 | bytes 29600000 | tf_op jit(solution)/shard_map/backward/pallas_call | solution.py:292
  61.7 2.0 %collective-permute-start.5 = (bf16[2,8,2,48,128]{4,3,2,1,0:T(8,128)(2,1)S(1)}, bf16[2,8,2,48,128]{4,3,2,1,0:T(8,128)(2,1)S(1)}, u32[]{:S(2)}, u32[]{:S(2)}) collective-permute-start(bf16[2,8,2,48,128]{4,3,2,1,0:T(8,128)(2,1)S(1)} %get-tuple-element.47), channel_id=1, source_target_pairs={{0,8},{8,0},{1,9},{9,1},{2,10},{10,2},{3,11},{11,3},{4,12},{12,4},... | collective-permute-start | bytes 1179656 | tf_op jit(solution)/shard_map/ppermute | solution.py:380
  63.7 0.8 partial_rows.1
  64.5 0.8 collective-permute-done.5.got_ref
  65.3 0.1 add_halves.5
  65.4 1.9 %collective-permute-start.6 = (bf16[1,8,2,48,128]{4,3,2,1,0:T(8,128)(2,1)S(1)}, bf16[1,8,2,48,128]{4,3,2,1,0:T(8,128)(2,1)S(1)}, u32[]{:S(2)}, u32[]{:S(2)}) collective-permute-start(bf16[1,8,2,48,128]{4,3,2,1,0:T(8,128)(2,1)S(1)} %get-tuple-element.50), channel_id=1, source_target_pairs={{0,32},{32,0},{1,33},{33,1},{2,34},{34,2},{3,35},{35,3},{4,36},{36... | collective-permute-start | bytes 589832 | tf_op jit(solution)/shard_map/ppermute | solution.py:380
  67.3 3.4 %collective-permute-start.2 = (bf16[4,16,2048]{2,1,0:T(8,128)(2,1)S(1)}, bf16[4,16,2048]{2,1,0:T(8,128)(2,1)S(1)}, u32[]{:S(2)}, u32[]{:S(2)}) collective-permute-start(bf16[4,16,2048]{2,1,0:T(8,128)(2,1)S(1)} %get-tuple-element.39), channel_id=1, source_target_pairs={{0,2},{1,3},{2,0},{3,1},{4,6},{5,7},{6,4},{7,5},{8,10},{9,11},{10,... | collective-permute-start | bytes 786440 | tf_op jit(solution)/shard_map/ppermute | solution.py:380
  70.7 3.5 %collective-permute-done.6 = bf16[1,8,2,48,128]{4,3,2,1,0:T(8,128)(2,1)S(1)} collective-permute-done((bf16[1,8,2,48,128]{4,3,2,1,0:T(8,128)(2,1)S(1)}, bf16[1,8,2,48,128]{4,3,2,1,0:T(8,128)(2,1)S(1)}, u32[]{:S(2)}, u32[]{:S(2)}) %collective-permute-start.6) | collective-permute-done | bytes 196640 | tf_op jit(solution)/shard_map/ppermute | solution.py:380
  74.2 0.7 add_convert_fusion
  74.9 7.6 %all-to-all-start.1 = ((bf16[16,48,128]{2,1,0:T(8,128)(2,1)}), bf16[16,48,128]{2,1,0:T(8,128)(2,1)S(1)}, u32[]{:S(2)}, u32[]{:S(2)}) async-start(bf16[16,48,128]{2,1,0:T(8,128)(2,1)} %bitcast.6), calls=%async_computation.1 | async-start | bytes 393216 | tf_op jit(solution)/shard_map/all_to_all | solution.py:406
  82.5 0.0 collective-permute-done.2.got_ref
  82.6 0.1 add_halves.3
  82.6 0.0 copy-start
  82.6 0.0 copy-start.1
  82.6 2.6 %collective-permute-start.3 = (bf16[2,16,2048]{2,1,0:T(8,128)(2,1)S(1)}, bf16[2,16,2048]{2,1,0:T(8,128)(2,1)S(1)}, u32[]{:S(2)}, u32[]{:S(2)}) collective-permute-start(bf16[2,16,2048]{2,1,0:T(8,128)(2,1)S(1)} %get-tuple-element.41), channel_id=1, source_target_pairs={{0,1},{1,0},{2,3},{3,2},{4,5},{5,4},{6,7},{7,6},{8,9},{9,8},{10,11... | collective-permute-start | bytes 393224 | tf_op jit(solution)/shard_map/ppermute | solution.py:380
  85.3 4.2 %collective-permute-done.3.got_ref = bf16[2,16,2048]{2,1,0:T(8,128)(2,1)S(1)} collective-permute-done((bf16[2,16,2048]{2,1,0:T(8,128)(2,1)S(1)}, bf16[2,16,2048]{2,1,0:T(8,128)(2,1)S(1)}, u32[]{:S(2)}, u32[]{:S(2)}) %collective-permute-start.3) | collective-permute-done | bytes 131104 | tf_op jit(solution)/shard_map/ppermute | solution.py:380
  89.5 4.6 %collective-permute-start.4 = (bf16[1,16,2048]{2,1,0:T(8,128)(2,1)S(1)}, bf16[1,16,2048]{2,1,0:T(8,128)(2,1)S(1)}, u32[]{:S(2)}, u32[]{:S(2)}) collective-permute-start(bf16[1,16,2048]{2,1,0:T(8,128)(2,1)S(1)} %get-tuple-element.43), channel_id=1, source_target_pairs={{0,4},{4,0},{1,5},{5,1},{2,6},{6,2},{3,7},{7,3},{8,12},{12,8},{9,1... | collective-permute-start | bytes 196616 | tf_op jit(solution)/shard_map/ppermute | solution.py:380
  94.1 3.3 %collective-permute-done.4.got_ref = bf16[1,16,2048]{2,1,0:T(8,128)(2,1)S(1)} collective-permute-done((bf16[1,16,2048]{2,1,0:T(8,128)(2,1)S(1)}, bf16[1,16,2048]{2,1,0:T(8,128)(2,1)S(1)}, u32[]{:S(2)}, u32[]{:S(2)}) %collective-permute-start.4) | collective-permute-done | bytes 65568 | tf_op jit(solution)/shard_map/ppermute | solution.py:380
  97.4 0.0 copy-done
  97.4 0.0 copy-done.1
  97.4 1.1 %mix.1 = bf16[128,2048]{1,0:T(8,128)(2,1)} custom-call(f32[1,16,2048]{2,1,0:T(8,128)S(1)} %get-tuple-element.42.own_ref, bf16[1,16,2048]{2,1,0:T(8,128)(2,1)S(1)} %collective-permute-done.4.got_ref, bf16[16,128]{1,0:T(8,128)(2,1)S(1)} %copy-done.1, f32[16,128]{1,0:T(8,128)S(1)} %copy-done), custom_call_target="tpu_custom_call" | custom-call | flops 1100000000 | bytes 3700000 | tf_op jit(solution)/shard_map/mix/pallas_call | solution.py:338
  98.5 2.1 %all-to-all-done.1.blocks_ref = bf16[16,48,128]{2,1,0:T(8,128)(2,1)S(1)} async-done(((bf16[16,48,128]{2,1,0:T(8,128)(2,1)}), bf16[16,48,128]{2,1,0:T(8,128)(2,1)S(1)}, u32[]{:S(2)}, u32[]{:S(2)}) %all-to-all-start.1) | async-done | bytes 196640 | tf_op jit(solution)/shard_map/all_to_all | solution.py:406
  100.6 0.7 finish.1
  (1 shorter events, 0.0 us)
Async XLA Ops:
  1.4 6.4 %collective-permute-start = (bf16[3,32,128]{2,1,0:T(8,128)(2,1)S(1)}, bf16[3,32,128]{2,1,0:T(8,128)(2,1)S(1)}, u32[]{:S(2)}, u32[]{:S(2)}) collective-permute-start(bf16[3,32,128]{2,1,0:T(8,128)(2,1)S(1)} %pad_maximum_fusion.own_ref), channel_id=1, source_target_pairs={{0,16},{16,0},{1,17},{17,1},{2,18},{18,2},{3,19},{19,3},{4,20},{20... | collective-permute-start | bytes 73736 | tf_op jit(solution)/shard_map/ppermute | solution.py:380
  7.8 47.2 %all-to-all-start = ((bf16[16,32,2048]{2,1,0:T(8,128)(2,1)}), bf16[16,32,2048]{2,1,0:T(8,128)(2,1)S(1)}, u32[]{:S(2)}, u32[]{:S(2)}) async-start(bf16[16,32,2048]{2,1,0:T(8,128)(2,1)} %get-tuple-element.31), calls=%async_computation | async-start | bytes 4194304 | tf_op jit(solution)/shard_map/all_to_all | solution.py:391
  16.5 43.2 %copy-start.2 = (s32[64]{0:T(128)S(1)}, s32[64]{0:T(128)}, u32[]{:S(2)}) copy-start(s32[64]{0:T(128)} %join_ref.1) | copy-start | bytes 772
  55.1 4.2 %collective-permute-start.1 = (bf16[16,192,128]{2,1,0:T(8,128)(2,1)S(1)}, bf16[16,192,128]{2,1,0:T(8,128)(2,1)S(1)}, u32[]{:S(2)}, u32[]{:S(2)}) collective-permute-start(bf16[16,192,128]{2,1,0:T(8,128)(2,1)S(1)} %bitcast.7), channel_id=1, source_target_pairs={{0,8},{8,0},{1,9},{9,1},{2,10},{10,2},{3,11},{11,3},{4,12},{12,4},... | collective-permute-start | bytes 2359304 | tf_op jit(solution)/shard_map/ppermute | solution.py:380
  61.7 3.6 %collective-permute-start.5 = (bf16[2,8,2,48,128]{4,3,2,1,0:T(8,128)(2,1)S(1)}, bf16[2,8,2,48,128]{4,3,2,1,0:T(8,128)(2,1)S(1)}, u32[]{:S(2)}, u32[]{:S(2)}) collective-permute-start(bf16[2,8,2,48,128]{4,3,2,1,0:T(8,128)(2,1)S(1)} %get-tuple-element.47), channel_id=1, source_target_pairs={{0,8},{8,0},{1,9},{9,1},{2,10},{10,2},{3,11},{11,3},{4,12},{12,4},... | collective-permute-start | bytes 1179656 | tf_op jit(solution)/shard_map/ppermute | solution.py:380
  65.4 8.8 %collective-permute-start.6 = (bf16[1,8,2,48,128]{4,3,2,1,0:T(8,128)(2,1)S(1)}, bf16[1,8,2,48,128]{4,3,2,1,0:T(8,128)(2,1)S(1)}, u32[]{:S(2)}, u32[]{:S(2)}) collective-permute-start(bf16[1,8,2,48,128]{4,3,2,1,0:T(8,128)(2,1)S(1)} %get-tuple-element.50), channel_id=1, source_target_pairs={{0,32},{32,0},{1,33},{33,1},{2,34},{34,2},{3,35},{35,3},{4,36},{36... | collective-permute-start | bytes 589832 | tf_op jit(solution)/shard_map/ppermute | solution.py:380
  67.3 15.3 %collective-permute-start.2 = (bf16[4,16,2048]{2,1,0:T(8,128)(2,1)S(1)}, bf16[4,16,2048]{2,1,0:T(8,128)(2,1)S(1)}, u32[]{:S(2)}, u32[]{:S(2)}) collective-permute-start(bf16[4,16,2048]{2,1,0:T(8,128)(2,1)S(1)} %get-tuple-element.39), channel_id=1, source_target_pairs={{0,2},{1,3},{2,0},{3,1},{4,6},{5,7},{6,4},{7,5},{8,10},{9,11},{10,... | collective-permute-start | bytes 786440 | tf_op jit(solution)/shard_map/ppermute | solution.py:380
  74.9 25.7 %all-to-all-start.1 = ((bf16[16,48,128]{2,1,0:T(8,128)(2,1)}), bf16[16,48,128]{2,1,0:T(8,128)(2,1)S(1)}, u32[]{:S(2)}, u32[]{:S(2)}) async-start(bf16[16,48,128]{2,1,0:T(8,128)(2,1)} %bitcast.6), calls=%async_computation.1 | async-start | bytes 393216 | tf_op jit(solution)/shard_map/all_to_all | solution.py:406
  82.6 14.8 %copy-start = (f32[16,128]{1,0:T(8,128)S(1)}, f32[16,128]{1,0:T(8,128)}, u32[]{:S(2)}) copy-start(f32[16,128]{1,0:T(8,128)} %get-tuple-element.45.slot_weight_ref) | copy-start | bytes 24580
  82.6 14.8 %copy-start.1 = (bf16[16,128]{1,0:T(8,128)(2,1)S(1)}, bf16[16,128]{1,0:T(8,128)(2,1)}, u32[]{:S(2)}) copy-start(bf16[16,128]{1,0:T(8,128)(2,1)} %get-tuple-element.44.chooser_ref) | copy-start | bytes 12292
  82.6 6.9 %collective-permute-start.3 = (bf16[2,16,2048]{2,1,0:T(8,128)(2,1)S(1)}, bf16[2,16,2048]{2,1,0:T(8,128)(2,1)S(1)}, u32[]{:S(2)}, u32[]{:S(2)}) collective-permute-start(bf16[2,16,2048]{2,1,0:T(8,128)(2,1)S(1)} %get-tuple-element.41), channel_id=1, source_target_pairs={{0,1},{1,0},{2,3},{3,2},{4,5},{5,4},{6,7},{7,6},{8,9},{9,8},{10,11... | collective-permute-start | bytes 393224 | tf_op jit(solution)/shard_map/ppermute | solution.py:380
  89.5 7.8 %collective-permute-start.4 = (bf16[1,16,2048]{2,1,0:T(8,128)(2,1)S(1)}, bf16[1,16,2048]{2,1,0:T(8,128)(2,1)S(1)}, u32[]{:S(2)}, u32[]{:S(2)}) collective-permute-start(bf16[1,16,2048]{2,1,0:T(8,128)(2,1)S(1)} %get-tuple-element.43), channel_id=1, source_target_pairs={{0,4},{4,0},{1,5},{5,1},{2,6},{6,2},{3,7},{7,3},{8,12},{12,8},{9,1... | collective-permute-start | bytes 196616 | tf_op jit(solution)/shard_map/ppermute | solution.py:380
